TPU v7x, 256 devices: a whole 4x4x8 slice. The times are simulated.
256 devices in a mesh: angle: 8 (over x_hi, y), batch: 32 (over z, x_lo, core).
Axes of the slice: x: 4 (x_hi: 2, x_lo: 2; x = x_hi * 2 + x_lo), y: 4, z: 8, core: 2. Of those that a mesh axis runs over, the one named last changes fastest.
Arguments:
- signals: bfloat16 [32, 24576, 256], P('batch', 'angle'), may hold values from -6 to 6
- cotangent: bfloat16 [32, 24576, 256], P('batch', 'angle'), may hold values from -6 to 6
- first_dilated_kernel: bfloat16 [3, 256, 256], replicated, may hold values from -0.21875 to 0.21875
- first_conv_bias: float32 [256], replicated, may hold values from -3 to 3
- first_output_projection: bfloat16 [256, 256], replicated, may hold values from -0.375 to 0.375
- second_dilated_kernel: bfloat16 [3, 256, 256], replicated, may hold values from -0.21875 to 0.21875
- second_conv_bias: float32 [256], replicated, may hold values from -3 to 3
- second_output_projection: bfloat16 [256, 256], replicated, may hold values from -0.375 to 0.375
Outputs:
- signal_input_gradient: bfloat16 [32, 24576, 256], P('batch', 'angle')
- conv_grad_a: float32 [3, 256, 256], replicated
- bias_grad_a: float32 [256], replicated
- proj_grad_a: float32 [256, 256], replicated
- conv_grad_b: float32 [3, 256, 256], replicated
- bias_grad_b: float32 [256], replicated
- proj_grad_b: float32 [256, 256], replicated
All inputs are finite; a program needn't handle non-finite values.
Results may differ from a plain program's by a relative error of at most 0.013.
Values may be sent and summed in bfloat16 or wider, within the bound.
No kernel may reach another device: no remote copies, remote signals or barrier semaphores. Data moves between devices by JAX's collectives and lax.ppermute only.
A program may use at most 64 MiB of HBM per device.

v0:
```python
import math

import jax
import jax.numpy as jnp
from jax import lax
from jax.sharding import PartitionSpec as P

FIRST_DILATION = 512
SECOND_DILATION = 1024


def extended(cells, sides, width):
    for axis, dim in sides:
        count = lax.axis_size(axis)
        head = lax.slice_in_dim(cells, 0, width, axis=dim)
        tail = lax.slice_in_dim(cells, cells.shape[dim] - width, cells.shape[dim], axis=dim)
        cells = jnp.concatenate(
            [
                lax.ppermute(tail, axis, [(i, (i + 1) % count) for i in range(count)]),
                cells,
                lax.ppermute(head, axis, [((i + 1) % count, i) for i in range(count)]),
            ],
            axis=dim,
        )
    return cells


def gelu_exact(v):
    return 0.5 * v * (1.0 + lax.erf(v / math.sqrt(2.0)))


def gelu_slope(v):
    return 0.5 * (1.0 + lax.erf(v / math.sqrt(2.0))) + v * jnp.exp(-0.5 * v * v) / math.sqrt(
        2.0 * math.pi
    )


def wrap_extended(field, dilation):
    return extended(field, (("angle", 1),), dilation)


def dilated_forward(padded, kernel, bias, dilation, sequence_length):
    total = jnp.zeros(padded.shape[:1] + (sequence_length, kernel.shape[2]), jnp.float32)
    for k in range(3):
        window = padded[:, k * dilation : k * dilation + sequence_length]
        total = total + jnp.einsum(
            "btc,cd->btd", window, kernel[k], preferred_element_type=jnp.float32
        )
    return total + bias


def reduce_grads(grads):
    return lax.psum((grads[0], grads[1], grads[2]), ("angle", "batch"))


def lower_grad(delta, upstream, kernel, dilation, sequence_length):
    below = upstream.astype(jnp.float32)
    padded = extended(delta, (("angle", 1),), dilation)
    for k in range(3):
        window = padded[:, (2 - k) * dilation : (2 - k) * dilation + sequence_length]
        below = below + jnp.einsum(
            "btd,cd->btc", window, kernel[k], preferred_element_type=jnp.float32
        )
    return below.astype(jnp.bfloat16)


def residual_block_backward(padded, upstream, act, pre, kernel, proj, dilation, sequence_length):
    proj_grad = jnp.einsum("btc,btd->cd", act, upstream, preferred_element_type=jnp.float32)
    delta = (
        jnp.einsum("btd,cd->btc", upstream, proj, preferred_element_type=jnp.float32)
        * gelu_slope(pre)
    ).astype(jnp.bfloat16)
    bias_grad = jnp.sum(delta.astype(jnp.float32), axis=(0, 1))
    conv_grad = jnp.stack(
        [
            jnp.einsum(
                "btc,btd->cd",
                padded[:, k * dilation : k * dilation + sequence_length],
                delta,
                preferred_element_type=jnp.float32,
            )
            for k in range(3)
        ]
    )
    summed = reduce_grads((conv_grad, bias_grad, proj_grad))
    below = lower_grad(delta, upstream, kernel, dilation, sequence_length)
    return (below, summed)


def on_device(
    signals,
    cotangent,
    first_dilated_kernel,
    first_conv_bias,
    first_output_projection,
    second_dilated_kernel,
    second_conv_bias,
    second_output_projection,
):
    sequence_length = signals.shape[1]
    first_padded_input = wrap_extended(signals, FIRST_DILATION)
    first_preactivation = dilated_forward(
        first_padded_input, first_dilated_kernel, first_conv_bias, FIRST_DILATION, sequence_length
    )
    first_activation = gelu_exact(first_preactivation).astype(jnp.bfloat16)
    between_blocks = (
        signals.astype(jnp.float32)
        + jnp.einsum(
            "btc,cd->btd",
            first_activation,
            first_output_projection,
            preferred_element_type=jnp.float32,
        )
    ).astype(jnp.bfloat16)
    second_padded_input = wrap_extended(between_blocks, SECOND_DILATION)
    second_preactivation = dilated_forward(
        second_padded_input,
        second_dilated_kernel,
        second_conv_bias,
        SECOND_DILATION,
        sequence_length,
    )
    second_activation = gelu_exact(second_preactivation).astype(jnp.bfloat16)
    between_blocks_gradient, grads_b = residual_block_backward(
        second_padded_input,
        cotangent,
        second_activation,
        second_preactivation,
        second_dilated_kernel,
        second_output_projection,
        SECOND_DILATION,
        sequence_length,
    )
    signal_input_gradient, grads_a = residual_block_backward(
        first_padded_input,
        between_blocks_gradient,
        first_activation,
        first_preactivation,
        first_dilated_kernel,
        first_output_projection,
        FIRST_DILATION,
        sequence_length,
    )
    return (
        signal_input_gradient,
        grads_a[0],
        grads_a[1],
        grads_a[2],
        grads_b[0],
        grads_b[1],
        grads_b[2],
    )


def solution(mesh):
    in_specs = (P("batch", "angle", None), P("batch", "angle", None), P(), P(), P(), P(), P(), P())
    out_specs = (P("batch", "angle", None), P(), P(), P(), P(), P(), P())
    return jax.shard_map(
        on_device, mesh=mesh, in_specs=in_specs, out_specs=out_specs, check_vma=False
    )
```

profile of v0, /device:TPU:1, one launch (start us, length us, event | category | flops | bytes accessed | tf_op | source)
XLA Modules:
  0.0 344.6 jit_solution(3315424802316499119)
XLA Ops:
  7.2 0.0 copy-start
  7.2 0.0 all-reduce.4.cloned.1.call-start
  7.2 1.1 fusion.111
  8.3 2.2 collective-permute-start
  10.5 4.0 %collective-permute-start.1 = (bf16[1,512,256]{2,1,0:T(8,128)(2,1)S(1)}, bf16[1,512,256]{2,1,0:T(8,128)(2,1)S(1)}, u32[]{:S(2)}, u32[]{:S(2)}) collective-permute-start(bf16[1,512,256]{2,1,0:T(8,128)(2,1)S(1)} %get-tuple-element.20), channel_id=1, source_target_pairs={{32,0},{64,32},{96,64},{128,96},{160,128},{192,160},{224,192},{0,2... | collective-permute-start | bytes 786440 | tf_op jit(solution)/shard_map/ppermute | solution.py:21
  14.5 2.0 fusion.50
  16.5 0.0 copy-start.9
  16.5 1.3 collective-permute-done.1
  17.9 0.0 copy-done.1
  17.9 0.0 copy-done.3
  17.9 0.6 fusion.64
  18.4 0.0 collective-permute-done
  18.4 0.0 copy-done.9
  18.5 1.1 multiply_convert_fusion.1
  19.5 0.6 fusion.13
  20.1 0.0 copy-start.4
  20.1 0.1 fusion.110
  20.2 5.6 %collective-permute-start.3 = (bf16[1,1024,256]{2,1,0:T(8,128)(2,1)S(1)}, bf16[1,1024,256]{2,1,0:T(8,128)(2,1)S(1)}, u32[]{:S(2)}, u32[]{:S(2)}) collective-permute-start(bf16[1,1024,256]{2,1,0:T(8,128)(2,1)S(1)} %get-tuple-element.18), channel_id=1, source_target_pairs={{32,0},{64,32},{96,64},{128,96},{160,128},{192,160},{224,192},{0,2... | collective-permute-start | bytes 1572872 | tf_op jit(solution)/shard_map/ppermute | solution.py:21
  25.8 0.0 collective-permute-start.2
  25.8 0.0 copy-done.4
  25.8 0.6 fusion.46
  26.4 0.0 copy-start.10
  26.4 7.0 %collective-permute-done.3 = bf16[1,1024,256]{2,1,0:T(8,128)(2,1)S(1)} collective-permute-done((bf16[1,1024,256]{2,1,0:T(8,128)(2,1)S(1)}, bf16[1,1024,256]{2,1,0:T(8,128)(2,1)S(1)}, u32[]{:S(2)}, u32[]{:S(2)}) %collective-permute-start.3) | collective-permute-done | bytes 524320 | tf_op jit(solution)/shard_map/ppermute | solution.py:21
  33.4 0.6 fusion.69
  34.0 0.0 copy-start.5
  34.0 0.0 copy-start.11
  34.0 4.9 %collective-permute-done.2 = bf16[1,1024,256]{2,1,0:T(8,128)(2,1)S(1)} collective-permute-done((bf16[1,1024,256]{2,1,0:T(8,128)(2,1)S(1)}, bf16[1,1024,256]{2,1,0:T(8,128)(2,1)S(1)}, u32[]{:S(2)}, u32[]{:S(2)}) %collective-permute-start.2) | collective-permute-done | bytes 524320 | tf_op jit(solution)/shard_map/ppermute | solution.py:19
  39.0 0.7 fusion.1
  39.6 1.7 convert_reduce_fusion
  41.3 0.6 fusion.58
  41.9 0.6 convolution_bitcast_fusion.4
  42.5 0.1 fusion.109
  42.6 1.6 collective-permute-start.4
  44.3 0.0 collective-permute-start.5
  44.3 0.6 convolution_bitcast_fusion.7
  44.9 0.6 convolution_bitcast_fusion.8
  45.5 0.9 pad_maximum_fusion.9
  46.4 1.6 fusion.24
  48.1 8.4 %collective-permute-done.5 = bf16[1,1024,256]{2,1,0:T(8,128)(2,1)S(1)} collective-permute-done((bf16[1,1024,256]{2,1,0:T(8,128)(2,1)S(1)}, bf16[1,1024,256]{2,1,0:T(8,128)(2,1)S(1)}, u32[]{:S(2)}, u32[]{:S(2)}) %collective-permute-start.5) | collective-permute-done | bytes 524320 | tf_op jit(solution)/shard_map/ppermute | solution.py:19
  56.5 0.6 convolution_bitcast_fusion.3
  57.1 0.0 collective-permute-done.4
  57.1 0.7 fusion.12
  57.8 1.3 fusion.41
  59.1 1.7 convert_reduce_fusion.1
  60.7 0.7 fusion.55
  61.5 0.6 convolution_bitcast_fusion.9
  62.1 0.6 convolution_bitcast_fusion.10
  62.7 0.9 pad_maximum_fusion.8
  63.6 0.0 all-reduce.4.cloned.1.call-update
  63.6 0.8 fusion.108
  64.5 0.0 collective-permute-start.7
  64.5 5.1 %collective-permute-start.6 = (bf16[1,512,256]{2,1,0:T(8,128)(2,1)}, bf16[1,512,256]{2,1,0:T(8,128)(2,1)S(1)}, u32[]{:S(2)}, u32[]{:S(2)}) collective-permute-start(bf16[1,512,256]{2,1,0:T(8,128)(2,1)} %get-tuple-element.13), channel_id=1, source_target_pairs={{32,0},{64,32},{96,64},{128,96},{160,128},{192,160},{224,192},{0,2... | collective-permute-start | bytes 786440 | tf_op jit(solution)/shard_map/ppermute | solution.py:21
  69.6 3.2 convolution_bitcast_fusion.1
  72.7 87.6 %all-reduce = (f32[256]{0:T(256)}, f32[256]{0:T(256)}) all-reduce(f32[256]{0:T(256)S(1)} %get-tuple-element.23, f32[256]{0:T(256)S(1)} %get-tuple-element.25), channel_id=1, replica_groups=mesh['angle'=8,'batch'=32] {'angle','batch'}, use_global_device_ids=true, to_apply=%region_2.0 | all-reduce | flops 512 | bytes 4096 | tf_op jit(solution)/shard_map/psum | solution.py:53
  160.4 0.0 collective-permute-done.7
  160.4 1.7 convolution_bitcast_fusion
  162.1 0.0 collective-permute-done.6
  162.1 0.3 copy-done.2
  162.4 2.7 fusion.11
  165.1 168.2 %all-reduce.4.cloned.1.call-done = (f32[3,256,256]{2,1,0:T(8,128)}, f32[256,256]{1,0:T(8,128)}, f32[3,256,256]{2,1,0:T(8,128)}, f32[256,256]{1,0:T(8,128)}) async-done(((f32[3,256,256]{2,1,0:T(8,128)}, f32[256,256]{1,0:T(8,128)}, f32[3,256,256]{2,1,0:T(8,128)}, f32[256,256]{1,0:T(8,128)}), (f32[3,256,256]{2,1,0:T(8,128)}, f32[256,256]{1,0:T(8,128)}, f32[3,256,256]{2,1,0:T(8,128)}, ...) | async-done | bytes 2097168 | tf_op jit(solution)/shard_map/psum | solution.py:53
  333.3 2.2 copy.21
  335.5 0.7 copy.22
  336.2 0.9 copy.23
  337.1 0.7 copy.24
  (13 shorter events, 0.0 us)
Async XLA Ops:
  7.2 12.4 %copy-start = (bf16[256,256]{1,0:T(8,128)(2,1)S(1)}, bf16[256,256]{1,0:T(8,128)(2,1)}, u32[]{:S(2)}) copy-start(bf16[256,256]{1,0:T(8,128)(2,1)} %param.12) | copy-start | bytes 393220
  7.2 326.1 %all-reduce.4.cloned.1.call-start = ((), (), s32[]{:S(2)}) async-start(), calls=%async_computation | async-start | bytes 4194304 | tf_op jit(solution)/shard_map/psum | solution.py:53
  8.3 10.1 %collective-permute-start = (bf16[1,512,256]{2,1,0:T(8,128)(2,1)S(1)}, bf16[1,512,256]{2,1,0:T(8,128)(2,1)S(1)}, u32[]{:S(2)}, u32[]{:S(2)}) collective-permute-start(bf16[1,512,256]{2,1,0:T(8,128)(2,1)S(1)} %get-tuple-element.19), channel_id=1, source_target_pairs={{0,32},{32,64},{64,96},{96,128},{128,160},{160,192},{192,224},{224... | collective-permute-start | bytes 786440 | tf_op jit(solution)/shard_map/ppermute | solution.py:19
  10.5 7.3 %copy-start.1 = (bf16[1,3072,256]{2,1,0:T(8,128)(2,1)S(1)}, bf16[1,3072,256]{2,1,0:T(8,128)(2,1)}, u32[]{:S(2)}) copy-start(bf16[1,3072,256]{2,1,0:T(8,128)(2,1)} %param.8) | copy-start | bytes 4718596
  10.5 7.3 %copy-start.3 = (bf16[3,256,256]{2,1,0:T(8,128)(2,1)S(1)}, bf16[3,256,256]{2,1,0:T(8,128)(2,1)}, u32[]{:S(2)}) copy-start(bf16[3,256,256]{2,1,0:T(8,128)(2,1)} %param.10) | copy-start | bytes 1179652
  10.5 7.3 %collective-permute-start.1 = (bf16[1,512,256]{2,1,0:T(8,128)(2,1)S(1)}, bf16[1,512,256]{2,1,0:T(8,128)(2,1)S(1)}, u32[]{:S(2)}, u32[]{:S(2)}) collective-permute-start(bf16[1,512,256]{2,1,0:T(8,128)(2,1)S(1)} %get-tuple-element.20), channel_id=1, source_target_pairs={{32,0},{64,32},{96,64},{128,96},{160,128},{192,160},{224,192},{0,2... | collective-permute-start | bytes 786440 | tf_op jit(solution)/shard_map/ppermute | solution.py:21
  16.5 1.9 copy-start.9
  20.1 5.7 %copy-start.4 = (bf16[3,256,256]{2,1,0:T(8,128)(2,1)S(1)}, bf16[3,256,256]{2,1,0:T(8,128)(2,1)}, u32[]{:S(2)}) copy-start(bf16[3,256,256]{2,1,0:T(8,128)(2,1)} %param.13) | copy-start | bytes 1179652
  20.2 13.2 %collective-permute-start.3 = (bf16[1,1024,256]{2,1,0:T(8,128)(2,1)S(1)}, bf16[1,1024,256]{2,1,0:T(8,128)(2,1)S(1)}, u32[]{:S(2)}, u32[]{:S(2)}) collective-permute-start(bf16[1,1024,256]{2,1,0:T(8,128)(2,1)S(1)} %get-tuple-element.18), channel_id=1, source_target_pairs={{32,0},{64,32},{96,64},{128,96},{160,128},{192,160},{224,192},{0,2... | collective-permute-start | bytes 1572872 | tf_op jit(solution)/shard_map/ppermute | solution.py:21
  25.8 13.1 %collective-permute-start.2 = (bf16[1,1024,256]{2,1,0:T(8,128)(2,1)S(1)}, bf16[1,1024,256]{2,1,0:T(8,128)(2,1)S(1)}, u32[]{:S(2)}, u32[]{:S(2)}) collective-permute-start(bf16[1,1024,256]{2,1,0:T(8,128)(2,1)S(1)} %get-tuple-element.17), channel_id=1, source_target_pairs={{0,32},{32,64},{64,96},{96,128},{128,160},{160,192},{192,224},{224... | collective-permute-start | bytes 1572872 | tf_op jit(solution)/shard_map/ppermute | solution.py:19
  26.4 12.6 %copy-start.10 = (f32[256]{0:T(256)S(1)}, f32[256]{0:T(256)}, u32[]{:S(2)}) copy-start(f32[256]{0:T(256)} %param.14) | copy-start | bytes 3076
  34.0 5.6 %copy-start.5 = (bf16[1,3072,256]{2,1,0:T(8,128)(2,1)S(1)}, bf16[1,3072,256]{2,1,0:T(8,128)(2,1)}, u32[]{:S(2)}) copy-start(bf16[1,3072,256]{2,1,0:T(8,128)(2,1)} %param.9) | copy-start | bytes 4718596
  34.0 5.6 %copy-start.11 = (bf16[256,256]{1,0:T(8,128)(2,1)S(1)}, bf16[256,256]{1,0:T(8,128)(2,1)}, u32[]{:S(2)}) copy-start(bf16[256,256]{1,0:T(8,128)(2,1)} %param.15) | copy-start | bytes 393220
  42.6 14.5 %collective-permute-start.4 = (bf16[1,1024,256]{2,1,0:T(8,128)(2,1)S(1)}, bf16[1,1024,256]{2,1,0:T(8,128)(2,1)S(1)}, u32[]{:S(2)}, u32[]{:S(2)}) collective-permute-start(bf16[1,1024,256]{2,1,0:T(8,128)(2,1)S(1)} %get-tuple-element.15), channel_id=1, source_target_pairs={{32,0},{64,32},{96,64},{128,96},{160,128},{192,160},{224,192},{0,2... | collective-permute-start | bytes 1572872 | tf_op jit(solution)/shard_map/ppermute | solution.py:21
  44.3 12.2 %collective-permute-start.5 = (bf16[1,1024,256]{2,1,0:T(8,128)(2,1)S(1)}, bf16[1,1024,256]{2,1,0:T(8,128)(2,1)S(1)}, u32[]{:S(2)}, u32[]{:S(2)}) collective-permute-start(bf16[1,1024,256]{2,1,0:T(8,128)(2,1)S(1)} %get-tuple-element.16), channel_id=1, source_target_pairs={{0,32},{32,64},{64,96},{96,128},{128,160},{160,192},{192,224},{224... | collective-permute-start | bytes 1572872 | tf_op jit(solution)/shard_map/ppermute | solution.py:19
  64.5 95.9 %collective-permute-start.7 = (bf16[1,512,256]{2,1,0:T(8,128)(2,1)}, bf16[1,512,256]{2,1,0:T(8,128)(2,1)}, u32[]{:S(2)}, u32[]{:S(2)}) collective-permute-start(bf16[1,512,256]{2,1,0:T(8,128)(2,1)} %get-tuple-element.14), channel_id=1, source_target_pairs={{0,32},{32,64},{64,96},{96,128},{128,160},{160,192},{192,224},{224... | collective-permute-start | bytes 786440 | tf_op jit(solution)/shard_map/ppermute | solution.py:19
  64.5 97.6 %collective-permute-start.6 = (bf16[1,512,256]{2,1,0:T(8,128)(2,1)}, bf16[1,512,256]{2,1,0:T(8,128)(2,1)S(1)}, u32[]{:S(2)}, u32[]{:S(2)}) collective-permute-start(bf16[1,512,256]{2,1,0:T(8,128)(2,1)} %get-tuple-element.13), channel_id=1, source_target_pairs={{32,0},{64,32},{96,64},{128,96},{160,128},{192,160},{224,192},{0,2... | collective-permute-start | bytes 786440 | tf_op jit(solution)/shard_map/ppermute | solution.py:21
  160.4 2.1 copy-start.2
  333.3 2.2 copy-start.8
  333.3 2.9 copy-start.6
  333.3 3.8 %copy-start.7 = (f32[256,256]{1,0:T(8,128)S(1)}, f32[256,256]{1,0:T(8,128)}, u32[]{:S(2)}) copy-start(f32[256,256]{1,0:T(8,128)} %get-tuple-element.33) | copy-start | bytes 786436
Sparse Core Ops, SparseCore 0:
  63.8 269.4 all-reduce.3
where the time goes:
time: 346 us; the launch traced here: 345 us
  waiting for transfers between devices  190 us (55%)
  blocking collectives  87.6 us (25%)
  matrix products  25.5 us (7%)
  starting transfers between devices  18.6 us (5%)
  between operations  14.3 us (4%)
  local copies, waits for them, and re-layouts  6.87 us (2%)
    psum x1, waiting for transfers between devices, reduce_grads(): return lax.psum((grads[0], grads[1], grads[2]), ('angle', 'batch'))  168 us
    psum x1, blocking collectives, reduce_grads(): return lax.psum((grads[0], grads[1], grads[2]), ('angle', 'batch'))  87.6 us
    ppermute x4, starting transfers between devices, extended(): lax.ppermute(head, axis, [((i + 1) % count, i) for i in range(count)])  16.3 us
    ppermute x4, waiting for transfers between devices, extended(): lax.ppermute(tail, axis, [(i, (i + 1) % count) for i in range(count)])  13.3 us
    dot_general x6, matrix products, lower_grad(): jnp.einsum('btd,cd->btc', window, kernel[k], preferred_element_type=jnp.f...  9.49 us
    ppermute x4, waiting for transfers between devices, extended(): lax.ppermute(head, axis, [((i + 1) % count, i) for i in range(count)])  8.36 us
  transfers between devices with their start and end apart: 9, of which 5 were waited for; matrix products, arithmetic and copies ran while one was open for 5% of the time, Pallas kernels for 0%

commit v1 on v0

--- a/solution.py
+++ b/solution.py
@@ -49,8 +49,34 @@
     return total + bias
 
 
-def reduce_grads(grads):
-    return lax.psum((grads[0], grads[1], grads[2]), ("angle", "batch"))
+def reduce_grads(matrices, biases):
+    angles, turbines = lax.axis_size("angle"), lax.axis_size("batch")
+    parts, rows, lanes = matrices.shape
+    share = biases.size // parts
+    extra = jnp.pad(biases.reshape(parts, 1, share), ((0, 0), (0, 7), (0, lanes - share)))
+    sent = jnp.concatenate([matrices, extra], axis=1).astype(jnp.bfloat16)
+    got = lax.all_to_all(sent, "angle", 0, 0)
+    total = jnp.sum(got.astype(jnp.float32), axis=0)
+    small = share // turbines
+    sent = jnp.concatenate(
+        [
+            total[:rows].reshape(turbines, rows // turbines, lanes),
+            jnp.pad(
+                total[rows, :share].reshape(turbines, 1, small),
+                ((0, 0), (0, rows // turbines - 1), (0, 128 - small)),
+            ),
+        ],
+        axis=2,
+    ).astype(jnp.bfloat16)
+    got = lax.all_to_all(sent, "batch", 0, 0)
+    total = jnp.sum(got.astype(jnp.float32), axis=0).astype(jnp.bfloat16)
+    got = lax.all_to_all(jnp.broadcast_to(total, (turbines,) + total.shape), "batch", 0, 0)
+    matrix = got[:, :, :lanes].reshape(rows, lanes)
+    bias = jnp.pad(got[:, 0, lanes : lanes + small].reshape(1, share), ((0, 7), (0, lanes - share)))
+    own = jnp.concatenate([matrix, bias], axis=0)
+    got = lax.all_to_all(jnp.broadcast_to(own, (angles,) + own.shape), "angle", 0, 0)
+    got = got.astype(jnp.float32)
+    return got[:, :rows], got[:, rows, :share].reshape(biases.shape)
 
 
 def lower_grad(delta, upstream, kernel, dilation, sequence_length):
@@ -82,9 +108,8 @@
             for k in range(3)
         ]
     )
-    summed = reduce_grads((conv_grad, bias_grad, proj_grad))
     below = lower_grad(delta, upstream, kernel, dilation, sequence_length)
-    return (below, summed)
+    return (below, (conv_grad, bias_grad, proj_grad))
 
 
 def on_device(
@@ -141,14 +166,18 @@
         FIRST_DILATION,
         sequence_length,
     )
+    matrices, biases = reduce_grads(
+        jnp.concatenate([grads_b[0], grads_b[2][None], grads_a[0], grads_a[2][None]]),
+        jnp.stack([grads_b[1], grads_a[1]]),
+    )
     return (
         signal_input_gradient,
-        grads_a[0],
-        grads_a[1],
-        grads_a[2],
-        grads_b[0],
-        grads_b[1],
-        grads_b[2],
+        matrices[4:7],
+        biases[1],
+        matrices[7],
+        matrices[0:3],
+        biases[0],
+        matrices[3],
     )
 
 

time: 346 us -> 150 us (0.43)
  waiting for transfers between devices: 190 us -> 49.6 us
  blocking collectives: 87.6 us -> 42.7 us
  between operations: 14.3 us -> 0.99 us
  starting transfers between devices: 18.6 us -> 25.9 us
  matrix products: 25.5 us -> 20 us
    psum x1 -> x0, waiting for transfers between devices: 168 us -> none  [reduce_grads(): return lax.psum((grads[0], grads[1], grads[2]), ('angle', 'batch'))]
    psum x1 -> x0, blocking collectives: 87.6 us -> none  [reduce_grads(): return lax.psum((grads[0], grads[1], grads[2]), ('angle', 'batch'))]
    all_to_all x0 -> x2, blocking collectives: none -> 42.7 us  [the longest x1 24.2 us: reduce_grads(): got = lax.all_to_all(sent, 'batch', 0, 0)]
    ppermute x4, waiting for transfers between devices: 8.36 us -> 24.7 us  [extended(): lax.ppermute(head, axis, [((i + 1) % count, i) for i in range(count)])]
    all_to_all x0 -> x2, waiting for transfers between devices: none -> 9.26 us  [the longest x1 9.26 us: reduce_grads(): lax.all_to_all(jnp.broadcast_to(total, (turbines,) + total.shape), 'batch...]
    all_to_all x0 -> x2, starting transfers between devices: none -> 7.78 us  [the longest x1 4.22 us: reduce_grads(): lax.all_to_all(jnp.broadcast_to(total, (turbines,) + total.shape), 'batch...]
    unnamed x28 -> x20, local copies, waits for them, and re-layouts: 4.81 us -> 0.06 us
    dot_general x6, matrix products: 9.49 us -> 4.89 us  [lower_grad(): jnp.einsum('btd,cd->btc', window, kernel[k], preferred_element_type=jnp.f...]
  transfers between devices with their start and end apart: 9 -> 10, of which waited for: 5 -> 7; matrix products, arithmetic and copies ran while one was open for 5% -> 8% of each run, Pallas kernels for 0% -> 0%
where the time goes in v1:
time: 150 us; the launch traced here: 147 us
  waiting for transfers between devices  49.6 us (33%)
  blocking collectives  42.7 us (28%)
  starting transfers between devices  25.9 us (17%)
  matrix products  20 us (13%)
  local copies, waits for them, and re-layouts  7.7 us (5%)
    ppermute x4, waiting for transfers between devices, extended(): lax.ppermute(head, axis, [((i + 1) % count, i) for i in range(count)])  24.7 us
    all_to_all x1, blocking collectives, reduce_grads(): got = lax.all_to_all(sent, 'batch', 0, 0)  24.2 us
    all_to_all x1, blocking collectives, reduce_grads(): got = lax.all_to_all(sent, 'angle', 0, 0)  18.5 us
    ppermute x4, starting transfers between devices, extended(): lax.ppermute(head, axis, [((i + 1) % count, i) for i in range(count)])  17.2 us
    ppermute x4, waiting for transfers between devices, extended(): lax.ppermute(tail, axis, [(i, (i + 1) % count) for i in range(count)])  15.7 us
    all_to_all x1, waiting for transfers between devices, reduce_grads(): lax.all_to_all(jnp.broadcast_to(total, (turbines,) + total.shape), 'batch...  9.26 us
    dot_general x6, matrix products, dilated_forward(): jnp.einsum('btc,cd->btd', window, kernel[k], preferred_element_type=jnp.f...  5.53 us
    dot_general x6, matrix products, lower_grad(): jnp.einsum('btd,cd->btc', window, kernel[k], preferred_element_type=jnp.f...  4.89 us
  transfers between devices with their start and end apart: 10, of which 7 were waited for; matrix products, arithmetic and copies ran while one was open for 8% of the time, Pallas kernels for 0%

profile of v1, /device:TPU:1, one launch (start us, length us, event | category | flops | bytes accessed | tf_op | source)
XLA Modules:
  0.0 147.4 jit_solution(8900240052404860982)
XLA Ops:
  0.6 0.0 copy-start
  0.6 1.1 fusion.155
  1.8 6.1 %collective-permute-start.1 = (bf16[1,512,256]{2,1,0:T(8,128)(2,1)S(1)}, bf16[1,512,256]{2,1,0:T(8,128)(2,1)S(1)}, u32[]{:S(2)}, u32[]{:S(2)}) collective-permute-start(bf16[1,512,256]{2,1,0:T(8,128)(2,1)S(1)} %get-tuple-element.18), channel_id=1, source_target_pairs={{32,0},{64,32},{96,64},{128,96},{160,128},{192,160},{224,192},{0,2... | collective-permute-start | bytes 786440 | tf_op jit(solution)/shard_map/ppermute | solution.py:21
  7.9 2.1 %fusion.51 = f32[3072,256]{1,0:T(8,128)S(1)} fusion(bf16[1,3072,256]{2,1,0:T(8,128)(2,1)} %param.8, bf16[3,256,256]{2,1,0:T(8,128)(2,1)} %param.10), kind=kOutput, calls=%fused_computation.73 | convolution fusion | flops 402653184 | bytes 4849664 | tf_op jit(solution)/shard_map/btc,cd->btd/dot_general | solution.py:46
  10.0 0.0 copy-start.7
  10.0 2.8 %collective-permute-done.1 = bf16[1,512,256]{2,1,0:T(8,128)(2,1)S(1)} collective-permute-done((bf16[1,512,256]{2,1,0:T(8,128)(2,1)S(1)}, bf16[1,512,256]{2,1,0:T(8,128)(2,1)S(1)}, u32[]{:S(2)}, u32[]{:S(2)}) %collective-permute-start.1) | collective-permute-done | bytes 262176 | tf_op jit(solution)/shard_map/ppermute | solution.py:21
  12.8 0.6 fusion.104
  13.4 4.9 %collective-permute-done = bf16[1,512,256]{2,1,0:T(8,128)(2,1)S(1)} collective-permute-done((bf16[1,512,256]{2,1,0:T(8,128)(2,1)S(1)}, bf16[1,512,256]{2,1,0:T(8,128)(2,1)S(1)}, u32[]{:S(2)}, u32[]{:S(2)}) %collective-permute-start) | collective-permute-done | bytes 262176 | tf_op jit(solution)/shard_map/ppermute | solution.py:19
  18.3 1.1 multiply_convert_fusion.1
  19.4 0.6 fusion.13
  20.0 0.1 fusion.154
  20.1 1.0 collective-permute-start.3
  21.1 0.6 collective-permute-start.2
  21.6 0.6 fusion.47
  22.2 9.5 %collective-permute-done.3 = bf16[1,1024,256]{2,1,0:T(8,128)(2,1)S(1)} collective-permute-done((bf16[1,1024,256]{2,1,0:T(8,128)(2,1)S(1)}, bf16[1,1024,256]{2,1,0:T(8,128)(2,1)S(1)}, u32[]{:S(2)}, u32[]{:S(2)}) %collective-permute-start.3) | collective-permute-done | bytes 524320 | tf_op jit(solution)/shard_map/ppermute | solution.py:21
  31.7 0.6 fusion.109
  32.3 0.0 copy-start.6
  32.3 0.0 copy-start.9
  32.3 4.0 %collective-permute-done.2 = bf16[1,1024,256]{2,1,0:T(8,128)(2,1)S(1)} collective-permute-done((bf16[1,1024,256]{2,1,0:T(8,128)(2,1)S(1)}, bf16[1,1024,256]{2,1,0:T(8,128)(2,1)S(1)}, u32[]{:S(2)}, u32[]{:S(2)}) %collective-permute-start.2) | collective-permute-done | bytes 524320 | tf_op jit(solution)/shard_map/ppermute | solution.py:19
  36.3 0.7 fusion.1
  36.9 1.7 %fusion.158 = (bf16[256]{0:T(256)(128)(2,1)S(1)}, bf16[3072,256]{1,0:T(8,128)(2,1)S(1)}) fusion(f32[3072,256]{1,0:T(8,128)S(1)} %fusion.1, bf16[256,256]{1,0:T(8,128)(2,1)S(1)} %copy-done.9, bf16[1,3072,256]{2,1,0:T(8,128)(2,1)S(1)} %copy-done.6), kind=kOutput, calls=%fused_computation.163 | convolution fusion | flops 411303680 | bytes 6423040 | tf_op jit(solution)/shard_map/btd,cd->btc/dot_general | solution.py:96
  38.6 0.6 fusion.69
  39.3 0.6 fusion.85
  39.9 0.1 fusion.153
  40.0 0.1 collective-permute-start.5
  40.1 5.1 %collective-permute-start.4 = (bf16[1,1024,256]{2,1,0:T(8,128)(2,1)S(1)}, bf16[1,1024,256]{2,1,0:T(8,128)(2,1)S(1)}, u32[]{:S(2)}, u32[]{:S(2)}) collective-permute-start(bf16[1,1024,256]{2,1,0:T(8,128)(2,1)S(1)} %get-tuple-element.13), channel_id=1, source_target_pairs={{32,0},{64,32},{96,64},{128,96},{160,128},{192,160},{224,192},{0,2... | collective-permute-start | bytes 1572872 | tf_op jit(solution)/shard_map/ppermute | solution.py:21
  45.1 0.6 fusion.71
  45.8 0.6 convolution_bitcast_fusion.4
  46.4 1.2 fusion.97
  47.6 6.8 %collective-permute-done.5 = bf16[1,1024,256]{2,1,0:T(8,128)(2,1)S(1)} collective-permute-done((bf16[1,1024,256]{2,1,0:T(8,128)(2,1)S(1)}, bf16[1,1024,256]{2,1,0:T(8,128)(2,1)S(1)}, u32[]{:S(2)}, u32[]{:S(2)}) %collective-permute-start.5) | collective-permute-done | bytes 524320 | tf_op jit(solution)/shard_map/ppermute | solution.py:19
  54.3 0.6 convolution_bitcast_fusion.3
  54.9 0.7 fusion.12
  55.6 0.0 copy-start.2
  55.6 1.7 %fusion.157 = (bf16[256]{0:T(256)(128)(2,1)S(1)}, bf16[3072,256]{1,0:T(8,128)(2,1)S(1)}) fusion(f32[3072,256]{1,0:T(8,128)S(1)} %get-tuple-element.22, bf16[256,256]{1,0:T(8,128)(2,1)S(1)} %copy-done, bf16[1,3072,256]{2,1,0:T(8,128)(2,1)S(1)} %fusion.12), kind=kOutput, calls=%fused_computation.162 | convolution fusion | flops 411303680 | bytes 6423040 | tf_op jit(solution)/shard_map/btd,cd->btc/dot_general | solution.py:96
  57.3 0.6 fusion.73
  57.9 0.7 fusion.91
  58.7 0.6 fusion.75
  59.3 0.6 fusion.79
  60.0 0.1 reshape.171
  60.0 0.1 fusion.100
  60.1 18.5 %all_to_all.20 = bf16[8,264,256]{2,1,0:T(8,128)(2,1)S(1)} all-to-all(bf16[8,264,256]{2,1,0:T(8,128)(2,1)S(1)} %fusion.100), channel_id=1, replica_groups=mesh['angle'=8,'batch'=32] {'angle'}, dimensions={0} | all-to-all | bytes 2162688 | tf_op jit(solution)/shard_map/all_to_all | solution.py:58
  78.6 0.2 reduce.7
  78.8 0.1 reshape_squeeze.10
  79.0 24.2 %all_to_all.21 = bf16[32,8,384]{2,1,0:T(8,128)(2,1)S(1)} all-to-all(bf16[32,8,384]{2,1,0:T(8,128)(2,1)S(1)} %fusion.113), channel_id=1, replica_groups=mesh['angle'=8,'batch'=32] {'batch'}, dimensions={0} | all-to-all | bytes 393216 | tf_op jit(solution)/shard_map/all_to_all | solution.py:71
  103.3 0.7 broadcast_in_dim.18
  104.0 4.2 %all-to-all-start.2 = ((bf16[32,8,384]{2,1,0:T(8,128)(2,1)}), bf16[32,8,384]{2,1,0:T(8,128)(2,1)S(1)}, u32[]{:S(2)}, u32[]{:S(2)}) async-start(bf16[32,8,384]{2,1,0:T(8,128)(2,1)} %broadcast_in_dim.18), calls=%async_computation.2 | async-start | bytes 393216 | tf_op jit(solution)/shard_map/all_to_all | solution.py:73
  108.2 0.8 fusion.152
  109.0 0.3 collective-permute-start.7
  109.3 9.3 %all-to-all-done.2 = bf16[32,8,384]{2,1,0:T(8,128)(2,1)S(1)} async-done(((bf16[32,8,384]{2,1,0:T(8,128)(2,1)}), bf16[32,8,384]{2,1,0:T(8,128)(2,1)S(1)}, u32[]{:S(2)}, u32[]{:S(2)}) %all-to-all-start.2) | async-done | bytes 196640 | tf_op jit(solution)/shard_map/all_to_all | solution.py:73
  118.6 0.1 slice_reduce_fusion
  118.6 0.1 reshape_squeeze.9
  118.8 1.1 broadcast_in_dim.19
  119.8 3.6 %all-to-all-start.3 = ((bf16[8,264,256]{2,1,0:T(8,128)(2,1)}), bf16[8,264,256]{2,1,0:T(8,128)(2,1)S(1)}, u32[]{:S(2)}, u32[]{:S(2)}) async-start(bf16[8,264,256]{2,1,0:T(8,128)(2,1)} %broadcast_in_dim.19), calls=%async_computation.3 | async-start | bytes 2162688 | tf_op jit(solution)/shard_map/all_to_all | solution.py:77
  123.4 5.0 %collective-permute-start.6 = (bf16[1,512,256]{2,1,0:T(8,128)(2,1)}, bf16[1,512,256]{2,1,0:T(8,128)(2,1)S(1)}, u32[]{:S(2)}, u32[]{:S(2)}) collective-permute-start(bf16[1,512,256]{2,1,0:T(8,128)(2,1)} %get-tuple-element.11), channel_id=1, source_target_pairs={{32,0},{64,32},{96,64},{128,96},{160,128},{192,160},{224,192},{0,2... | collective-permute-start | bytes 786440 | tf_op jit(solution)/shard_map/ppermute | solution.py:21
  128.4 0.6 convolution_bitcast_fusion.1
  129.0 0.0 copy-start.3
  129.0 0.6 convolution_bitcast_fusion
  129.6 12.3 %collective-permute-done.6 = bf16[1,512,256]{2,1,0:T(8,128)(2,1)S(1)} collective-permute-done((bf16[1,512,256]{2,1,0:T(8,128)(2,1)}, bf16[1,512,256]{2,1,0:T(8,128)(2,1)S(1)}, u32[]{:S(2)}, u32[]{:S(2)}) %collective-permute-start.6) | collective-permute-done | bytes 262176 | tf_op jit(solution)/shard_map/ppermute | solution.py:21
  142.0 1.8 %fusion.11 = bf16[1,3072,256]{2,1,0:T(8,128)(2,1)} fusion(f32[1,3072,256]{2,1,0:T(8,128)S(1)} %convolution_bitcast_fusion, f32[1,3072,256]{2,1,0:T(8,128)S(1)} %convolution_bitcast_fusion.1, bf16[1,3072,256]{2,1,0:T(8,128)(2,1)S(1)} %copy-done.3, bf16[1,512,256]{2,1,0:T(8,128)(2,1)S(1)} %collective-permute-done.6, bf16[1,3072,256]{2,1,0:T(8,128)(2,1)S(1)} %bitcast.206, ...), kind=kOutput, calls=%fused_computation.24 | convolution fusion | flops 409731072 | bytes 11403264 | tf_op jit(solution)/shard_map/btd,cd->btc/dot_general | solution.py:87
  143.8 0.2 convert_element_type.77
  144.0 0.8 slice_bitcast_fusion
  144.8 0.6 squeeze.42
  145.5 0.6 squeeze.44
  146.1 1.3 fusion.156
  (28 shorter events, 0.2 us)
Async XLA Ops:
  0.6 18.8 %copy-start = (bf16[256,256]{1,0:T(8,128)(2,1)S(1)}, bf16[256,256]{1,0:T(8,128)(2,1)}, u32[]{:S(2)}) copy-start(bf16[256,256]{1,0:T(8,128)(2,1)} %param.12) | copy-start | bytes 393220
  1.8 11.1 %collective-permute-start.1 = (bf16[1,512,256]{2,1,0:T(8,128)(2,1)S(1)}, bf16[1,512,256]{2,1,0:T(8,128)(2,1)S(1)}, u32[]{:S(2)}, u32[]{:S(2)}) collective-permute-start(bf16[1,512,256]{2,1,0:T(8,128)(2,1)S(1)} %get-tuple-element.18), channel_id=1, source_target_pairs={{32,0},{64,32},{96,64},{128,96},{160,128},{192,160},{224,192},{0,2... | collective-permute-start | bytes 786440 | tf_op jit(solution)/shard_map/ppermute | solution.py:21
  7.9 5.0 %copy-start.1 = (bf16[1,3072,256]{2,1,0:T(8,128)(2,1)S(1)}, bf16[1,3072,256]{2,1,0:T(8,128)(2,1)}, u32[]{:S(2)}) copy-start(bf16[1,3072,256]{2,1,0:T(8,128)(2,1)} %param.8) | copy-start | bytes 4718596
  7.9 5.0 %copy-start.4 = (bf16[3,256,256]{2,1,0:T(8,128)(2,1)S(1)}, bf16[3,256,256]{2,1,0:T(8,128)(2,1)}, u32[]{:S(2)}) copy-start(bf16[3,256,256]{2,1,0:T(8,128)(2,1)} %param.10) | copy-start | bytes 1179652
  7.9 10.5 %collective-permute-start = (bf16[1,512,256]{2,1,0:T(8,128)(2,1)S(1)}, bf16[1,512,256]{2,1,0:T(8,128)(2,1)S(1)}, u32[]{:S(2)}, u32[]{:S(2)}) collective-permute-start(bf16[1,512,256]{2,1,0:T(8,128)(2,1)S(1)} %get-tuple-element.17), channel_id=1, source_target_pairs={{0,32},{32,64},{64,96},{96,128},{128,160},{160,192},{192,224},{224... | collective-permute-start | bytes 786440 | tf_op jit(solution)/shard_map/ppermute | solution.py:19
  10.0 8.3 %copy-start.7 = (f32[256]{0:T(256)S(1)}, f32[256]{0:T(256)}, u32[]{:S(2)}) copy-start(f32[256]{0:T(256)} %param.11) | copy-start | bytes 3076
  20.0 1.6 %copy-start.5 = (bf16[3,256,256]{2,1,0:T(8,128)(2,1)S(1)}, bf16[3,256,256]{2,1,0:T(8,128)(2,1)}, u32[]{:S(2)}) copy-start(bf16[3,256,256]{2,1,0:T(8,128)(2,1)} %param.13) | copy-start | bytes 1179652
  20.1 11.6 %collective-permute-start.3 = (bf16[1,1024,256]{2,1,0:T(8,128)(2,1)S(1)}, bf16[1,1024,256]{2,1,0:T(8,128)(2,1)S(1)}, u32[]{:S(2)}, u32[]{:S(2)}) collective-permute-start(bf16[1,1024,256]{2,1,0:T(8,128)(2,1)S(1)} %get-tuple-element.16), channel_id=1, source_target_pairs={{32,0},{64,32},{96,64},{128,96},{160,128},{192,160},{224,192},{0,2... | collective-permute-start | bytes 1572872 | tf_op jit(solution)/shard_map/ppermute | solution.py:21
  21.1 15.2 %collective-permute-start.2 = (bf16[1,1024,256]{2,1,0:T(8,128)(2,1)S(1)}, bf16[1,1024,256]{2,1,0:T(8,128)(2,1)S(1)}, u32[]{:S(2)}, u32[]{:S(2)}) collective-permute-start(bf16[1,1024,256]{2,1,0:T(8,128)(2,1)S(1)} %get-tuple-element.15), channel_id=1, source_target_pairs={{0,32},{32,64},{64,96},{96,128},{128,160},{160,192},{192,224},{224... | collective-permute-start | bytes 1572872 | tf_op jit(solution)/shard_map/ppermute | solution.py:19
  22.2 14.1 %copy-start.8 = (f32[256]{0:T(256)S(1)}, f32[256]{0:T(256)}, u32[]{:S(2)}) copy-start(f32[256]{0:T(256)} %param.14) | copy-start | bytes 3076
  32.3 4.7 %copy-start.6 = (bf16[1,3072,256]{2,1,0:T(8,128)(2,1)S(1)}, bf16[1,3072,256]{2,1,0:T(8,128)(2,1)}, u32[]{:S(2)}) copy-start(bf16[1,3072,256]{2,1,0:T(8,128)(2,1)} %param.9) | copy-start | bytes 4718596
  32.3 4.6 %copy-start.9 = (bf16[256,256]{1,0:T(8,128)(2,1)S(1)}, bf16[256,256]{1,0:T(8,128)(2,1)}, u32[]{:S(2)}) copy-start(bf16[256,256]{1,0:T(8,128)(2,1)} %param.15) | copy-start | bytes 393220
  40.0 14.4 %collective-permute-start.5 = (bf16[1,1024,256]{2,1,0:T(8,128)(2,1)S(1)}, bf16[1,1024,256]{2,1,0:T(8,128)(2,1)S(1)}, u32[]{:S(2)}, u32[]{:S(2)}) collective-permute-start(bf16[1,1024,256]{2,1,0:T(8,128)(2,1)S(1)} %get-tuple-element.14), channel_id=1, source_target_pairs={{0,32},{32,64},{64,96},{96,128},{128,160},{160,192},{192,224},{224... | collective-permute-start | bytes 1572872 | tf_op jit(solution)/shard_map/ppermute | solution.py:19
  40.1 14.9 %collective-permute-start.4 = (bf16[1,1024,256]{2,1,0:T(8,128)(2,1)S(1)}, bf16[1,1024,256]{2,1,0:T(8,128)(2,1)S(1)}, u32[]{:S(2)}, u32[]{:S(2)}) collective-permute-start(bf16[1,1024,256]{2,1,0:T(8,128)(2,1)S(1)} %get-tuple-element.13), channel_id=1, source_target_pairs={{32,0},{64,32},{96,64},{128,96},{160,128},{192,160},{224,192},{0,2... | collective-permute-start | bytes 1572872 | tf_op jit(solution)/shard_map/ppermute | solution.py:21
  55.6 3.7 %copy-start.2 = (bf16[1,3072,256]{2,1,0:T(8,128)(2,1)}, bf16[1,3072,256]{2,1,0:T(8,128)(2,1)S(1)}, u32[]{:S(2)}) copy-start(bf16[1,3072,256]{2,1,0:T(8,128)(2,1)S(1)} %fusion.12) | copy-start | bytes 4718596
  104.0 14.6 %all-to-all-start.2 = ((bf16[32,8,384]{2,1,0:T(8,128)(2,1)}), bf16[32,8,384]{2,1,0:T(8,128)(2,1)S(1)}, u32[]{:S(2)}, u32[]{:S(2)}) async-start(bf16[32,8,384]{2,1,0:T(8,128)(2,1)} %broadcast_in_dim.18), calls=%async_computation.2 | async-start | bytes 393216 | tf_op jit(solution)/shard_map/all_to_all | solution.py:73
  109.0 20.0 %collective-permute-start.7 = (bf16[1,512,256]{2,1,0:T(8,128)(2,1)}, bf16[1,512,256]{2,1,0:T(8,128)(2,1)S(1)}, u32[]{:S(2)}, u32[]{:S(2)}) collective-permute-start(bf16[1,512,256]{2,1,0:T(8,128)(2,1)} %get-tuple-element.12), channel_id=1, source_target_pairs={{0,32},{32,64},{64,96},{96,128},{128,160},{160,192},{192,224},{224... | collective-permute-start | bytes 786440 | tf_op jit(solution)/shard_map/ppermute | solution.py:19
  119.8 24.0 %all-to-all-start.3 = ((bf16[8,264,256]{2,1,0:T(8,128)(2,1)}), bf16[8,264,256]{2,1,0:T(8,128)(2,1)S(1)}, u32[]{:S(2)}, u32[]{:S(2)}) async-start(bf16[8,264,256]{2,1,0:T(8,128)(2,1)} %broadcast_in_dim.19), calls=%async_computation.3 | async-start | bytes 2162688 | tf_op jit(solution)/shard_map/all_to_all | solution.py:77
  123.4 18.6 %collective-permute-start.6 = (bf16[1,512,256]{2,1,0:T(8,128)(2,1)}, bf16[1,512,256]{2,1,0:T(8,128)(2,1)S(1)}, u32[]{:S(2)}, u32[]{:S(2)}) collective-permute-start(bf16[1,512,256]{2,1,0:T(8,128)(2,1)} %get-tuple-element.11), channel_id=1, source_target_pairs={{32,0},{64,32},{96,64},{128,96},{160,128},{192,160},{224,192},{0,2... | collective-permute-start | bytes 786440 | tf_op jit(solution)/shard_map/ppermute | solution.py:21
  129.0 13.0 %copy-start.3 = (bf16[1,3072,256]{2,1,0:T(8,128)(2,1)S(1)}, bf16[1,3072,256]{2,1,0:T(8,128)(2,1)}, u32[]{:S(2)}) copy-start(bf16[1,3072,256]{2,1,0:T(8,128)(2,1)} %copy-done.2) | copy-start | bytes 4718596

commit v2 on v0

v2 whole, which is shorter than its diff:
```python
import math

import jax
import jax.numpy as jnp
from jax import lax
from jax.experimental import pallas as pl
from jax.experimental.pallas import tpu as pltpu
from jax.sharding import Mesh, PartitionSpec as P

BLOCK = 512
RING = ("xh", "y")
REST = ("z", "xl")
BF, F32 = jnp.bfloat16, jnp.float32
C = 256


def dot(a, b):
    return jnp.dot(a, b, preferred_element_type=F32)


def t_dot(a, b):
    return lax.dot_general(a, b, (((0,), (0,)), ((), ())), preferred_element_type=F32)


def normal_cdf(v):
    return 0.5 * (1.0 + lax.erf(v * math.sqrt(0.5)))


def slope_of(v, cdf):
    return cdf + v * jnp.exp(-0.5 * v * v) * (1.0 / math.sqrt(2.0 * math.pi))


def taps(at, j, hop):
    return jnp.concatenate([at(j - hop), at(j), at(j + hop)], axis=1)


def cut_kernel(s_ref, left_ref, right_ref, sems):
    n = s_ref.shape[0]
    one = pltpu.make_async_copy(s_ref.at[pl.ds(0, 3)], left_ref, sems.at[0])
    two = pltpu.make_async_copy(s_ref.at[pl.ds(n - 3, 3)], right_ref, sems.at[1])
    one.start()
    two.start()
    one.wait()
    two.wait()


def near_kernel(
    s_ref, w_ref, bias_ref, proj_ref, w2_ref, proj2_ref,
    act_ref, slope_ref, mid_ref, w_t_ref, w2_t_ref, proj_t_ref, proj2_t_ref,
):
    at = lambda j: s_ref[j]

    def product(j):
        return dot(taps(at, j, 1), w_ref[...]) + bias_ref[...]

    pre = product(1)
    for j in range(1, 5):
        after = product(j + 1) if j < 4 else None
        cdf = normal_cdf(pre)
        act = (pre * cdf).astype(BF)
        act_ref[j - 1] = act
        slope_ref[j - 1] = slope_of(pre, cdf).astype(BF)
        mid_ref[j - 1] = (s_ref[j].astype(F32) + dot(act, proj_ref[...])).astype(BF)
        pre = after
    for k in range(3):
        to = slice((2 - k) * C, (3 - k) * C)
        w_t_ref[to] = w_ref[k * C : (k + 1) * C].T
        w2_t_ref[to] = w2_ref[k * C : (k + 1) * C].T
    proj_t_ref[...] = proj_ref[...].T
    proj2_t_ref[...] = proj2_ref[...].T


def far_kernel(
    s_ref, left_ref, right_ref, up_ref, near_ref, w_ref, bias_ref, proj_ref, w2_ref, bias2_ref, proj2_ref,
    act_ref, slope_ref, mid_ref, act2_ref, delta_ref, to_left_ref, to_right_ref,
):
    def at(j):
        return left_ref[j + 3] if j < 0 else right_ref[j - 6] if j > 5 else s_ref[j]

    def mid_at(j):
        return mid_ref[j + 2] if j < 1 else mid_ref[j - 2] if j > 4 else near_ref[j - 1]

    def product(j):
        return dot(taps(at, j, 1), w_ref[...]) + bias_ref[...]

    def product2(j):
        return dot(taps(mid_at, j, 2), w2_ref[...]) + bias2_ref[...]

    order = (0, 5, -2, 7, -1, 6)
    order2 = (2, 3, 0, 5, 1, 4)
    pre = product(order[0])
    for i, j in enumerate(order):
        after = product(order[i + 1]) if i < 5 else product2(order2[0])
        cdf = normal_cdf(pre)
        act = (pre * cdf).astype(BF)
        if j in (0, 5):
            act_ref[j // 5] = act
            slope_ref[j // 5] = slope_of(pre, cdf).astype(BF)
        mid = (at(j).astype(F32) + dot(act, proj_ref[...])).astype(BF)
        mid_ref[j + 2 if j < 1 else j - 2] = mid
        pre = after
    for i, j in enumerate(order2):
        back = dot(up_ref[j], proj2_ref[...])
        after = product2(order2[i + 1]) if i < 5 else None
        cdf = normal_cdf(pre)
        act2_ref[j] = (pre * cdf).astype(BF)
        delta = (back * slope_of(pre, cdf)).astype(BF)
        delta_ref[j] = delta
        if j < 2:
            to_left_ref[j] = delta
        if j > 3:
            to_right_ref[j - 4] = delta
        pre = after


def add_grads(sum_ref, j, cells, delta, act, up):
    conv = t_dot(cells, delta)
    proj = t_dot(act, up)
    if j == 0:
        sum_ref[: 3 * C] = conv
        sum_ref[3 * C :] = proj
    else:
        sum_ref[: 3 * C] += conv
        sum_ref[3 * C :] += proj


def put_halves(sum_ref, base, away_ref, mine_ref):
    core = lax.axis_index("core")
    half = 2 * C
    to = slice(base, base + half)
    mine_ref[to] = sum_ref[pl.ds(pl.multiple_of(core * half, half), half)].astype(BF)
    away_ref[to] = sum_ref[pl.ds(pl.multiple_of((1 - core) * half, half), half)].astype(BF)


def grads_b_kernel(near_ref, far_ref, act_ref, up_ref, delta_ref, sum_ref, bias_ref):
    def mid_at(j):
        return far_ref[j + 2] if j < 1 else far_ref[j - 2] if j > 4 else near_ref[j - 1]

    bias = jnp.zeros((1, C), F32)
    for j in range(6):
        delta = delta_ref[j]
        add_grads(sum_ref, j, taps(mid_at, j, 2), delta, act_ref[j], up_ref[j])
        bias += jnp.sum(delta.astype(F32), axis=0, keepdims=True)
    bias_ref[...] = bias


def lower_b_kernel(
    delta_ref, left_ref, right_ref, up_ref, w_ref, proj_ref, slope_ref, slope_far_ref,
    grad_ref, out_ref, to_left_ref, to_right_ref,
):
    def at(j):
        return left_ref[j + 2] if j < 0 else right_ref[j - 6] if j > 5 else delta_ref[j]

    def product(j):
        return (up_ref[j].astype(F32) + dot(taps(at, j, 2), w_ref[...])).astype(BF)

    order = (0, 5, 1, 4, 2, 3)
    below = product(order[0])
    for i, j in enumerate(order):
        after = product(order[i + 1]) if i < 5 else None
        grad_ref[j] = below
        slope = slope_far_ref[j // 5] if j in (0, 5) else slope_ref[j - 1]
        delta = (dot(below, proj_ref[...]) * slope.astype(F32)).astype(BF)
        out_ref[j] = delta
        if j == 0:
            to_left_ref[0] = delta
        if j == 5:
            to_right_ref[0] = delta
        below = after


def grads_a_kernel(
    s_ref, left_ref, right_ref, act_ref, act_far_ref, up_ref, delta_ref, other_ref, other_bias_ref,
    away_ref, mine_ref, sum_ref,
):
    def at(j):
        return left_ref[2] if j < 0 else right_ref[0] if j > 5 else s_ref[j]

    bias = jnp.zeros((1, C), F32)
    for j in range(6):
        delta = delta_ref[j]
        act = act_far_ref[j // 5] if j in (0, 5) else act_ref[j - 1]
        add_grads(sum_ref, j, taps(at, j, 1), delta, act, up_ref[j])
        bias += jnp.sum(delta.astype(F32), axis=0, keepdims=True)
    put_halves(other_ref, 0, away_ref, mine_ref)
    put_halves(sum_ref, 2 * C, away_ref, mine_ref)
    row = lax.broadcasted_iota(jnp.int32, (16, C), 0)
    tail = jnp.where(row == 0, jnp.broadcast_to(other_bias_ref[...], (16, C)), 0.0)
    tail = jnp.where(row == 1, jnp.broadcast_to(bias, (16, C)), tail).astype(BF)
    mine_ref[4 * C :] = tail
    away_ref[4 * C :] = tail


def pair_kernel(mine_ref, near_ref, out_ref):
    n, rows, _ = out_ref.shape
    chunk = (rows - 16) // 2
    tail = (mine_ref[4 * C :].astype(F32) + near_ref[4 * C :].astype(F32)).astype(BF)
    for i in range(n):
        for base, to in ((0, 0), (2 * C, chunk)):
            part = slice(base + i * chunk, base + (i + 1) * chunk)
            total = mine_ref[part].astype(F32) + near_ref[part].astype(F32)
            out_ref[i, to : to + chunk] = total.astype(BF)
        out_ref[i, 2 * chunk :] = tail


def rest_kernel(got_ref, left_ref, right_ref, out_ref):
    total = jnp.sum(got_ref[...].astype(F32), axis=0).astype(BF)
    for i in range(out_ref.shape[0]):
        out_ref[i] = total


def ring_kernel(got_ref, out_ref, bias_b_ref, bias_a_ref):
    total = jnp.sum(got_ref[...].astype(F32), axis=0)
    chunk = out_ref.shape[1]
    own = total[:chunk].astype(BF)
    for i in range(out_ref.shape[0]):
        out_ref[i] = own
    bias_b_ref[...] = total[chunk : chunk + 1]
    bias_a_ref[...] = total[chunk + 1 : chunk + 2]


def tail_kernel(mine_ref, other_ref, conv_b_ref, proj_b_ref, conv_a_ref, proj_a_ref):
    core = lax.axis_index("core")
    n, rows, _ = mine_ref.shape
    chunk = rows // 2

    def put(low, high):
        for i in range(n // 2):
            to = slice(i * chunk, (i + 1) * chunk)
            for part, conv, proj in ((0, conv_b_ref, proj_b_ref), (1, conv_a_ref, proj_a_ref)):
                of = slice(part * chunk, (part + 1) * chunk)
                conv[0, to] = low[i, of].astype(F32)
                conv[1, to] = low[i + n // 2, of].astype(F32)
                conv[2, to] = high[i, of].astype(F32)
                proj[to] = high[i + n // 2, of].astype(F32)

    @pl.when(core == 0)
    def _():
        put(mine_ref, other_ref)

    @pl.when(core != 0)
    def _():
        put(other_ref, mine_ref)


def lower_a_kernel(delta_ref, left_ref, right_ref, up_ref, w_ref, out_ref):
    def at(j):
        return left_ref[0] if j < 0 else right_ref[0] if j > 5 else delta_ref[j]

    for j in (1, 2, 3, 4, 0, 5):
        below = up_ref[j].astype(F32) + dot(taps(at, j, 1), w_ref[...])
        out_ref[j] = below.astype(BF)


def call(kernel, outs, args, flops=0, scratch=(), loose=0):
    vmem = pl.BlockSpec(memory_space=pltpu.VMEM)
    moved = sum(a.size * a.dtype.itemsize for a in args) + sum(
        math.prod(s) * jnp.dtype(t).itemsize for s, t in outs
    )
    return pl.pallas_call(
        kernel,
        out_shape=[jax.ShapeDtypeStruct(s, t) for s, t in outs],
        in_specs=[vmem] * (len(args) - loose) + [pl.BlockSpec(memory_space=pl.ANY)] * loose,
        out_specs=[vmem] * len(outs),
        scratch_shapes=list(scratch),
        compiler_params=pltpu.CompilerParams(vmem_limit_bytes=32 * 2**20),
        cost_estimate=pl.CostEstimate(flops=flops, bytes_accessed=moved, transcendentals=0),
        name=kernel.__name__[: -len("_kernel")],
    )(*args)


def from_left(cells):
    n = lax.axis_size(RING)
    return lax.ppermute(cells, RING, [(i, (i + 1) % n) for i in range(n)])


def from_right(cells):
    n = lax.axis_size(RING)
    return lax.ppermute(cells, RING, [((i + 1) % n, i) for i in range(n)])


def across(cells):
    return lax.ppermute(cells, "core", [(0, 1), (1, 0)])


def on_device(signals, cotangent, kernel_a, bias_a, proj_a, kernel_b, bias_b, proj_b):
    batch, length, channels = signals.shape
    unit = 2 * BLOCK * C * C
    cells = signals.reshape(-1, BLOCK, C)
    up = cotangent.reshape(-1, BLOCK, C)
    rest, ring = lax.axis_size(REST), lax.axis_size(RING)
    wa, wb = kernel_a.reshape(3 * C, C), kernel_b.reshape(3 * C, C)
    ba, bb = bias_a.reshape(1, C), bias_b.reshape(1, C)

    def like(n):
        return ((n, BLOCK, C), BF)

    to_left, to_right = call(
        cut_kernel, [like(3)] * 2, [cells], scratch=[pltpu.SemaphoreType.DMA((2,))], loose=1
    )
    s_left, s_right = from_left(to_right), from_right(to_left)
    act_near, slope_near, mid_near, wa_t, wb_t, pa_t, pb_t = call(
        near_kernel,
        [like(4)] * 3 + [((3 * C, C), BF)] * 2 + [((C, C), BF)] * 2,
        [cells, wa, ba, proj_a, wb, proj_b],
        16 * unit,
    )
    act_far, slope_far, mid_far, act_b, delta_b, to_left, to_right = call(
        far_kernel,
        [like(2), like(2), like(6), like(6), like(6), like(2), like(2)],
        [cells, s_left, s_right, up, mid_near, wa, ba, proj_a, wb, bb, pb_t],
        48 * unit,
    )
    d_left, d_right = from_left(to_right), from_right(to_left)
    sum_b, part_bias_b = call(
        grads_b_kernel,
        [((4 * C, C), F32), ((1, C), F32)],
        [mid_near, mid_far, act_b, up, delta_b],
        24 * unit,
    )
    grad, delta_a, to_left, to_right = call(
        lower_b_kernel,
        [like(6), like(6), like(1), like(1)],
        [delta_b, d_left, d_right, up, wb_t, pa_t, slope_near, slope_far],
        24 * unit,
    )
    e_left, e_right = from_left(to_right), from_right(to_left)
    away, mine = call(
        grads_a_kernel,
        [((4 * C + 16, C), BF)] * 2,
        [cells, s_left, s_right, act_near, act_far, grad, delta_a, sum_b, part_bias_b],
        24 * unit,
        [pltpu.VMEM((4 * C, C), F32)],
    )
    chunk = 2 * C // rest
    (sent,) = call(pair_kernel, [((rest, 2 * chunk + 16, C), BF)], [mine, across(away)])
    got = lax.all_to_all(sent, REST, 0, 0)
    (sent,) = call(
        rest_kernel, [((ring, 2 * chunk + 16, C), BF)], [got, e_left, e_right], loose=2
    )
    got = lax.all_to_all(sent, RING, 0, 0)
    sent, sum_bias_b, sum_bias_a = call(
        ring_kernel, [((rest, 2 * chunk, C), BF), ((1, C), F32), ((1, C), F32)], [got]
    )
    mine = lax.all_to_all(sent, REST, 0, 0)
    conv_b, grad_proj_b, conv_a, grad_proj_a = call(
        tail_kernel, [((3, C, C), F32), ((C, C), F32)] * 2, [mine, across(mine)]
    )
    (out,) = call(lower_a_kernel, [like(6)], [delta_a, e_left, e_right, grad, wa_t], 18 * unit)
    return (
        out.reshape(batch, length, channels),
        conv_a,
        sum_bias_a.reshape(C),
        grad_proj_a,
        conv_b,
        sum_bias_b.reshape(C),
        grad_proj_b,
    )


def solution(mesh):
    split = Mesh(mesh.devices.reshape(2, 4, 8, 2, 2), RING + REST + ("core",))
    data = P(REST + ("core",), RING, None)
    return jax.shard_map(
        on_device,
        mesh=split,
        in_specs=(data, data, P(), P(), P(), P(), P(), P()),
        out_specs=(data, P(), P(), P(), P(), P(), P()),
        check_vma=False,
    )
```

time: 346 us -> 128 us (0.37)
  waiting for transfers between devices: 190 us -> 32.8 us
  blocking collectives: 87.6 us -> 33.3 us
  matrix products: 25.5 us -> 0 us
  starting transfers between devices: 18.6 us -> 37.6 us
  Pallas kernels: 0 us -> 18.1 us
  between operations: 14.3 us -> 0.79 us
    psum x1 -> x0, waiting for transfers between devices: 168 us -> none  [reduce_grads(): return lax.psum((grads[0], grads[1], grads[2]), ('angle', 'batch'))]
    psum x1 -> x0, blocking collectives: 87.6 us -> none  [reduce_grads(): return lax.psum((grads[0], grads[1], grads[2]), ('angle', 'batch'))]
    all_to_all x0 -> x2, blocking collectives: none -> 33.3 us  [the longest x1 18.4 us: on_device(): mine = lax.all_to_all(sent, REST, 0, 0)]
    dot_general x23 -> x0, matrix products: 25.5 us -> none  [the longest x6 9.49 us: lower_grad(): jnp.einsum('btd,cd->btc', window, kernel[k], preferred_element_type=jnp.f...]
    pallas_call x0 -> x11, Pallas kernels: none -> 18.1 us  [call(): pl.pallas_call(kernel, out_shape=[jax.ShapeDtypeStruct(s, t) for s, t in...]
    all_to_all x0 -> x1, starting transfers between devices: none -> 10.8 us  [on_device(): got = lax.all_to_all(sent, REST, 0, 0)]
    ppermute x8, starting transfers between devices: 18.5 us -> 26.8 us  [the longest x3 14.8 us: from_right(): return lax.ppermute(cells, RING, [((i + 1) % n, i) for i in range(n)])]
    ppermute x8, waiting for transfers between devices: 21.7 us -> 29.6 us  [the longest x3 26.6 us: from_left(): return lax.ppermute(cells, RING, [(i, (i + 1) % n) for i in range(n)])]
  transfers between devices with their start and end apart: 9 -> 9, of which waited for: 5 -> 6; matrix products, arithmetic and copies ran while one was open for 5% -> 0% of each run, Pallas kernels for 0% -> 5%
where the time goes in v2:
time: 128 us
  starting transfers between devices  37.6 us (29%)
  blocking collectives  33.3 us (26%)
  waiting for transfers between devices  32.8 us (26%)
  Pallas kernels  18.1 us (14%)
  local copies, waits for them, and re-layouts  5.45 us (4%)
    ppermute x3, waiting for transfers between devices, from_left(): return lax.ppermute(cells, RING, [(i, (i + 1) % n) for i in range(n)])  26.6 us
    all_to_all x1, blocking collectives, on_device(): mine = lax.all_to_all(sent, REST, 0, 0)  18.4 us
    pallas_call x11, Pallas kernels, call(): pl.pallas_call(kernel, out_shape=[jax.ShapeDtypeStruct(s, t) for s, t in...  18.1 us
    all_to_all x1, blocking collectives, on_device(): got = lax.all_to_all(sent, RING, 0, 0)  15 us
    ppermute x3, starting transfers between devices, from_right(): return lax.ppermute(cells, RING, [((i + 1) % n, i) for i in range(n)])  14.8 us
    all_to_all x1, starting transfers between devices, on_device(): got = lax.all_to_all(sent, REST, 0, 0)  10.8 us
    ppermute x2, starting transfers between devices, across(): return lax.ppermute(cells, 'core', [(0, 1), (1, 0)])  9.45 us
    unnamed x34, local copies, waits for them, and re-layouts  5.45 us
  transfers between devices with their start and end apart: 9, of which 6 were waited for; matrix products, arithmetic and copies ran while one was open for 0% of the time, Pallas kernels for 5%

profile of v2, /device:TPU:1, one launch (start us, length us, event | category | flops | bytes accessed | tf_op | source)
XLA Modules:
  0.0 128.0 jit_solution(1567447989507189488)
XLA Ops:
  0.6 0.0 copy-start.15
  0.6 0.0 copy-start.1
  0.7 1.4 %copy-done.1 = bf16[1,3072,256]{2,1,0:T(8,128)(2,1)S(1)} copy-done((bf16[1,3072,256]{2,1,0:T(8,128)(2,1)S(1)}, bf16[1,3072,256]{2,1,0:T(8,128)(2,1)}, u32[]{:S(2)}) %copy-start.1) | copy-done | bytes 1572888
  2.1 0.0 copy-start.9
  2.1 0.0 copy-start.10
  2.1 0.0 copy-start.13
  2.1 0.1 cut.1
  2.2 2.2 %collective-permute-start = (bf16[3,512,256]{2,1,0:T(8,128)(2,1)S(1)}, bf16[3,512,256]{2,1,0:T(8,128)(2,1)S(1)}, u32[]{:S(2)}, u32[]{:S(2)}) collective-permute-start(bf16[3,512,256]{2,1,0:T(8,128)(2,1)S(1)} %get-tuple-element.38), channel_id=1, source_target_pairs={{0,32},{32,64},{64,96},{96,128},{128,160},{160,192},{192,224},{224... | collective-permute-start | bytes 2359304 | tf_op jit(solution)/shard_map/ppermute | solution.py:274
  4.4 4.0 %collective-permute-start.1 = (bf16[3,512,256]{2,1,0:T(8,128)(2,1)S(1)}, bf16[3,512,256]{2,1,0:T(8,128)(2,1)S(1)}, u32[]{:S(2)}, u32[]{:S(2)}) collective-permute-start(bf16[3,512,256]{2,1,0:T(8,128)(2,1)S(1)} %get-tuple-element.39), channel_id=1, source_target_pairs={{32,0},{64,32},{96,64},{128,96},{160,128},{192,160},{224,192},{0,2... | collective-permute-start | bytes 2359304 | tf_op jit(solution)/shard_map/ppermute | solution.py:279
  8.4 0.0 copy-done.15
  8.4 0.0 copy-done.9
  8.4 0.0 copy-done.10
  8.4 0.0 copy-done.13
  8.4 0.0 copy-done.14
  8.4 0.0 copy-start
  8.4 0.0 copy-start.16
  8.4 1.8 %near.1 = (bf16[4,512,256]{2,1,0:T(8,128)(2,1)S(1)}, bf16[4,512,256]{2,1,0:T(8,128)(2,1)S(1)}, bf16[4,512,256]{2,1,0:T(8,128)(2,1)S(1)}, bf16[768,256]{1,0:T(8,1...) custom-call(bf16[6,512,256]{2,1,0:T(8,128)(2,1)S(1)} %bitcast.13, ...), custom_call_target="tpu_custom_call" | custom-call | flops 1073741824 | bytes 6816768 | tf_op jit(solution)/shard_map/near/pallas_call | solution.py:260
  10.3 0.0 copy-start.7
  10.3 0.7 copy-done.7
  11.0 12.5 %collective-permute-done.left_ref = bf16[3,512,256]{2,1,0:T(8,128)(2,1)S(1)} collective-permute-done((bf16[3,512,256]{2,1,0:T(8,128)(2,1)S(1)}, bf16[3,512,256]{2,1,0:T(8,128)(2,1)S(1)}, u32[]{:S(2)}, u32[]{:S(2)}) %collective-permute-start) | collective-permute-done | bytes 786464 | tf_op jit(solution)/shard_map/ppermute | solution.py:274
  23.6 0.0 collective-permute-done.1.right_ref
  23.6 0.0 copy-done
  23.6 0.0 copy-done.16
  23.6 4.3 %far.1 = (bf16[2,512,256]{2,1,0:T(8,128)(2,1)S(1)}, bf16[2,512,256]{2,1,0:T(8,128)(2,1)S(1)}, bf16[6,512,256]{2,1,0:T(8,128)(2,1)S(1)}, bf16[6,512,256]{2,1,0:T(...) custom-call(bf16[6,512,256]{2,1,0:T(8,128)(2,1)S(1)} %bitcast.14, ...), custom_call_target="tpu_custom_call" | custom-call | flops 3221225472 | bytes 13633536 | tf_op jit(solution)/shard_map/far/pallas_call | solution.py:260
  27.9 0.3 collective-permute-start.2
  28.2 5.0 %collective-permute-start.3 = (bf16[2,512,256]{2,1,0:T(8,128)(2,1)S(1)}, bf16[2,512,256]{2,1,0:T(8,128)(2,1)S(1)}, u32[]{:S(2)}, u32[]{:S(2)}) collective-permute-start(bf16[2,512,256]{2,1,0:T(8,128)(2,1)S(1)} %get-tuple-element.44), channel_id=1, source_target_pairs={{32,0},{64,32},{96,64},{128,96},{160,128},{192,160},{224,192},{0,2... | collective-permute-start | bytes 1572872 | tf_op jit(solution)/shard_map/ppermute | solution.py:279
  33.2 1.9 %grads_b.1 = (f32[1024,256]{1,0:T(8,128)S(1)}, f32[1,256]{1,0:T(1,128)S(1)}) custom-call(bf16[4,512,256]{2,1,0:T(8,128)(2,1)S(1)} %get-tuple-element.40.near_ref, bf16[6,512,256]{2,1,0:T(8,128)(2,1)S(1)} %get-tuple-element.56.far_ref, bf16[6,512,256]{2,1,0:T(8,128)(2,1)S(1)} %get-tuple-element.57.act_ref, bf16[6,512,256]{2,1,0:T(8,128)(2,1)S(1)} %bitcast.10, ...), custom_call_target="tpu_custom_call" | custom-call | flops 1610612736 | bytes 8389632 | tf_op jit(solution)/shard_map/grads_b/pallas_call | solution.py:260
  35.1 6.7 %collective-permute-done.2.left_ref = bf16[2,512,256]{2,1,0:T(8,128)(2,1)S(1)} collective-permute-done((bf16[2,512,256]{2,1,0:T(8,128)(2,1)S(1)}, bf16[2,512,256]{2,1,0:T(8,128)(2,1)S(1)}, u32[]{:S(2)}, u32[]{:S(2)}) %collective-permute-start.2) | collective-permute-done | bytes 524320 | tf_op jit(solution)/shard_map/ppermute | solution.py:274
  41.8 0.0 collective-permute-done.3.right_ref
  41.8 0.0 copy-start.2
  41.8 2.0 %lower_b.1 = (bf16[6,512,256]{2,1,0:T(8,128)(2,1)S(1)}, bf16[6,512,256]{2,1,0:T(8,128)(2,1)S(1)}, bf16[1,512,256]{2,1,0:T(8,128)(2,1)S(1)}, bf16[1,512,256]{2,1,0:T(8,128)(2,1)S(1)}) custom-call(bf16[6,512,256]{2,1,0:T(8,128)(2,1)S(1)} %get-tuple-element.42.delta_ref, bf16[2,512,256]{2,1,0:T(8,128)(2,1)S(1)} %collective-permute-done.2.left_ref, ...), custom_call_target="tpu_custom_call" | custom-call | flops 1610612736 | bytes 9961472 | tf_op jit(solution)/shard_map/lower_b/pallas_call | solution.py:260
  43.8 0.0 copy-start.11
  43.8 0.0 copy-start.12
  43.8 0.7 copy-done.11
  44.5 0.1 copy-done.12
  44.6 0.0 copy-done.2
  44.6 2.0 %grads_a.1 = (bf16[1040,256]{1,0:T(8,128)(2,1)S(1)}, bf16[1040,256]{1,0:T(8,128)(2,1)S(1)}) custom-call(bf16[6,512,256]{2,1,0:T(8,128)(2,1)S(1)} %bitcast.15, bf16[3,512,256]{2,1,0:T(8,128)(2,1)S(1)} %collective-permute-done.left_ref, bf16[3,512,256]{2,1,0:T(8,128)(2,1)S(1)} %collective-permute-done.1.right_ref, ...), custom_call_target="tpu_custom_call" | custom-call | flops 1610612736 | bytes 9978880 | tf_op jit(solution)/shard_map/grads_a/pallas_call | solution.py:260
  46.6 4.2 %collective-permute-start.6 = (bf16[1040,256]{1,0:T(8,128)(2,1)S(1)}, bf16[1040,256]{1,0:T(8,128)(2,1)S(1)}, u32[]{:S(2)}, u32[]{:S(2)}) collective-permute-start(bf16[1040,256]{1,0:T(8,128)(2,1)S(1)} %get-tuple-element.61), channel_id=1, source_target_pairs={{0,1},{1,0},{2,3},{3,2},{4,5},{5,4},{6,7},{7,6},{8,9},{9,8},{10,11... | collective-permute-start | bytes 1597448 | tf_op jit(solution)/shard_map/ppermute | solution.py:283
  50.8 1.5 %collective-permute-done.6.near_ref = bf16[1040,256]{1,0:T(8,128)(2,1)S(1)} collective-permute-done((bf16[1040,256]{1,0:T(8,128)(2,1)S(1)}, bf16[1040,256]{1,0:T(8,128)(2,1)S(1)}, u32[]{:S(2)}, u32[]{:S(2)}) %collective-permute-start.6) | collective-permute-done | bytes 532512 | tf_op jit(solution)/shard_map/ppermute | solution.py:283
  52.4 0.1 pair.1
  52.5 0.0 copy-start.3
  52.5 0.8 copy-done.3
  53.4 10.8 %all-to-all-start = ((bf16[16,80,256]{2,1,0:T(8,128)(2,1)}), bf16[16,80,256]{2,1,0:T(8,128)(2,1)}, u32[]{:S(2)}, u32[]{:S(2)}) async-start(bf16[16,80,256]{2,1,0:T(8,128)(2,1)} %copy-done.3), calls=%async_computation | async-start | bytes 1310720 | tf_op jit(solution)/shard_map/all_to_all | solution.py:337
  64.2 0.1 collective-permute-start.4
  64.3 5.8 %collective-permute-start.5 = (bf16[1,512,256]{2,1,0:T(8,128)(2,1)}, bf16[1,512,256]{2,1,0:T(8,128)(2,1)S(1)}, u32[]{:S(2)}, u32[]{:S(2)}) collective-permute-start(bf16[1,512,256]{2,1,0:T(8,128)(2,1)} %copy-done.11), channel_id=1, source_target_pairs={{32,0},{64,32},{96,64},{128,96},{160,128},{192,160},{224,192},{0,2... | collective-permute-start | bytes 786440 | tf_op jit(solution)/shard_map/ppermute | solution.py:279
  70.0 7.3 %collective-permute-done.4.left_ref = bf16[1,512,256]{2,1,0:T(8,128)(2,1)S(1)} collective-permute-done((bf16[1,512,256]{2,1,0:T(8,128)(2,1)}, bf16[1,512,256]{2,1,0:T(8,128)(2,1)S(1)}, u32[]{:S(2)}, u32[]{:S(2)}) %collective-permute-start.4) | collective-permute-done | bytes 262176 | tf_op jit(solution)/shard_map/ppermute | solution.py:274
  77.3 1.5 %collective-permute-done.5.right_ref = bf16[1,512,256]{2,1,0:T(8,128)(2,1)S(1)} collective-permute-done((bf16[1,512,256]{2,1,0:T(8,128)(2,1)}, bf16[1,512,256]{2,1,0:T(8,128)(2,1)S(1)}, u32[]{:S(2)}, u32[]{:S(2)}) %collective-permute-start.5) | collective-permute-done | bytes 262176 | tf_op jit(solution)/shard_map/ppermute | solution.py:279
  78.8 0.0 copy-start.4
  78.8 0.7 copy-done.4
  79.5 3.2 %all-to-all-done.got_ref = bf16[16,80,256]{2,1,0:T(8,128)(2,1)} async-done(((bf16[16,80,256]{2,1,0:T(8,128)(2,1)}), bf16[16,80,256]{2,1,0:T(8,128)(2,1)}, u32[]{:S(2)}, u32[]{:S(2)}) %all-to-all-start) | async-done | bytes 655392 | tf_op jit(solution)/shard_map/all_to_all | solution.py:337
  82.7 0.0 copy-start.5
  82.7 0.9 copy-done.5
  83.6 0.0 copy-start.6
  83.7 0.0 copy-start.8
  83.7 1.2 rest.1
  84.9 15.0 %all_to_all.15.got_ref = bf16[8,80,256]{2,1,0:T(8,128)(2,1)S(1)} all-to-all(bf16[8,80,256]{2,1,0:T(8,128)(2,1)S(1)} %rest.1), channel_id=1, replica_groups=mesh['xh'=2,'y'=4,'z'=8,'xl'=2,'core'=2] {'xh','y'}, dimensions={0} | all-to-all | bytes 655360 | tf_op jit(solution)/shard_map/all_to_all | solution.py:341
  99.9 0.6 ring.1
  100.5 18.4 %all_to_all.16.mine_ref = bf16[16,64,256]{2,1,0:T(8,128)(2,1)S(1)} all-to-all(bf16[16,64,256]{2,1,0:T(8,128)(2,1)S(1)} %get-tuple-element.62), channel_id=1, replica_groups=mesh['xh'=2,'y'=4,'z'=8,'xl'=2,'core'=2] {'z','xl'}, dimensions={0} | all-to-all | bytes 1048576 | tf_op jit(solution)/shard_map/all_to_all | solution.py:345
  118.8 5.2 %collective-permute-start.7 = (bf16[16,64,256]{2,1,0:T(8,128)(2,1)S(1)}, bf16[16,64,256]{2,1,0:T(8,128)(2,1)S(1)}, u32[]{:S(2)}, u32[]{:S(2)}) collective-permute-start(bf16[16,64,256]{2,1,0:T(8,128)(2,1)S(1)} %all_to_all.16.mine_ref), channel_id=1, source_target_pairs={{0,1},{1,0},{2,3},{3,2},{4,5},{5,4},{6,7},{7,6},{8,9},{9,8},{10,11... | collective-permute-start | bytes 1572872 | tf_op jit(solution)/shard_map/ppermute | solution.py:283
  124.1 0.0 copy-done.6
  124.1 0.0 copy-done.8
  124.1 2.5 %lower_a.1 = bf16[6,512,256]{2,1,0:T(8,128)(2,1)} custom-call(bf16[6,512,256]{2,1,0:T(8,128)(2,1)S(1)} %get-tuple-element.49.delta_ref, bf16[1,512,256]{2,1,0:T(8,128)(2,1)S(1)} %collective-permute-done.4.left_ref, bf16[1,512,256]{2,1,0:T(8,128)(2,1)S(1)} %copy-done.6, bf16[6,512,256]{2,1,0:T(8,128)(2,1)S(1)} %get-tuple-element.52.up_ref, ...), custom_call_target="tpu_custom_call" | custom-call | flops 1207959552 | bytes 5636096 | tf_op jit(solution)/shard_map/lower_a/pallas_call | solution.py:260
  126.6 0.0 collective-permute-done.7.other_ref
  126.6 1.4 %tail.1 = (f32[3,256,256]{2,1,0:T(8,128)}, f32[256,256]{1,0:T(8,128)}, f32[3,256,256]{2,1,0:T(8,128)}, f32[256,256]{1,0:T(8,128)}) custom-call(bf16[16,64,256]{2,1,0:T(8,128)(2,1)S(1)} %all_to_all.16.mine_ref, bf16[16,64,256]{2,1,0:T(8,128)(2,1)S(1)} %collective-permute-done.7.other_ref), custom_call_target="tpu_custom_call" | custom-call | bytes 3145728 | tf_op jit(solution)/shard_map/tail/pallas_call | solution.py:260
  (1 shorter events, 0.0 us)
Async XLA Ops:
  0.6 7.8 %copy-start.15 = (f32[256]{0:T(256)S(1)}, f32[256]{0:T(256)}, u32[]{:S(2)}) copy-start(f32[256]{0:T(256)} %param.11) | copy-start | bytes 3076
  0.6 1.4 %copy-start.1 = (bf16[1,3072,256]{2,1,0:T(8,128)(2,1)S(1)}, bf16[1,3072,256]{2,1,0:T(8,128)(2,1)}, u32[]{:S(2)}) copy-start(bf16[1,3072,256]{2,1,0:T(8,128)(2,1)} %param.8) | copy-start | bytes 4718596
  2.1 6.3 %copy-start.9 = (bf16[3,256,256]{2,1,0:T(8,128)(2,1)S(1)}, bf16[3,256,256]{2,1,0:T(8,128)(2,1)}, u32[]{:S(2)}) copy-start(bf16[3,256,256]{2,1,0:T(8,128)(2,1)} %param.10) | copy-start | bytes 1179652
  2.1 6.3 %copy-start.10 = (bf16[3,256,256]{2,1,0:T(8,128)(2,1)S(1)}, bf16[3,256,256]{2,1,0:T(8,128)(2,1)}, u32[]{:S(2)}) copy-start(bf16[3,256,256]{2,1,0:T(8,128)(2,1)} %param.13) | copy-start | bytes 1179652
  2.1 6.3 %copy-start.13 = (bf16[256,256]{1,0:T(8,128)(2,1)S(1)}, bf16[256,256]{1,0:T(8,128)(2,1)}, u32[]{:S(2)}) copy-start(bf16[256,256]{1,0:T(8,128)(2,1)} %proj2_ref.1) | copy-start | bytes 393220
  2.1 6.3 %copy-start.14 = (bf16[256,256]{1,0:T(8,128)(2,1)S(1)}, bf16[256,256]{1,0:T(8,128)(2,1)}, u32[]{:S(2)}) copy-start(bf16[256,256]{1,0:T(8,128)(2,1)} %proj_ref.3) | copy-start | bytes 393220
  2.2 21.4 %collective-permute-start = (bf16[3,512,256]{2,1,0:T(8,128)(2,1)S(1)}, bf16[3,512,256]{2,1,0:T(8,128)(2,1)S(1)}, u32[]{:S(2)}, u32[]{:S(2)}) collective-permute-start(bf16[3,512,256]{2,1,0:T(8,128)(2,1)S(1)} %get-tuple-element.38), channel_id=1, source_target_pairs={{0,32},{32,64},{64,96},{96,128},{128,160},{160,192},{192,224},{224... | collective-permute-start | bytes 2359304 | tf_op jit(solution)/shard_map/ppermute | solution.py:274
  4.4 19.2 %collective-permute-start.1 = (bf16[3,512,256]{2,1,0:T(8,128)(2,1)S(1)}, bf16[3,512,256]{2,1,0:T(8,128)(2,1)S(1)}, u32[]{:S(2)}, u32[]{:S(2)}) collective-permute-start(bf16[3,512,256]{2,1,0:T(8,128)(2,1)S(1)} %get-tuple-element.39), channel_id=1, source_target_pairs={{32,0},{64,32},{96,64},{128,96},{160,128},{192,160},{224,192},{0,2... | collective-permute-start | bytes 2359304 | tf_op jit(solution)/shard_map/ppermute | solution.py:279
  8.4 15.2 %copy-start = (bf16[1,3072,256]{2,1,0:T(8,128)(2,1)S(1)}, bf16[1,3072,256]{2,1,0:T(8,128)(2,1)}, u32[]{:S(2)}) copy-start(bf16[1,3072,256]{2,1,0:T(8,128)(2,1)} %param.9) | copy-start | bytes 4718596
  8.4 15.2 %copy-start.16 = (f32[256]{0:T(256)S(1)}, f32[256]{0:T(256)}, u32[]{:S(2)}) copy-start(f32[256]{0:T(256)} %param.14) | copy-start | bytes 3076
  10.3 0.8 copy-start.7
  27.9 13.9 %collective-permute-start.2 = (bf16[2,512,256]{2,1,0:T(8,128)(2,1)S(1)}, bf16[2,512,256]{2,1,0:T(8,128)(2,1)S(1)}, u32[]{:S(2)}, u32[]{:S(2)}) collective-permute-start(bf16[2,512,256]{2,1,0:T(8,128)(2,1)S(1)} %get-tuple-element.43), channel_id=1, source_target_pairs={{0,32},{32,64},{64,96},{96,128},{128,160},{160,192},{192,224},{224... | collective-permute-start | bytes 1572872 | tf_op jit(solution)/shard_map/ppermute | solution.py:274
  28.2 13.6 %collective-permute-start.3 = (bf16[2,512,256]{2,1,0:T(8,128)(2,1)S(1)}, bf16[2,512,256]{2,1,0:T(8,128)(2,1)S(1)}, u32[]{:S(2)}, u32[]{:S(2)}) collective-permute-start(bf16[2,512,256]{2,1,0:T(8,128)(2,1)S(1)} %get-tuple-element.44), channel_id=1, source_target_pairs={{32,0},{64,32},{96,64},{128,96},{160,128},{192,160},{224,192},{0,2... | collective-permute-start | bytes 1572872 | tf_op jit(solution)/shard_map/ppermute | solution.py:279
  41.8 2.8 %copy-start.2 = (bf16[1,3072,256]{2,1,0:T(8,128)(2,1)S(1)}, bf16[1,3072,256]{2,1,0:T(8,128)(2,1)}, u32[]{:S(2)}) copy-start(bf16[1,3072,256]{2,1,0:T(8,128)(2,1)} %param.8) | copy-start | bytes 4718596
  43.8 0.7 copy-start.11
  43.8 0.8 copy-start.12
  46.6 5.8 %collective-permute-start.6 = (bf16[1040,256]{1,0:T(8,128)(2,1)S(1)}, bf16[1040,256]{1,0:T(8,128)(2,1)S(1)}, u32[]{:S(2)}, u32[]{:S(2)}) collective-permute-start(bf16[1040,256]{1,0:T(8,128)(2,1)S(1)} %get-tuple-element.61), channel_id=1, source_target_pairs={{0,1},{1,0},{2,3},{3,2},{4,5},{5,4},{6,7},{7,6},{8,9},{9,8},{10,11... | collective-permute-start | bytes 1597448 | tf_op jit(solution)/shard_map/ppermute | solution.py:283
  52.5 0.8 copy-start.3
  53.4 29.3 %all-to-all-start = ((bf16[16,80,256]{2,1,0:T(8,128)(2,1)}), bf16[16,80,256]{2,1,0:T(8,128)(2,1)}, u32[]{:S(2)}, u32[]{:S(2)}) async-start(bf16[16,80,256]{2,1,0:T(8,128)(2,1)} %copy-done.3), calls=%async_computation | async-start | bytes 1310720 | tf_op jit(solution)/shard_map/all_to_all | solution.py:337
  64.2 13.2 %collective-permute-start.4 = (bf16[1,512,256]{2,1,0:T(8,128)(2,1)}, bf16[1,512,256]{2,1,0:T(8,128)(2,1)S(1)}, u32[]{:S(2)}, u32[]{:S(2)}) collective-permute-start(bf16[1,512,256]{2,1,0:T(8,128)(2,1)} %copy-done.12), channel_id=1, source_target_pairs={{0,32},{32,64},{64,96},{96,128},{128,160},{160,192},{192,224},{224... | collective-permute-start | bytes 786440 | tf_op jit(solution)/shard_map/ppermute | solution.py:274
  64.3 14.5 %collective-permute-start.5 = (bf16[1,512,256]{2,1,0:T(8,128)(2,1)}, bf16[1,512,256]{2,1,0:T(8,128)(2,1)S(1)}, u32[]{:S(2)}, u32[]{:S(2)}) collective-permute-start(bf16[1,512,256]{2,1,0:T(8,128)(2,1)} %copy-done.11), channel_id=1, source_target_pairs={{32,0},{64,32},{96,64},{128,96},{160,128},{192,160},{224,192},{0,2... | collective-permute-start | bytes 786440 | tf_op jit(solution)/shard_map/ppermute | solution.py:279
  78.8 0.7 copy-start.4
  82.7 1.0 copy-start.5
  83.6 40.4 %copy-start.6 = (bf16[1,512,256]{2,1,0:T(8,128)(2,1)S(1)}, bf16[1,512,256]{2,1,0:T(8,128)(2,1)}, u32[]{:S(2)}) copy-start(bf16[1,512,256]{2,1,0:T(8,128)(2,1)} %copy-done.4) | copy-start | bytes 786436
  83.7 40.4 %copy-start.8 = (bf16[768,256]{1,0:T(8,128)(2,1)S(1)}, bf16[768,256]{1,0:T(8,128)(2,1)}, u32[]{:S(2)}) copy-start(bf16[768,256]{1,0:T(8,128)(2,1)} %copy-done.7) | copy-start | bytes 1179652
  118.8 7.8 %collective-permute-start.7 = (bf16[16,64,256]{2,1,0:T(8,128)(2,1)S(1)}, bf16[16,64,256]{2,1,0:T(8,128)(2,1)S(1)}, u32[]{:S(2)}, u32[]{:S(2)}) collective-permute-start(bf16[16,64,256]{2,1,0:T(8,128)(2,1)S(1)} %all_to_all.16.mine_ref), channel_id=1, source_target_pairs={{0,1},{1,0},{2,3},{3,2},{4,5},{5,4},{6,7},{7,6},{8,9},{9,8},{10,11... | collective-permute-start | bytes 1572872 | tf_op jit(solution)/shard_map/ppermute | solution.py:283

commit v3 on v2

v3 whole, which is shorter than its diff:
```python
import math

import jax
import jax.numpy as jnp
from jax import lax
from jax.experimental import pallas as pl
from jax.experimental.pallas import tpu as pltpu
from jax.sharding import Mesh, PartitionSpec as P

BLOCK = 512
RING = ("xh", "y")
PLANE = ("xh", "y", "xl")
COLUMN = "z"
BF, F32 = jnp.bfloat16, jnp.float32
C = 256


def dot(a, b):
    return jnp.dot(a, b, preferred_element_type=F32)


def t_dot(a, b):
    return lax.dot_general(a, b, (((0,), (0,)), ((), ())), preferred_element_type=F32)


def normal_cdf(v):
    return 0.5 * (1.0 + lax.erf(v * math.sqrt(0.5)))


def slope_of(v, cdf):
    return cdf + v * jnp.exp(-0.5 * v * v) * (1.0 / math.sqrt(2.0 * math.pi))


def taps(at, j, hop):
    return jnp.concatenate([at(j - hop), at(j), at(j + hop)], axis=1)


def cut_kernel(s_ref, left_ref, right_ref, sems):
    n = s_ref.shape[0]
    one = pltpu.make_async_copy(s_ref.at[pl.ds(0, 3)], left_ref, sems.at[0])
    two = pltpu.make_async_copy(s_ref.at[pl.ds(n - 3, 3)], right_ref, sems.at[1])
    one.start()
    two.start()
    one.wait()
    two.wait()


def tap(w_ref, k):
    return w_ref[k * C : (k + 1) * C]


def near_kernel(
    s_ref, up_ref, w_ref, bias_ref, proj_ref, w2_ref, bias2_ref, proj2_ref,
    act_ref, slope_ref, mid_ref, pre_ref, pre2_ref, back_ref, w_t_ref, w2_t_ref, proj_t_ref,
):
    at = lambda j: s_ref[j]

    def product(j):
        return dot(taps(at, j, 1), w_ref[...]) + bias_ref[...]

    pre = product(1)
    for j in range(1, 5):
        after = product(j + 1) if j < 4 else None
        cdf = normal_cdf(pre)
        act = (pre * cdf).astype(BF)
        act_ref[j - 1] = act
        slope_ref[j - 1] = slope_of(pre, cdf).astype(BF)
        mid_ref[j - 1] = (s_ref[j].astype(F32) + dot(act, proj_ref[...])).astype(BF)
        pre = after
    pre_ref[0] = dot(s_ref[0], tap(w_ref, 2)) + bias_ref[...]
    pre_ref[1] = dot(s_ref[0], tap(w_ref, 1)) + dot(s_ref[1], tap(w_ref, 2)) + bias_ref[...]
    pre_ref[2] = dot(s_ref[4], tap(w_ref, 0)) + dot(s_ref[5], tap(w_ref, 1)) + bias_ref[...]
    pre_ref[3] = dot(s_ref[5], tap(w_ref, 0)) + bias_ref[...]
    for j in range(6):
        total = bias2_ref[...]
        for k in range(3):
            if 1 <= j + 2 * (k - 1) <= 4:
                total = total + dot(mid_ref[j + 2 * (k - 1) - 1], tap(w2_ref, k))
        pre2_ref[j] = total
    for k in range(3):
        to = slice((2 - k) * C, (3 - k) * C)
        w_t_ref[to] = tap(w_ref, k).T
        w2_t_ref[to] = tap(w2_ref, k).T
    proj_t_ref[...] = proj_ref[...].T
    proj2_t = proj2_ref[...].T
    for j in range(6):
        back_ref[j] = dot(up_ref[j], proj2_t)


def far_kernel(
    s_ref, left_ref, right_ref, near_ref, pre_ref, pre2_ref, back_ref, w_ref, bias_ref, proj_ref, w2_ref,
    act_ref, slope_ref, mid_ref, act2_ref, delta_ref, to_left_ref, to_right_ref,
):
    def at(j):
        return left_ref[j + 3] if j < 0 else right_ref[j - 6] if j > 5 else s_ref[j]

    def mid_at(j):
        return mid_ref[j + 2] if j < 1 else mid_ref[j - 2]

    def pair(one, two):
        return jnp.concatenate([one, two], axis=1)

    def product(j):
        if j == 0:
            return pre_ref[1] + dot(at(-1), tap(w_ref, 0))
        if j == 5:
            return pre_ref[2] + dot(at(6), tap(w_ref, 2))
        if j == -1:
            return pre_ref[0] + dot(pair(at(-2), at(-1)), w_ref[: 2 * C])
        if j == 6:
            return pre_ref[3] + dot(pair(at(6), at(7)), w_ref[C:])
        return dot(taps(at, j, 1), w_ref[...]) + bias_ref[...]

    def product2(j):
        if j == 0:
            return pre2_ref[0] + dot(pair(mid_at(-2), mid_at(0)), w2_ref[: 2 * C])
        if j == 5:
            return pre2_ref[5] + dot(pair(mid_at(5), mid_at(7)), w2_ref[C:])
        if j < 3:
            return pre2_ref[j] + dot(mid_at(j - 2), tap(w2_ref, 0))
        return pre2_ref[j] + dot(mid_at(j + 2), tap(w2_ref, 2))

    order = (0, 5, -2, 7, -1, 6)
    order2 = (2, 3, 0, 5, 1, 4)
    pre = product(order[0])
    for i, j in enumerate(order):
        after = product(order[i + 1]) if i < 5 else product2(order2[0])
        cdf = normal_cdf(pre)
        act = (pre * cdf).astype(BF)
        if j in (0, 5):
            act_ref[j // 5] = act
            slope_ref[j // 5] = slope_of(pre, cdf).astype(BF)
        mid = (at(j).astype(F32) + dot(act, proj_ref[...])).astype(BF)
        mid_ref[j + 2 if j < 1 else j - 2] = mid
        pre = after
    for i, j in enumerate(order2):
        after = product2(order2[i + 1]) if i < 5 else None
        cdf = normal_cdf(pre)
        act2_ref[j] = (pre * cdf).astype(BF)
        delta = (back_ref[j] * slope_of(pre, cdf)).astype(BF)
        delta_ref[j] = delta
        if j < 2:
            to_left_ref[j] = delta
        if j > 3:
            to_right_ref[j - 4] = delta
        pre = after


def add_grads(sum_ref, first, cells, delta, act, up):
    conv = t_dot(cells, delta)
    proj = t_dot(act, up)
    if first:
        sum_ref[: 3 * C] = conv
        sum_ref[3 * C :] = proj
    else:
        sum_ref[: 3 * C] += conv
        sum_ref[3 * C :] += proj
    return jnp.sum(delta.astype(F32), axis=0, keepdims=True)


def put_halves(sum_ref, bias, row, away_ref, mine_ref):
    core = lax.axis_index("core")
    half = 2 * C
    mine_ref[:half] = sum_ref[pl.ds(pl.multiple_of(core * half, half), half)].astype(BF)
    away_ref[:half] = sum_ref[pl.ds(pl.multiple_of((1 - core) * half, half), half)].astype(BF)
    at = lax.broadcasted_iota(jnp.int32, (16, C), 0)
    tail = jnp.where(at == row, jnp.broadcast_to(bias, (16, C)), 0.0).astype(BF)
    mine_ref[half:] = tail
    away_ref[half:] = tail


def inner_kernel(
    near_ref, far_ref, act2_ref, up_ref, delta_ref, w_t_ref, proj_t_ref, slope_ref, s_ref, act_ref,
    away_ref, mine_ref, below_ref, grad_ref, out_ref, sum_ref, bias_ref, total_ref,
):
    def mid_at(j):
        return far_ref[j + 2] if j < 1 else far_ref[j - 2] if j > 4 else near_ref[j - 1]

    at = lambda j: s_ref[j]
    bias = jnp.zeros((1, C), F32)
    for j in range(6):
        bias += add_grads(total_ref, j == 0, taps(mid_at, j, 2), delta_ref[j], act2_ref[j], up_ref[j])
    put_halves(total_ref, bias, 0, away_ref, mine_ref)
    for i, j in enumerate((0, 1, 4, 5)):
        low = slice(C, 3 * C) if j < 2 else slice(0, 2 * C)
        two = (delta_ref[j], delta_ref[j + 2]) if j < 2 else (delta_ref[j - 2], delta_ref[j])
        below_ref[i] = up_ref[j].astype(F32) + dot(jnp.concatenate(two, axis=1), w_t_ref[low])
    bias = jnp.zeros((1, C), F32)
    for j in (2, 3):
        three = jnp.concatenate([delta_ref[j - 2], delta_ref[j], delta_ref[j + 2]], axis=1)
        below = (up_ref[j].astype(F32) + dot(three, w_t_ref[...])).astype(BF)
        grad_ref[j - 2] = below
        delta = (dot(below, proj_t_ref[...]) * slope_ref[j - 1].astype(F32)).astype(BF)
        out_ref[j - 2] = delta
        bias += add_grads(sum_ref, j == 2, taps(at, j, 1), delta, act_ref[j - 1], below)
    bias_ref[...] = bias


def edge_kernel(
    below_ref, left_ref, right_ref, w_t_ref, proj_t_ref, slope_ref, slope_far_ref, s_ref, s_left_ref, s_right_ref,
    act_ref, act_far_ref, part_ref, part_bias_ref,
    grad_ref, out_ref, to_left_ref, to_right_ref, away_ref, mine_ref, sum_ref,
):
    def at(j):
        return s_left_ref[2] if j < 0 else s_right_ref[0] if j > 5 else s_ref[j]

    def product(i):
        far = dot(left_ref[i], tap(w_t_ref, 0)) if i < 2 else dot(right_ref[i - 2], tap(w_t_ref, 2))
        return (below_ref[i] + far).astype(BF)

    blocks = (0, 1, 4, 5)
    order = (0, 3, 1, 2)
    bias = part_bias_ref[...]
    sum_ref[...] = part_ref[...]
    below = product(order[0])
    held = None
    for n, i in enumerate(order):
        j = blocks[i]
        after = product(order[n + 1]) if n < 3 else None
        grad_ref[i] = below
        slope, act = (slope_far_ref[j // 5], act_far_ref[j // 5]) if j in (0, 5) else (slope_ref[j - 1], act_ref[j - 1])
        delta = (dot(below, proj_t_ref[...]) * slope.astype(F32)).astype(BF)
        out_ref[i] = delta
        if j == 0:
            to_left_ref[0] = delta
        if j == 5:
            to_right_ref[0] = delta
        if held is not None:
            bias += add_grads(sum_ref, False, *held)
        held = (taps(at, j, 1), delta, act, below)
        below = after
    bias += add_grads(sum_ref, False, *held)
    put_halves(sum_ref, bias, 1, away_ref, mine_ref)


def pair_kernel(mine_b_ref, near_b_ref, mine_a_ref, near_a_ref, out_ref):
    n, rows, _ = out_ref.shape
    chunk = (rows - 16) // 2

    def both(mine, near, part):
        return mine[part].astype(F32) + near[part].astype(F32)

    last = slice(n * chunk, n * chunk + 16)
    tail = (both(mine_b_ref, near_b_ref, last) + both(mine_a_ref, near_a_ref, last)).astype(BF)
    for i in range(n):
        part = slice(i * chunk, (i + 1) * chunk)
        out_ref[i, :chunk] = both(mine_b_ref, near_b_ref, part).astype(BF)
        out_ref[i, chunk : 2 * chunk] = both(mine_a_ref, near_a_ref, part).astype(BF)
        out_ref[i, 2 * chunk :] = tail


def rest_kernel(got_ref, out_ref):
    total = got_ref[0].astype(F32)
    for i in range(1, got_ref.shape[0]):
        total += got_ref[i].astype(F32)
    total = total.astype(BF)
    for i in range(out_ref.shape[0]):
        out_ref[i] = total


def token_kernel(left_ref, right_ref, out_ref):
    out_ref[...] = jnp.zeros(out_ref.shape, F32)


def ring_kernel(got_ref, token_ref, out_ref, bias_b_ref, bias_a_ref):
    total = got_ref[0].astype(F32) + token_ref[0:1, 0:1]
    for i in range(1, got_ref.shape[0]):
        total += got_ref[i].astype(F32)
    chunk = out_ref.shape[1]
    own = total[:chunk].astype(BF)
    for i in range(out_ref.shape[0]):
        out_ref[i] = own
    bias_b_ref[...] = total[chunk : chunk + 1]
    bias_a_ref[...] = total[chunk + 1 : chunk + 2]


def tail_kernel(mine_ref, other_ref, conv_b_ref, proj_b_ref, conv_a_ref, proj_a_ref):
    core = lax.axis_index("core")
    n, rows, _ = mine_ref.shape
    chunk = rows // 2

    def put(low, high):
        for i in range(n // 2):
            to = slice(i * chunk, (i + 1) * chunk)
            for part, conv, proj in ((0, conv_b_ref, proj_b_ref), (1, conv_a_ref, proj_a_ref)):
                of = slice(part * chunk, (part + 1) * chunk)
                conv[0, to] = low[i, of].astype(F32)
                conv[1, to] = low[i + n // 2, of].astype(F32)
                conv[2, to] = high[i, of].astype(F32)
                proj[to] = high[i + n // 2, of].astype(F32)

    @pl.when(core == 0)
    def _():
        put(mine_ref, other_ref)

    @pl.when(core != 0)
    def _():
        put(other_ref, mine_ref)


def lower_a_kernel(inner_ref, edge_ref, in_up_ref, edge_up_ref, w_ref, left_ref, right_ref, out_ref, ends, sems):
    one = pltpu.make_async_copy(left_ref, ends.at[0], sems.at[0])
    two = pltpu.make_async_copy(right_ref, ends.at[1], sems.at[1])
    one.start()
    two.start()

    def at(j):
        if j < 0 or j > 5:
            return ends[0 if j < 0 else 1, 0]
        return inner_ref[j - 2] if j in (2, 3) else edge_ref[j if j < 2 else j - 2]

    for j in (1, 2, 3, 4, 0, 5):
        if j == 0:
            one.wait()
            two.wait()
        up = in_up_ref[j - 2] if j in (2, 3) else edge_up_ref[j if j < 2 else j - 2]
        out_ref[j] = (up.astype(F32) + dot(taps(at, j, 1), w_ref[...])).astype(BF)


def call(kernel, outs, args, flops=0, scratch=(), far=0):
    vmem = pl.BlockSpec(memory_space=pltpu.VMEM)
    moved = sum(a.size * a.dtype.itemsize for a in args) + sum(
        math.prod(s) * jnp.dtype(t).itemsize for s, t in outs
    )
    return pl.pallas_call(
        kernel,
        out_shape=[jax.ShapeDtypeStruct(s, t) for s, t in outs],
        in_specs=[vmem] * (len(args) - far) + [pl.BlockSpec(memory_space=pltpu.HBM)] * far,
        out_specs=[vmem] * len(outs),
        scratch_shapes=list(scratch),
        compiler_params=pltpu.CompilerParams(vmem_limit_bytes=32 * 2**20),
        cost_estimate=pl.CostEstimate(flops=flops, bytes_accessed=moved, transcendentals=0),
        name=kernel.__name__[: -len("_kernel")],
    )(*args)


def from_left(cells):
    n = lax.axis_size(RING)
    return lax.ppermute(cells, RING, [(i, (i + 1) % n) for i in range(n)])


def from_right(cells):
    n = lax.axis_size(RING)
    return lax.ppermute(cells, RING, [((i + 1) % n, i) for i in range(n)])


def across(cells):
    return lax.ppermute(cells, "core", [(0, 1), (1, 0)])


def on_device(signals, cotangent, kernel_a, bias_a, proj_a, kernel_b, bias_b, proj_b):
    batch, length, channels = signals.shape
    unit = 2 * BLOCK * C * C
    cells = signals.reshape(-1, BLOCK, C)
    up = cotangent.reshape(-1, BLOCK, C)
    rest, ring = lax.axis_size(PLANE), lax.axis_size(COLUMN)
    wa, wb = kernel_a.reshape(3 * C, C), kernel_b.reshape(3 * C, C)
    ba, bb = bias_a.reshape(1, C), bias_b.reshape(1, C)

    def like(n, t=BF):
        return ((n, BLOCK, C), t)

    to_left, to_right = call(
        cut_kernel, [like(3)] * 2, [cells], scratch=[pltpu.SemaphoreType.DMA((2,))], far=1
    )
    s_left, s_right = from_left(to_right), from_right(to_left)
    act_near, slope_near, mid_near, pre_a, pre_b, back, wa_t, wb_t, pa_t = call(
        near_kernel,
        [like(4)] * 3 + [like(4, F32), like(6, F32), like(6, F32)] + [((3 * C, C), BF)] * 2 + [((C, C), BF)],
        [cells, up, wa, ba, proj_a, wb, bb, proj_b],
        38 * unit,
    )
    act_far, slope_far, mid_far, act_b, delta_b, to_left, to_right = call(
        far_kernel,
        [like(2), like(2), like(6), like(6), like(6), like(2), like(2)],
        [cells, s_left, s_right, mid_near, pre_a, pre_b, back, wa, ba, proj_a, wb],
        26 * unit,
    )
    d_left, d_right = from_left(to_right), from_right(to_left)
    half = ((2 * C + 16, C), BF)
    away_b, mine_b, below, grad_in, delta_in, part, part_bias = call(
        inner_kernel,
        [half, half, like(4, F32), like(2), like(2), ((4 * C, C), F32), ((1, C), F32)],
        [mid_near, mid_far, act_b, up, delta_b, wb_t, pa_t, slope_near, cells, act_near],
        48 * unit,
        [pltpu.VMEM((4 * C, C), F32)],
    )
    near_b = across(away_b)
    grad_out, delta_out, to_left, to_right, away_a, mine_a = call(
        edge_kernel,
        [like(4), like(4), like(1), like(1), half, half],
        [below, d_left, d_right, wb_t, pa_t, slope_near, slope_far, cells, s_left, s_right]
        + [act_near, act_far, part, part_bias],
        24 * unit,
        [pltpu.VMEM((4 * C, C), F32)],
    )
    e_left, e_right = from_left(to_right), from_right(to_left)
    chunk = 2 * C // rest
    (sent,) = call(
        pair_kernel,
        [((rest, 2 * chunk + 16, C), BF)],
        [mine_b, near_b, mine_a, across(away_a)],
    )
    got = lax.all_to_all(sent, PLANE, 0, 0)
    (sent,) = call(rest_kernel, [((ring, 2 * chunk + 16, C), BF)], [got])
    got = lax.all_to_all(sent, COLUMN, 0, 0)
    (token,) = call(token_kernel, [((8, 128), F32)], [e_left, e_right], far=2)
    sent, sum_bias_b, sum_bias_a = call(
        ring_kernel, [((rest, 2 * chunk, C), BF), ((1, C), F32), ((1, C), F32)], [got, token]
    )
    mine = lax.all_to_all(sent, PLANE, 0, 0)
    conv_b, grad_proj_b, conv_a, grad_proj_a = call(
        tail_kernel, [((3, C, C), F32), ((C, C), F32)] * 2, [mine, across(mine)]
    )
    (out,) = call(
        lower_a_kernel,
        [like(6)],
        [delta_in, delta_out, grad_in, grad_out, wa_t, e_left, e_right],
        18 * unit,
        [pltpu.VMEM((2, 1, BLOCK, C), BF), pltpu.SemaphoreType.DMA((2,))],
        far=2,
    )
    return (
        out.reshape(batch, length, channels),
        conv_a,
        sum_bias_a.reshape(C),
        grad_proj_a,
        conv_b,
        sum_bias_b.reshape(C),
        grad_proj_b,
    )


def solution(mesh):
    split = Mesh(mesh.devices.reshape(2, 4, 8, 2, 2), ("xh", "y", "z", "xl", "core"))
    data = P(("z", "xl", "core"), RING, None)
    return jax.shard_map(
        on_device,
        mesh=split,
        in_specs=(data, data, P(), P(), P(), P(), P(), P()),
        out_specs=(data, P(), P(), P(), P(), P(), P()),
        check_vma=False,
    )
```

time: 128 us -> 113 us (0.88)
  waiting for transfers between devices: 32.8 us -> 17.2 us
    ppermute x3, waiting for transfers between devices: 26.6 us -> 14.2 us  [from_left(): return lax.ppermute(cells, RING, [(i, (i + 1) % n) for i in range(n)])]
    ppermute x2 -> x3, starting transfers between devices: 9.45 us -> 12.7 us  [across(): return lax.ppermute(cells, 'core', [(0, 1), (1, 0)])]
    all_to_all x1, starting transfers between devices: 10.8 us -> 8.17 us  [on_device(): got = lax.all_to_all(sent, COLUMN, 0, 0)]
    ppermute x3, waiting for transfers between devices: 1.48 us -> 0.01 us  [from_right(): return lax.ppermute(cells, RING, [((i + 1) % n, i) for i in range(n)])]
    all_to_all x1, waiting for transfers between devices: 3.18 us -> 1.83 us  [on_device(): got = lax.all_to_all(sent, COLUMN, 0, 0)]
    unnamed x34 -> x28, local copies, waits for them, and re-layouts: 5.45 us -> 4.38 us
  transfers between devices with their start and end apart: 9 -> 10, of which waited for: 6 -> 4; matrix products, arithmetic and copies ran while one was open for 0% -> 0% of each run, Pallas kernels for 5% -> 11%
where the time goes in v3:
time: 113 us
  starting transfers between devices  37.4 us (33%)
  blocking collectives  33.5 us (30%)
  Pallas kernels  19.3 us (17%)
  waiting for transfers between devices  17.2 us (15%)
  local copies, waits for them, and re-layouts  4.38 us (4%)
    all_to_all x1, blocking collectives, on_device(): got = lax.all_to_all(sent, PLANE, 0, 0)  20.6 us
    pallas_call x11, Pallas kernels, call(): pl.pallas_call(kernel, out_shape=[jax.ShapeDtypeStruct(s, t) for s, t in...  19.3 us
    ppermute x3, waiting for transfers between devices, from_left(): return lax.ppermute(cells, RING, [(i, (i + 1) % n) for i in range(n)])  14.2 us
    ppermute x3, starting transfers between devices, from_right(): return lax.ppermute(cells, RING, [((i + 1) % n, i) for i in range(n)])  14.1 us
    all_to_all x1, blocking collectives, on_device(): mine = lax.all_to_all(sent, PLANE, 0, 0)  12.9 us
    ppermute x3, starting transfers between devices, across(): return lax.ppermute(cells, 'core', [(0, 1), (1, 0)])  12.7 us
    all_to_all x1, starting transfers between devices, on_device(): got = lax.all_to_all(sent, COLUMN, 0, 0)  8.17 us
    unnamed x28, local copies, waits for them, and re-layouts  4.38 us
  transfers between devices with their start and end apart: 10, of which 4 were waited for; matrix products, arithmetic and copies ran while one was open for 0% of the time, Pallas kernels for 11%

profile of v3, /device:TPU:1, one launch (start us, length us, event | category | flops | bytes accessed | tf_op | source)
XLA Modules:
  0.0 112.6 jit_solution(331558601858360456)
XLA Ops:
  0.6 0.0 copy-start.8
  0.6 0.0 copy-start
  0.7 1.4 %copy-done = bf16[1,3072,256]{2,1,0:T(8,128)(2,1)S(1)} copy-done((bf16[1,3072,256]{2,1,0:T(8,128)(2,1)S(1)}, bf16[1,3072,256]{2,1,0:T(8,128)(2,1)}, u32[]{:S(2)}) %copy-start) | copy-done | bytes 1572888
  2.1 0.0 copy-start.3
  2.1 0.0 copy-start.4
  2.1 0.0 copy-start.7
  2.1 0.0 copy-start.12
  2.1 0.0 copy-start.13
  2.1 0.1 cut.1
  2.2 2.2 %collective-permute-start = (bf16[3,512,256]{2,1,0:T(8,128)(2,1)S(1)}, bf16[3,512,256]{2,1,0:T(8,128)(2,1)S(1)}, u32[]{:S(2)}, u32[]{:S(2)}) collective-permute-start(bf16[3,512,256]{2,1,0:T(8,128)(2,1)S(1)} %get-tuple-element.46), channel_id=1, source_target_pairs={{0,32},{32,64},{64,96},{96,128},{128,160},{160,192},{192,224},{224... | collective-permute-start | bytes 2359304 | tf_op jit(solution)/shard_map/ppermute | solution.py:339
  4.4 4.0 %collective-permute-start.1 = (bf16[3,512,256]{2,1,0:T(8,128)(2,1)S(1)}, bf16[3,512,256]{2,1,0:T(8,128)(2,1)S(1)}, u32[]{:S(2)}, u32[]{:S(2)}) collective-permute-start(bf16[3,512,256]{2,1,0:T(8,128)(2,1)S(1)} %get-tuple-element.47), channel_id=1, source_target_pairs={{32,0},{64,32},{96,64},{128,96},{160,128},{192,160},{224,192},{0,2... | collective-permute-start | bytes 2359304 | tf_op jit(solution)/shard_map/ppermute | solution.py:344
  8.4 0.0 copy-done.8
  8.4 0.0 copy-done.3
  8.4 0.0 copy-done.4
  8.4 0.0 copy-done.7
  8.4 0.0 copy-done.12
  8.4 0.0 copy-done.13
  8.4 0.0 copy-start.9
  8.5 1.4 %copy-done.9 = bf16[1,3072,256]{2,1,0:T(8,128)(2,1)S(1)} copy-done((bf16[1,3072,256]{2,1,0:T(8,128)(2,1)S(1)}, bf16[1,3072,256]{2,1,0:T(8,128)(2,1)}, u32[]{:S(2)}) %copy-start.9) | copy-done | bytes 1572888
  9.9 3.3 %near.1 = (bf16[4,512,256]{2,1,0:T(8,128)(2,1)S(1)}, bf16[4,512,256]{2,1,0:T(8,128)(2,1)S(1)}, bf16[4,512,256]{2,1,0:T(8,128)(2,1)S(1)}, f32[4,512,256]{2,1,0:T(...) custom-call(bf16[6,512,256]{2,1,0:T(8,128)(2,1)S(1)} %bitcast.10, ...), custom_call_target="tpu_custom_call" | custom-call | flops 2550136832 | bytes 16648192 | tf_op jit(solution)/shard_map/near/pallas_call | solution.py:325
  13.2 0.0 copy-start.5
  13.2 0.7 copy-done.5
  13.9 9.7 %collective-permute-done.left_ref.s_left_ref = bf16[3,512,256]{2,1,0:T(8,128)(2,1)S(1)} collective-permute-done((bf16[3,512,256]{2,1,0:T(8,128)(2,1)S(1)}, bf16[3,512,256]{2,1,0:T(8,128)(2,1)S(1)}, u32[]{:S(2)}, u32[]{:S(2)}) %collective-permute-start) | collective-permute-done | bytes 786464 | tf_op jit(solution)/shard_map/ppermute | solution.py:339
  23.6 0.0 collective-permute-done.1.right_ref.s_right_ref
  23.6 3.4 %far.1 = (bf16[2,512,256]{2,1,0:T(8,128)(2,1)S(1)}, bf16[2,512,256]{2,1,0:T(8,128)(2,1)S(1)}, bf16[6,512,256]{2,1,0:T(8,128)(2,1)S(1)}, bf16[6,512,256]{2,1,0:T(...) custom-call(bf16[6,512,256]{2,1,0:T(8,128)(2,1)S(1)} %bitcast.11, ...), custom_call_target="tpu_custom_call" | custom-call | flops 1744830464 | bytes 20317184 | tf_op jit(solution)/shard_map/far/pallas_call | solution.py:325
  27.1 0.3 collective-permute-start.2
  27.3 5.0 %collective-permute-start.3 = (bf16[2,512,256]{2,1,0:T(8,128)(2,1)S(1)}, bf16[2,512,256]{2,1,0:T(8,128)(2,1)S(1)}, u32[]{:S(2)}, u32[]{:S(2)}) collective-permute-start(bf16[2,512,256]{2,1,0:T(8,128)(2,1)S(1)} %get-tuple-element.61), channel_id=1, source_target_pairs={{32,0},{64,32},{96,64},{128,96},{160,128},{192,160},{224,192},{0,2... | collective-permute-start | bytes 1572872 | tf_op jit(solution)/shard_map/ppermute | solution.py:344
  32.4 4.2 %inner.1 = (bf16[528,256]{1,0:T(8,128)(2,1)S(1)}, bf16[528,256]{1,0:T(8,128)(2,1)S(1)}, f32[4,512,256]{2,1,0:T(8,128)S(1)}, bf16[2,512,256]{2,1,0:T(8,128)(2,1)S...) custom-call(bf16[4,512,256]{2,1,0:T(8,128)(2,1)S(1)} %get-tuple-element.45.near_ref, ...), custom_call_target="tpu_custom_call" | custom-call | flops 3221225472 | bytes 16270336 | tf_op jit(solution)/shard_map/inner/pallas_call | solution.py:325
  36.6 0.0 copy-start.1
  36.6 0.8 copy-done.1
  37.4 3.7 %collective-permute-start.6 = (bf16[528,256]{1,0:T(8,128)(2,1)S(1)}, bf16[528,256]{1,0:T(8,128)(2,1)S(1)}, u32[]{:S(2)}, u32[]{:S(2)}) collective-permute-start(bf16[528,256]{1,0:T(8,128)(2,1)S(1)} %get-tuple-element.73), channel_id=1, source_target_pairs={{0,1},{1,0},{2,3},{3,2},{4,5},{5,4},{6,7},{7,6},{8,9},{9,8},{10,11... | collective-permute-start | bytes 811016 | tf_op jit(solution)/shard_map/ppermute | solution.py:348
  41.1 0.0 collective-permute-done.2.left_ref
  41.1 0.0 collective-permute-done.3.right_ref
  41.1 2.3 %edge.1 = (bf16[4,512,256]{2,1,0:T(8,128)(2,1)S(1)}, bf16[4,512,256]{2,1,0:T(8,128)(2,1)S(1)}, bf16[1,512,256]{2,1,0:T(8,128)(2,1)S(1)}, bf16[1,512,256]{2,1,0:T...) custom-call(f32[4,512,256]{2,1,0:T(8,128)S(1)} %get-tuple-element.59.below_ref, ...), custom_call_target="tpu_custom_call" | custom-call | flops 1610612736 | bytes 14173184 | tf_op jit(solution)/shard_map/edge/pallas_call | solution.py:325
  43.4 0.0 copy-start.10
  43.4 0.0 copy-start.11
  43.5 4.1 %collective-permute-start.7 = (bf16[528,256]{1,0:T(8,128)(2,1)S(1)}, bf16[528,256]{1,0:T(8,128)(2,1)S(1)}, u32[]{:S(2)}, u32[]{:S(2)}) collective-permute-start(bf16[528,256]{1,0:T(8,128)(2,1)S(1)} %get-tuple-element.75), channel_id=1, source_target_pairs={{0,1},{1,0},{2,3},{3,2},{4,5},{5,4},{6,7},{7,6},{8,9},{9,8},{10,11... | collective-permute-start | bytes 811016 | tf_op jit(solution)/shard_map/ppermute | solution.py:348
  47.5 0.0 collective-permute-done.6.near_b_ref
  47.5 1.2 %collective-permute-done.7.near_a_ref = bf16[528,256]{1,0:T(8,128)(2,1)S(1)} collective-permute-done((bf16[528,256]{1,0:T(8,128)(2,1)S(1)}, bf16[528,256]{1,0:T(8,128)(2,1)S(1)}, u32[]{:S(2)}, u32[]{:S(2)}) %collective-permute-start.7) | collective-permute-done | bytes 270368 | tf_op jit(solution)/shard_map/ppermute | solution.py:348
  48.7 0.1 pair.1
  48.8 20.6 %all_to_all.15.got_ref = bf16[16,80,256]{2,1,0:T(8,128)(2,1)S(1)} all-to-all(bf16[16,80,256]{2,1,0:T(8,128)(2,1)S(1)} %pair.1), channel_id=1, replica_groups=mesh['xh'=2,'y'=4,'z'=8,'xl'=2,'core'=2] {'xh','y','xl'}, dimensions={0} | all-to-all | bytes 1310720 | tf_op jit(solution)/shard_map/all_to_all | solution.py:404
  69.4 0.0 copy-done.10
  69.4 0.0 copy-done.11
  69.4 0.8 rest.1
  70.2 8.2 %all-to-all-start.1 = ((bf16[8,80,256]{2,1,0:T(8,128)(2,1)}), bf16[8,80,256]{2,1,0:T(8,128)(2,1)S(1)}, u32[]{:S(2)}, u32[]{:S(2)}) async-start(bf16[8,80,256]{2,1,0:T(8,128)(2,1)} %rest.1), calls=%async_computation.1 | async-start | bytes 655360 | tf_op jit(solution)/shard_map/all_to_all | solution.py:406
  78.4 0.0 collective-permute-start.4
  78.4 5.1 %collective-permute-start.5 = (bf16[1,512,256]{2,1,0:T(8,128)(2,1)}, bf16[1,512,256]{2,1,0:T(8,128)(2,1)S(1)}, u32[]{:S(2)}, u32[]{:S(2)}) collective-permute-start(bf16[1,512,256]{2,1,0:T(8,128)(2,1)} %copy-done.10), channel_id=1, source_target_pairs={{32,0},{64,32},{96,64},{128,96},{160,128},{192,160},{224,192},{0,2... | collective-permute-start | bytes 786440 | tf_op jit(solution)/shard_map/ppermute | solution.py:344
  83.5 4.5 %collective-permute-done.4.left_ref = bf16[1,512,256]{2,1,0:T(8,128)(2,1)S(1)} collective-permute-done((bf16[1,512,256]{2,1,0:T(8,128)(2,1)}, bf16[1,512,256]{2,1,0:T(8,128)(2,1)S(1)}, u32[]{:S(2)}, u32[]{:S(2)}) %collective-permute-start.4) | collective-permute-done | bytes 262176 | tf_op jit(solution)/shard_map/ppermute | solution.py:339
  88.0 0.0 collective-permute-done.5.right_ref
  88.0 1.8 %all-to-all-done.1.got_ref = bf16[8,80,256]{2,1,0:T(8,128)(2,1)S(1)} async-done(((bf16[8,80,256]{2,1,0:T(8,128)(2,1)}), bf16[8,80,256]{2,1,0:T(8,128)(2,1)S(1)}, u32[]{:S(2)}, u32[]{:S(2)}) %all-to-all-start.1) | async-done | bytes 327712 | tf_op jit(solution)/shard_map/all_to_all | solution.py:406
  89.8 0.0 copy-start.2
  89.8 0.0 copy-start.6
  89.8 0.7 ring.1
  90.5 12.9 %all_to_all.16.mine_ref = bf16[16,64,256]{2,1,0:T(8,128)(2,1)S(1)} all-to-all(bf16[16,64,256]{2,1,0:T(8,128)(2,1)S(1)} %get-tuple-element.76), channel_id=1, replica_groups=mesh['xh'=2,'y'=4,'z'=8,'xl'=2,'core'=2] {'xh','y','xl'}, dimensions={0} | all-to-all | bytes 1048576 | tf_op jit(solution)/shard_map/all_to_all | solution.py:411
  103.4 4.9 %collective-permute-start.8 = (bf16[16,64,256]{2,1,0:T(8,128)(2,1)S(1)}, bf16[16,64,256]{2,1,0:T(8,128)(2,1)S(1)}, u32[]{:S(2)}, u32[]{:S(2)}) collective-permute-start(bf16[16,64,256]{2,1,0:T(8,128)(2,1)S(1)} %all_to_all.16.mine_ref), channel_id=1, source_target_pairs={{0,1},{1,0},{2,3},{3,2},{4,5},{5,4},{6,7},{7,6},{8,9},{9,8},{10,11... | collective-permute-start | bytes 1572872 | tf_op jit(solution)/shard_map/ppermute | solution.py:348
  108.3 0.0 copy-done.2
  108.3 0.0 copy-done.6
  108.3 2.8 %lower_a.1 = bf16[6,512,256]{2,1,0:T(8,128)(2,1)} custom-call(bf16[2,512,256]{2,1,0:T(8,128)(2,1)S(1)} %copy-done.2, bf16[4,512,256]{2,1,0:T(8,128)(2,1)S(1)} %get-tuple-element.66.edge_ref, bf16[2,512,256]{2,1,0:T(8,128)(2,1)S(1)} %get-tuple-element.67.in_up_ref, bf16[4,512,256]{2,1,0:T(8,128)(2,1)S(1)} %get-tuple-element.68.edge_up_ref, ...), custom_call_target="tpu_custom_call" | custom-call | flops 1207959552 | bytes 5636096 | tf_op jit(solution)/shard_map/lower_a/pallas_call | solution.py:325
  111.1 0.0 collective-permute-done.8.other_ref
  111.1 1.5 %tail.1 = (f32[3,256,256]{2,1,0:T(8,128)}, f32[256,256]{1,0:T(8,128)}, f32[3,256,256]{2,1,0:T(8,128)}, f32[256,256]{1,0:T(8,128)}) custom-call(bf16[16,64,256]{2,1,0:T(8,128)(2,1)S(1)} %all_to_all.16.mine_ref, bf16[16,64,256]{2,1,0:T(8,128)(2,1)S(1)} %collective-permute-done.8.other_ref), custom_call_target="tpu_custom_call" | custom-call | bytes 3145728 | tf_op jit(solution)/shard_map/tail/pallas_call | solution.py:325
  (1 shorter events, 0.0 us)
Async XLA Ops:
  0.6 7.8 %copy-start.8 = (f32[256]{0:T(256)S(1)}, f32[256]{0:T(256)}, u32[]{:S(2)}) copy-start(f32[256]{0:T(256)} %param.11) | copy-start | bytes 3076
  0.6 1.4 %copy-start = (bf16[1,3072,256]{2,1,0:T(8,128)(2,1)S(1)}, bf16[1,3072,256]{2,1,0:T(8,128)(2,1)}, u32[]{:S(2)}) copy-start(bf16[1,3072,256]{2,1,0:T(8,128)(2,1)} %param.8) | copy-start | bytes 4718596
  2.1 6.4 %copy-start.3 = (bf16[3,256,256]{2,1,0:T(8,128)(2,1)S(1)}, bf16[3,256,256]{2,1,0:T(8,128)(2,1)}, u32[]{:S(2)}) copy-start(bf16[3,256,256]{2,1,0:T(8,128)(2,1)} %param.10) | copy-start | bytes 1179652
  2.1 6.4 %copy-start.4 = (bf16[3,256,256]{2,1,0:T(8,128)(2,1)S(1)}, bf16[3,256,256]{2,1,0:T(8,128)(2,1)}, u32[]{:S(2)}) copy-start(bf16[3,256,256]{2,1,0:T(8,128)(2,1)} %param.13) | copy-start | bytes 1179652
  2.1 6.4 %copy-start.7 = (bf16[256,256]{1,0:T(8,128)(2,1)S(1)}, bf16[256,256]{1,0:T(8,128)(2,1)}, u32[]{:S(2)}) copy-start(bf16[256,256]{1,0:T(8,128)(2,1)} %proj_ref.3) | copy-start | bytes 393220
  2.1 6.4 %copy-start.12 = (bf16[256,256]{1,0:T(8,128)(2,1)S(1)}, bf16[256,256]{1,0:T(8,128)(2,1)}, u32[]{:S(2)}) copy-start(bf16[256,256]{1,0:T(8,128)(2,1)} %proj2_ref.1) | copy-start | bytes 393220
  2.1 6.4 %copy-start.13 = (f32[256]{0:T(256)S(1)}, f32[256]{0:T(256)}, u32[]{:S(2)}) copy-start(f32[256]{0:T(256)} %param.14) | copy-start | bytes 3076
  2.2 21.4 %collective-permute-start = (bf16[3,512,256]{2,1,0:T(8,128)(2,1)S(1)}, bf16[3,512,256]{2,1,0:T(8,128)(2,1)S(1)}, u32[]{:S(2)}, u32[]{:S(2)}) collective-permute-start(bf16[3,512,256]{2,1,0:T(8,128)(2,1)S(1)} %get-tuple-element.46), channel_id=1, source_target_pairs={{0,32},{32,64},{64,96},{96,128},{128,160},{160,192},{192,224},{224... | collective-permute-start | bytes 2359304 | tf_op jit(solution)/shard_map/ppermute | solution.py:339
  4.4 19.2 %collective-permute-start.1 = (bf16[3,512,256]{2,1,0:T(8,128)(2,1)S(1)}, bf16[3,512,256]{2,1,0:T(8,128)(2,1)S(1)}, u32[]{:S(2)}, u32[]{:S(2)}) collective-permute-start(bf16[3,512,256]{2,1,0:T(8,128)(2,1)S(1)} %get-tuple-element.47), channel_id=1, source_target_pairs={{32,0},{64,32},{96,64},{128,96},{160,128},{192,160},{224,192},{0,2... | collective-permute-start | bytes 2359304 | tf_op jit(solution)/shard_map/ppermute | solution.py:344
  8.4 1.4 %copy-start.9 = (bf16[1,3072,256]{2,1,0:T(8,128)(2,1)S(1)}, bf16[1,3072,256]{2,1,0:T(8,128)(2,1)}, u32[]{:S(2)}) copy-start(bf16[1,3072,256]{2,1,0:T(8,128)(2,1)} %param.9) | copy-start | bytes 4718596
  13.2 0.7 copy-start.5
  27.1 14.0 %collective-permute-start.2 = (bf16[2,512,256]{2,1,0:T(8,128)(2,1)S(1)}, bf16[2,512,256]{2,1,0:T(8,128)(2,1)S(1)}, u32[]{:S(2)}, u32[]{:S(2)}) collective-permute-start(bf16[2,512,256]{2,1,0:T(8,128)(2,1)S(1)} %get-tuple-element.60), channel_id=1, source_target_pairs={{0,32},{32,64},{64,96},{96,128},{128,160},{160,192},{192,224},{224... | collective-permute-start | bytes 1572872 | tf_op jit(solution)/shard_map/ppermute | solution.py:339
  27.3 13.8 %collective-permute-start.3 = (bf16[2,512,256]{2,1,0:T(8,128)(2,1)S(1)}, bf16[2,512,256]{2,1,0:T(8,128)(2,1)S(1)}, u32[]{:S(2)}, u32[]{:S(2)}) collective-permute-start(bf16[2,512,256]{2,1,0:T(8,128)(2,1)S(1)} %get-tuple-element.61), channel_id=1, source_target_pairs={{32,0},{64,32},{96,64},{128,96},{160,128},{192,160},{224,192},{0,2... | collective-permute-start | bytes 1572872 | tf_op jit(solution)/shard_map/ppermute | solution.py:344
  36.6 0.8 copy-start.1
  37.4 10.1 %collective-permute-start.6 = (bf16[528,256]{1,0:T(8,128)(2,1)S(1)}, bf16[528,256]{1,0:T(8,128)(2,1)S(1)}, u32[]{:S(2)}, u32[]{:S(2)}) collective-permute-start(bf16[528,256]{1,0:T(8,128)(2,1)S(1)} %get-tuple-element.73), channel_id=1, source_target_pairs={{0,1},{1,0},{2,3},{3,2},{4,5},{5,4},{6,7},{7,6},{8,9},{9,8},{10,11... | collective-permute-start | bytes 811016 | tf_op jit(solution)/shard_map/ppermute | solution.py:348
  43.4 26.0 %copy-start.10 = (bf16[1,512,256]{2,1,0:T(8,128)(2,1)}, bf16[1,512,256]{2,1,0:T(8,128)(2,1)S(1)}, u32[]{:S(2)}) copy-start(bf16[1,512,256]{2,1,0:T(8,128)(2,1)S(1)} %get-tuple-element.71) | copy-start | bytes 786436
  43.4 26.0 %copy-start.11 = (bf16[1,512,256]{2,1,0:T(8,128)(2,1)}, bf16[1,512,256]{2,1,0:T(8,128)(2,1)S(1)}, u32[]{:S(2)}) copy-start(bf16[1,512,256]{2,1,0:T(8,128)(2,1)S(1)} %get-tuple-element.70) | copy-start | bytes 786436
  43.5 5.3 %collective-permute-start.7 = (bf16[528,256]{1,0:T(8,128)(2,1)S(1)}, bf16[528,256]{1,0:T(8,128)(2,1)S(1)}, u32[]{:S(2)}, u32[]{:S(2)}) collective-permute-start(bf16[528,256]{1,0:T(8,128)(2,1)S(1)} %get-tuple-element.75), channel_id=1, source_target_pairs={{0,1},{1,0},{2,3},{3,2},{4,5},{5,4},{6,7},{7,6},{8,9},{9,8},{10,11... | collective-permute-start | bytes 811016 | tf_op jit(solution)/shard_map/ppermute | solution.py:348
  70.2 19.6 %all-to-all-start.1 = ((bf16[8,80,256]{2,1,0:T(8,128)(2,1)}), bf16[8,80,256]{2,1,0:T(8,128)(2,1)S(1)}, u32[]{:S(2)}, u32[]{:S(2)}) async-start(bf16[8,80,256]{2,1,0:T(8,128)(2,1)} %rest.1), calls=%async_computation.1 | async-start | bytes 655360 | tf_op jit(solution)/shard_map/all_to_all | solution.py:406
  78.4 9.6 %collective-permute-start.4 = (bf16[1,512,256]{2,1,0:T(8,128)(2,1)}, bf16[1,512,256]{2,1,0:T(8,128)(2,1)S(1)}, u32[]{:S(2)}, u32[]{:S(2)}) collective-permute-start(bf16[1,512,256]{2,1,0:T(8,128)(2,1)} %copy-done.11), channel_id=1, source_target_pairs={{0,32},{32,64},{64,96},{96,128},{128,160},{160,192},{192,224},{224... | collective-permute-start | bytes 786440 | tf_op jit(solution)/shard_map/ppermute | solution.py:339
  78.4 9.6 %collective-permute-start.5 = (bf16[1,512,256]{2,1,0:T(8,128)(2,1)}, bf16[1,512,256]{2,1,0:T(8,128)(2,1)S(1)}, u32[]{:S(2)}, u32[]{:S(2)}) collective-permute-start(bf16[1,512,256]{2,1,0:T(8,128)(2,1)} %copy-done.10), channel_id=1, source_target_pairs={{32,0},{64,32},{96,64},{128,96},{160,128},{192,160},{224,192},{0,2... | collective-permute-start | bytes 786440 | tf_op jit(solution)/shard_map/ppermute | solution.py:344
  89.8 18.5 %copy-start.2 = (bf16[2,512,256]{2,1,0:T(8,128)(2,1)S(1)}, bf16[2,512,256]{2,1,0:T(8,128)(2,1)}, u32[]{:S(2)}) copy-start(bf16[2,512,256]{2,1,0:T(8,128)(2,1)} %copy-done.1) | copy-start | bytes 1572868
  89.8 18.5 %copy-start.6 = (bf16[768,256]{1,0:T(8,128)(2,1)S(1)}, bf16[768,256]{1,0:T(8,128)(2,1)}, u32[]{:S(2)}) copy-start(bf16[768,256]{1,0:T(8,128)(2,1)} %copy-done.5) | copy-start | bytes 1179652
  103.4 7.7 %collective-permute-start.8 = (bf16[16,64,256]{2,1,0:T(8,128)(2,1)S(1)}, bf16[16,64,256]{2,1,0:T(8,128)(2,1)S(1)}, u32[]{:S(2)}, u32[]{:S(2)}) collective-permute-start(bf16[16,64,256]{2,1,0:T(8,128)(2,1)S(1)} %all_to_all.16.mine_ref), channel_id=1, source_target_pairs={{0,1},{1,0},{2,3},{3,2},{4,5},{5,4},{6,7},{7,6},{8,9},{9,8},{10,11... | collective-permute-start | bytes 1572872 | tf_op jit(solution)/shard_map/ppermute | solution.py:348

commit v4 on v3

--- a/solution.py
+++ b/solution.py
@@ -28,17 +28,20 @@
 
 
 def slope_of(v, cdf):
-    return cdf + v * jnp.exp(-0.5 * v * v) * (1.0 / math.sqrt(2.0 * math.pi))
+    return cdf + v * jnp.exp2(v * v * (-0.5 * math.log2(math.e)) - 0.5 * math.log2(2.0 * math.pi))
 
 
 def taps(at, j, hop):
     return jnp.concatenate([at(j - hop), at(j), at(j + hop)], axis=1)
 
 
-def cut_kernel(s_ref, left_ref, right_ref, sems):
-    n = s_ref.shape[0]
-    one = pltpu.make_async_copy(s_ref.at[pl.ds(0, 3)], left_ref, sems.at[0])
-    two = pltpu.make_async_copy(s_ref.at[pl.ds(n - 3, 3)], right_ref, sems.at[1])
+def odd():
+    return lax.rem(lax.axis_index("y"), 2)
+
+
+def cut_kernel(s_ref, one_ref, two_ref, sems):
+    one = pltpu.make_async_copy(s_ref.at[pl.ds(3 * odd(), 3)], one_ref, sems.at[0])
+    two = pltpu.make_async_copy(s_ref.at[pl.ds(3 - 3 * odd(), 3)], two_ref, sems.at[1])
     one.start()
     two.start()
     one.wait()
@@ -88,14 +91,22 @@
 
 
 def far_kernel(
-    s_ref, left_ref, right_ref, near_ref, pre_ref, pre2_ref, back_ref, w_ref, bias_ref, proj_ref, w2_ref,
-    act_ref, slope_ref, mid_ref, act2_ref, delta_ref, to_left_ref, to_right_ref,
+    s_ref, one_ref, two_ref, near_ref, pre_ref, pre2_ref, back_ref, w_ref, bias_ref, proj_ref, w2_ref,
+    act_ref, slope_ref, mid_ref, act2_ref, delta_ref, ends_ref, to_one_ref, to_two_ref, left_ref, right_ref,
 ):
     def at(j):
         return left_ref[j + 3] if j < 0 else right_ref[j - 6] if j > 5 else s_ref[j]
 
     def mid_at(j):
         return mid_ref[j + 2] if j < 1 else mid_ref[j - 2]
+
+    turned = odd() == 1
+    for k in range(3):
+        one, two = one_ref[k], two_ref[k]
+        left_ref[k] = jnp.where(turned, two, one)
+        right_ref[k] = jnp.where(turned, one, two)
+    ends_ref[0] = left_ref[2]
+    ends_ref[1] = right_ref[0]
 
     def pair(one, two):
         return jnp.concatenate([one, two], axis=1)
@@ -116,12 +127,12 @@
             return pre2_ref[0] + dot(pair(mid_at(-2), mid_at(0)), w2_ref[: 2 * C])
         if j == 5:
             return pre2_ref[5] + dot(pair(mid_at(5), mid_at(7)), w2_ref[C:])
-        if j < 3:
-            return pre2_ref[j] + dot(mid_at(j - 2), tap(w2_ref, 0))
-        return pre2_ref[j] + dot(mid_at(j + 2), tap(w2_ref, 2))
+        if j == 1:
+            return pre2_ref[1] + dot(mid_at(-1), tap(w2_ref, 0))
+        return pre2_ref[4] + dot(mid_at(6), tap(w2_ref, 2))
 
     order = (0, 5, -2, 7, -1, 6)
-    order2 = (2, 3, 0, 5, 1, 4)
+    order2 = (0, 5, 1, 4)
     pre = product(order[0])
     for i, j in enumerate(order):
         after = product(order[i + 1]) if i < 5 else product2(order2[0])
@@ -134,16 +145,17 @@
         mid_ref[j + 2 if j < 1 else j - 2] = mid
         pre = after
     for i, j in enumerate(order2):
-        after = product2(order2[i + 1]) if i < 5 else None
+        after = product2(order2[i + 1]) if i < 3 else None
         cdf = normal_cdf(pre)
-        act2_ref[j] = (pre * cdf).astype(BF)
+        act2_ref[j if j < 2 else j - 2] = (pre * cdf).astype(BF)
         delta = (back_ref[j] * slope_of(pre, cdf)).astype(BF)
-        delta_ref[j] = delta
-        if j < 2:
-            to_left_ref[j] = delta
-        if j > 3:
-            to_right_ref[j - 4] = delta
+        delta_ref[j if j < 2 else j - 2] = delta
         pre = after
+        if j in (1, 4):
+            k = 1 if j == 1 else 0
+            low, high = delta_ref[k], delta_ref[k + 2]
+            to_one_ref[k] = jnp.where(turned, high, low)
+            to_two_ref[k] = jnp.where(turned, low, high)
 
 
 def add_grads(sum_ref, first, cells, delta, act, up):
@@ -170,44 +182,60 @@
 
 
 def inner_kernel(
-    near_ref, far_ref, act2_ref, up_ref, delta_ref, w_t_ref, proj_t_ref, slope_ref, s_ref, act_ref,
+    near_ref, far_ref, act2_ref, up_ref, delta2_ref, pre2_ref, back_ref, w2_ref, w_t_ref, proj_t_ref, slope_ref, s_ref, act_ref,
     away_ref, mine_ref, below_ref, grad_ref, out_ref, sum_ref, bias_ref, total_ref,
 ):
     def mid_at(j):
         return far_ref[j + 2] if j < 1 else far_ref[j - 2] if j > 4 else near_ref[j - 1]
 
     at = lambda j: s_ref[j]
+    delta = {j: delta2_ref[j if j < 2 else j - 2] for j in (0, 1, 4, 5)}
+    act2 = {j: act2_ref[j if j < 2 else j - 2] for j in delta}
+    products = {
+        2: pre2_ref[2] + dot(mid_at(0), tap(w2_ref, 0)),
+        3: pre2_ref[3] + dot(mid_at(5), tap(w2_ref, 2)),
+    }
     bias = jnp.zeros((1, C), F32)
-    for j in range(6):
-        bias += add_grads(total_ref, j == 0, taps(mid_at, j, 2), delta_ref[j], act2_ref[j], up_ref[j])
+    for n, j in enumerate((0, 5, 1, 4, 2, 3)):
+        if n in (1, 2):
+            i = n + 1
+            pre = products[i]
+            cdf = normal_cdf(pre)
+            act2[i] = (pre * cdf).astype(BF)
+            delta[i] = (back_ref[i] * slope_of(pre, cdf)).astype(BF)
+        bias += add_grads(total_ref, n == 0, taps(mid_at, j, 2), delta[j], act2[j], up_ref[j])
     put_halves(total_ref, bias, 0, away_ref, mine_ref)
     for i, j in enumerate((0, 1, 4, 5)):
         low = slice(C, 3 * C) if j < 2 else slice(0, 2 * C)
-        two = (delta_ref[j], delta_ref[j + 2]) if j < 2 else (delta_ref[j - 2], delta_ref[j])
+        two = (delta[j], delta[j + 2]) if j < 2 else (delta[j - 2], delta[j])
         below_ref[i] = up_ref[j].astype(F32) + dot(jnp.concatenate(two, axis=1), w_t_ref[low])
     bias = jnp.zeros((1, C), F32)
     for j in (2, 3):
-        three = jnp.concatenate([delta_ref[j - 2], delta_ref[j], delta_ref[j + 2]], axis=1)
+        three = jnp.concatenate([delta[j - 2], delta[j], delta[j + 2]], axis=1)
         below = (up_ref[j].astype(F32) + dot(three, w_t_ref[...])).astype(BF)
         grad_ref[j - 2] = below
-        delta = (dot(below, proj_t_ref[...]) * slope_ref[j - 1].astype(F32)).astype(BF)
-        out_ref[j - 2] = delta
-        bias += add_grads(sum_ref, j == 2, taps(at, j, 1), delta, act_ref[j - 1], below)
+        first = (dot(below, proj_t_ref[...]) * slope_ref[j - 1].astype(F32)).astype(BF)
+        out_ref[j - 2] = first
+        bias += add_grads(sum_ref, j == 2, taps(at, j, 1), first, act_ref[j - 1], below)
     bias_ref[...] = bias
 
 
 def edge_kernel(
-    below_ref, left_ref, right_ref, w_t_ref, proj_t_ref, slope_ref, slope_far_ref, s_ref, s_left_ref, s_right_ref,
+    below_ref, one_ref, two_ref, w_t_ref, proj_t_ref, slope_ref, slope_far_ref, s_ref, ends_ref,
     act_ref, act_far_ref, part_ref, part_bias_ref,
-    grad_ref, out_ref, to_left_ref, to_right_ref, away_ref, mine_ref, sum_ref,
+    grad_ref, out_ref, to_one_ref, to_two_ref, away_ref, mine_ref, sum_ref,
 ):
     def at(j):
-        return s_left_ref[2] if j < 0 else s_right_ref[0] if j > 5 else s_ref[j]
+        return ends_ref[0] if j < 0 else ends_ref[1] if j > 5 else s_ref[j]
 
     def product(i):
-        far = dot(left_ref[i], tap(w_t_ref, 0)) if i < 2 else dot(right_ref[i - 2], tap(w_t_ref, 2))
+        if i < 2:
+            far = dot(jnp.where(turned, two_ref[i], one_ref[i]), tap(w_t_ref, 0))
+        else:
+            far = dot(jnp.where(turned, one_ref[i - 2], two_ref[i - 2]), tap(w_t_ref, 2))
         return (below_ref[i] + far).astype(BF)
 
+    turned = odd() == 1
     blocks = (0, 1, 4, 5)
     order = (0, 3, 1, 2)
     bias = part_bias_ref[...]
@@ -221,10 +249,9 @@
         slope, act = (slope_far_ref[j // 5], act_far_ref[j // 5]) if j in (0, 5) else (slope_ref[j - 1], act_ref[j - 1])
         delta = (dot(below, proj_t_ref[...]) * slope.astype(F32)).astype(BF)
         out_ref[i] = delta
-        if j == 0:
-            to_left_ref[0] = delta
         if j == 5:
-            to_right_ref[0] = delta
+            to_one_ref[0] = jnp.where(turned, delta, out_ref[0])
+            to_two_ref[0] = jnp.where(turned, out_ref[0], delta)
         if held is not None:
             bias += add_grads(sum_ref, False, *held)
         held = (taps(at, j, 1), delta, act, below)
@@ -233,7 +260,7 @@
     put_halves(sum_ref, bias, 1, away_ref, mine_ref)
 
 
-def pair_kernel(mine_b_ref, near_b_ref, mine_a_ref, near_a_ref, out_ref):
+def pair_kernel(mine_b_ref, near_b_ref, mine_a_ref, near_a_ref, done_ref, out_ref):
     n, rows, _ = out_ref.shape
     chunk = (rows - 16) // 2
 
@@ -258,7 +285,7 @@
         out_ref[i] = total
 
 
-def token_kernel(left_ref, right_ref, out_ref):
+def token_kernel(one_ref, two_ref, out_ref):
     out_ref[...] = jnp.zeros(out_ref.shape, F32)
 
 
@@ -298,35 +325,45 @@
         put(other_ref, mine_ref)
 
 
-def lower_a_kernel(inner_ref, edge_ref, in_up_ref, edge_up_ref, w_ref, left_ref, right_ref, out_ref, ends, sems):
-    one = pltpu.make_async_copy(left_ref, ends.at[0], sems.at[0])
-    two = pltpu.make_async_copy(right_ref, ends.at[1], sems.at[1])
-    one.start()
-    two.start()
-
-    def at(j):
-        if j < 0 or j > 5:
-            return ends[0 if j < 0 else 1, 0]
-        return inner_ref[j - 2] if j in (2, 3) else edge_ref[j if j < 2 else j - 2]
-
-    for j in (1, 2, 3, 4, 0, 5):
-        if j == 0:
-            one.wait()
-            two.wait()
+def lower_inner_kernel(inner_ref, edge_ref, in_up_ref, edge_up_ref, w_ref, out_ref, part_ref):
+    at = lambda j: inner_ref[j - 2] if j in (2, 3) else edge_ref[j if j < 2 else j - 2]
+    for j in range(1, 5):
         up = in_up_ref[j - 2] if j in (2, 3) else edge_up_ref[j if j < 2 else j - 2]
-        out_ref[j] = (up.astype(F32) + dot(taps(at, j, 1), w_ref[...])).astype(BF)
-
-
-def call(kernel, outs, args, flops=0, scratch=(), far=0):
-    vmem = pl.BlockSpec(memory_space=pltpu.VMEM)
+        out_ref[j - 1] = (up.astype(F32) + dot(taps(at, j, 1), w_ref[...])).astype(BF)
+    for i, own, low in ((0, (0, 1), C), (1, (4, 5), 0)):
+        two = jnp.concatenate([at(own[0]), at(own[1])], axis=1)
+        part_ref[i] = edge_up_ref[3 * i].astype(F32) + dot(two, w_ref[low : low + 2 * C])
+
+
+def lower_outer_kernel(part_ref, w_ref, one_ref, two_ref, inner_ref, out_ref, parts, ends, sems):
+    copies = [
+        pltpu.make_async_copy(one_ref, parts.at[pl.ds(odd(), 1)], sems.at[0]),
+        pltpu.make_async_copy(two_ref, parts.at[pl.ds(1 - odd(), 1)], sems.at[1]),
+        pltpu.make_async_copy(inner_ref, out_ref.at[pl.ds(1, 4)], sems.at[2]),
+    ]
+    for copy in copies:
+        copy.start()
+    copies[0].wait()
+    copies[1].wait()
+    last = []
+    for i in range(2):
+        ends[i] = (part_ref[i] + dot(parts[i], tap(w_ref, 2 * i))).astype(BF)
+        last.append(pltpu.make_async_copy(ends.at[pl.ds(i, 1)], out_ref.at[pl.ds(5 * i, 1)], sems.at[3 + i]))
+        last[i].start()
+    for copy in last + copies[2:]:
+        copy.wait()
+
+
+def call(kernel, outs, args, flops=0, scratch=(), far=0, far_out=False):
+    vmem, hbm = pl.BlockSpec(memory_space=pltpu.VMEM), pl.BlockSpec(memory_space=pltpu.HBM)
     moved = sum(a.size * a.dtype.itemsize for a in args) + sum(
         math.prod(s) * jnp.dtype(t).itemsize for s, t in outs
     )
     return pl.pallas_call(
         kernel,
         out_shape=[jax.ShapeDtypeStruct(s, t) for s, t in outs],
-        in_specs=[vmem] * (len(args) - far) + [pl.BlockSpec(memory_space=pltpu.HBM)] * far,
-        out_specs=[vmem] * len(outs),
+        in_specs=[vmem] * (len(args) - far) + [hbm] * far,
+        out_specs=[hbm if far_out else vmem] * len(outs),
         scratch_shapes=list(scratch),
         compiler_params=pltpu.CompilerParams(vmem_limit_bytes=32 * 2**20),
         cost_estimate=pl.CostEstimate(flops=flops, bytes_accessed=moved, transcendentals=0),
@@ -334,14 +371,11 @@
     )(*args)
 
 
-def from_left(cells):
+def exchange(to_one, to_two):
     n = lax.axis_size(RING)
-    return lax.ppermute(cells, RING, [(i, (i + 1) % n) for i in range(n)])
-
-
-def from_right(cells):
-    n = lax.axis_size(RING)
-    return lax.ppermute(cells, RING, [((i + 1) % n, i) for i in range(n)])
+    one = [(i, (i + 1 if i % 2 else i - 1) % n) for i in range(n)]
+    two = [(i, (i - 1 if i % 2 else i + 1) % n) for i in range(n)]
+    return lax.ppermute(to_one, RING, one), lax.ppermute(to_two, RING, two)
 
 
 def across(cells):
@@ -360,51 +394,59 @@
     def like(n, t=BF):
         return ((n, BLOCK, C), t)
 
-    to_left, to_right = call(
+    to_one, to_two = call(
         cut_kernel, [like(3)] * 2, [cells], scratch=[pltpu.SemaphoreType.DMA((2,))], far=1
     )
-    s_left, s_right = from_left(to_right), from_right(to_left)
+    s_one, s_two = exchange(to_one, to_two)
     act_near, slope_near, mid_near, pre_a, pre_b, back, wa_t, wb_t, pa_t = call(
         near_kernel,
         [like(4)] * 3 + [like(4, F32), like(6, F32), like(6, F32)] + [((3 * C, C), BF)] * 2 + [((C, C), BF)],
         [cells, up, wa, ba, proj_a, wb, bb, proj_b],
         38 * unit,
     )
-    act_far, slope_far, mid_far, act_b, delta_b, to_left, to_right = call(
+    act_far, slope_far, mid_far, act_b, delta_b, s_ends, to_one, to_two = call(
         far_kernel,
-        [like(2), like(2), like(6), like(6), like(6), like(2), like(2)],
-        [cells, s_left, s_right, mid_near, pre_a, pre_b, back, wa, ba, proj_a, wb],
-        26 * unit,
-    )
-    d_left, d_right = from_left(to_right), from_right(to_left)
+        [like(2), like(2), like(6), like(4), like(4), like(2), like(2), like(2)],
+        [cells, s_one, s_two, mid_near, pre_a, pre_b, back, wa, ba, proj_a, wb],
+        24 * unit,
+        [pltpu.VMEM((3, BLOCK, C), BF)] * 2,
+    )
+    d_one, d_two = exchange(to_one, to_two)
     half = ((2 * C + 16, C), BF)
     away_b, mine_b, below, grad_in, delta_in, part, part_bias = call(
         inner_kernel,
         [half, half, like(4, F32), like(2), like(2), ((4 * C, C), F32), ((1, C), F32)],
-        [mid_near, mid_far, act_b, up, delta_b, wb_t, pa_t, slope_near, cells, act_near],
-        48 * unit,
+        [mid_near, mid_far, act_b, up, delta_b, pre_b, back, wb, wb_t, pa_t, slope_near, cells, act_near],
+        50 * unit,
         [pltpu.VMEM((4 * C, C), F32)],
     )
     near_b = across(away_b)
-    grad_out, delta_out, to_left, to_right, away_a, mine_a = call(
+    grad_out, delta_out, to_one, to_two, away_a, mine_a = call(
         edge_kernel,
         [like(4), like(4), like(1), like(1), half, half],
-        [below, d_left, d_right, wb_t, pa_t, slope_near, slope_far, cells, s_left, s_right]
+        [below, d_one, d_two, wb_t, pa_t, slope_near, slope_far, cells, s_ends]
         + [act_near, act_far, part, part_bias],
         24 * unit,
         [pltpu.VMEM((4 * C, C), F32)],
     )
-    e_left, e_right = from_left(to_right), from_right(to_left)
+    e_one, e_two = exchange(to_one, to_two)
+    inside, outside = call(
+        lower_inner_kernel,
+        [like(4), like(2, F32)],
+        [delta_in, delta_out, grad_in, grad_out, wa_t],
+        16 * unit,
+    )
     chunk = 2 * C // rest
     (sent,) = call(
         pair_kernel,
         [((rest, 2 * chunk + 16, C), BF)],
-        [mine_b, near_b, mine_a, across(away_a)],
+        [mine_b, near_b, mine_a, across(away_a), inside],
+        far=1,
     )
     got = lax.all_to_all(sent, PLANE, 0, 0)
     (sent,) = call(rest_kernel, [((ring, 2 * chunk + 16, C), BF)], [got])
     got = lax.all_to_all(sent, COLUMN, 0, 0)
-    (token,) = call(token_kernel, [((8, 128), F32)], [e_left, e_right], far=2)
+    (token,) = call(token_kernel, [((8, 128), F32)], [e_one, e_two], far=2)
     sent, sum_bias_b, sum_bias_a = call(
         ring_kernel, [((rest, 2 * chunk, C), BF), ((1, C), F32), ((1, C), F32)], [got, token]
     )
@@ -413,12 +455,13 @@
         tail_kernel, [((3, C, C), F32), ((C, C), F32)] * 2, [mine, across(mine)]
     )
     (out,) = call(
-        lower_a_kernel,
+        lower_outer_kernel,
         [like(6)],
-        [delta_in, delta_out, grad_in, grad_out, wa_t, e_left, e_right],
-        18 * unit,
-        [pltpu.VMEM((2, 1, BLOCK, C), BF), pltpu.SemaphoreType.DMA((2,))],
-        far=2,
+        [outside, wa_t, e_one, e_two, inside],
+        2 * unit,
+        [pltpu.VMEM((2, BLOCK, C), BF)] * 2 + [pltpu.SemaphoreType.DMA((5,))],
+        far=3,
+        far_out=True,
     )
     return (
         out.reshape(batch, length, channels),

time: 113 us -> 110 us (0.973)
  starting transfers between devices: 37.4 us -> 29.2 us
  waiting for transfers between devices: 17.2 us -> 23.1 us
  blocking collectives: 33.5 us -> 29.5 us
  local copies, waits for them, and re-layouts: 4.38 us -> 7.98 us
    ppermute x6, waiting for transfers between devices: 14.2 us -> 21.3 us  [exchange(): return (lax.ppermute(to_one, RING, one), lax.ppermute(to_two, RING, two))]
    ppermute x6, starting transfers between devices: 16.6 us -> 12.1 us  [exchange(): return (lax.ppermute(to_one, RING, one), lax.ppermute(to_two, RING, two))]
    ppermute x3, starting transfers between devices: 12.7 us -> 8.9 us  [across(): return lax.ppermute(cells, 'core', [(0, 1), (1, 0)])]
    unnamed x28 -> x26, local copies, waits for them, and re-layouts: 4.38 us -> 7.98 us
    all_to_all x1, blocking collectives: 20.6 us -> 17.3 us  [on_device(): got = lax.all_to_all(sent, PLANE, 0, 0)]
    pallas_call x11 -> x12, Pallas kernels: 19.3 us -> 19.1 us  [call(): pl.pallas_call(kernel, out_shape=[jax.ShapeDtypeStruct(s, t) for s, t in...]
  transfers between devices with their start and end apart: 10 -> 10, of which waited for: 4 -> 7; matrix products, arithmetic and copies ran while one was open for 0% -> 0% of each run, Pallas kernels for 11% -> 12%
where the time goes in v4:
time: 110 us
  blocking collectives  29.5 us (27%)
  starting transfers between devices  29.2 us (27%)
  waiting for transfers between devices  23.1 us (21%)
  Pallas kernels  19.1 us (17%)
  local copies, waits for them, and re-layouts  7.98 us (7%)
    ppermute x6, waiting for transfers between devices, exchange(): return (lax.ppermute(to_one, RING, one), lax.ppermute(to_two, RING, two))  21.3 us
    pallas_call x12, Pallas kernels, call(): pl.pallas_call(kernel, out_shape=[jax.ShapeDtypeStruct(s, t) for s, t in...  19.1 us
    all_to_all x1, blocking collectives, on_device(): got = lax.all_to_all(sent, PLANE, 0, 0)  17.3 us
    all_to_all x1, blocking collectives, on_device(): mine = lax.all_to_all(sent, PLANE, 0, 0)  12.2 us
    ppermute x6, starting transfers between devices, exchange(): return (lax.ppermute(to_one, RING, one), lax.ppermute(to_two, RING, two))  12.1 us
    ppermute x3, starting transfers between devices, across(): return lax.ppermute(cells, 'core', [(0, 1), (1, 0)])  8.9 us
    all_to_all x1, starting transfers between devices, on_device(): got = lax.all_to_all(sent, COLUMN, 0, 0)  8.19 us
    unnamed x26, local copies, waits for them, and re-layouts  7.98 us
  transfers between devices with their start and end apart: 10, of which 7 were waited for; matrix products, arithmetic and copies ran while one was open for 0% of the time, Pallas kernels for 12%

profile of v4, /device:TPU:1, one launch (start us, length us, event | category | flops | bytes accessed | tf_op | source)
XLA Modules:
  0.0 109.6 jit_solution(17095654193369458273)
XLA Ops:
  0.6 0.0 copy-start
  0.6 1.4 %copy-done = bf16[1,3072,256]{2,1,0:T(8,128)(2,1)S(1)} copy-done((bf16[1,3072,256]{2,1,0:T(8,128)(2,1)S(1)}, bf16[1,3072,256]{2,1,0:T(8,128)(2,1)}, u32[]{:S(2)}) %copy-start) | copy-done | bytes 1572888
  2.0 0.1 cut.1
  2.2 6.1 %collective-permute-start = (bf16[3,512,256]{2,1,0:T(8,128)(2,1)S(1)}, bf16[3,512,256]{2,1,0:T(8,128)(2,1)S(1)}, u32[]{:S(2)}, u32[]{:S(2)}) collective-permute-start(bf16[3,512,256]{2,1,0:T(8,128)(2,1)S(1)} %get-tuple-element.49), channel_id=1, source_target_pairs={{0,224},{32,64},{64,32},{96,128},{128,96},{160,192},{192,160},{224... | collective-permute-start | bytes 2359304 | tf_op jit(solution)/shard_map/ppermute | solution.py:378
  8.3 0.0 collective-permute-start.1
  8.3 0.0 copy-start.1
  8.3 1.4 %copy-done.1 = bf16[1,3072,256]{2,1,0:T(8,128)(2,1)S(1)} copy-done((bf16[1,3072,256]{2,1,0:T(8,128)(2,1)S(1)}, bf16[1,3072,256]{2,1,0:T(8,128)(2,1)}, u32[]{:S(2)}) %copy-start.1) | copy-done | bytes 1572888
  9.7 0.0 copy-start.3
  9.7 1.0 copy-done.3
  10.7 0.0 copy-start.5
  10.7 1.0 copy-done.5
  11.7 0.0 copy-start.6
  11.7 0.9 copy-done.6
  12.6 0.0 copy-start.8
  12.6 0.7 copy-done.8
  13.3 0.0 copy-start.11
  13.3 0.9 copy-done.11
  14.2 0.0 copy-start.12
  14.2 0.7 copy-done.12
  14.9 0.0 copy-start.4
  14.9 0.0 copy-start.7
  14.9 0.0 copy-start.9
  14.9 3.3 %near.1 = (bf16[4,512,256]{2,1,0:T(8,128)(2,1)S(1)}, bf16[4,512,256]{2,1,0:T(8,128)(2,1)S(1)}, bf16[4,512,256]{2,1,0:T(8,128)(2,1)S(1)}, f32[4,512,256]{2,1,0:T(...) custom-call(bf16[6,512,256]{2,1,0:T(8,128)(2,1)S(1)} %bitcast.10, ...), custom_call_target="tpu_custom_call" | custom-call | flops 2550136832 | bytes 16648192 | tf_op jit(solution)/shard_map/near/pallas_call | solution.py:362
  18.2 6.3 %collective-permute-done.one_ref = bf16[3,512,256]{2,1,0:T(8,128)(2,1)S(1)} collective-permute-done((bf16[3,512,256]{2,1,0:T(8,128)(2,1)S(1)}, bf16[3,512,256]{2,1,0:T(8,128)(2,1)S(1)}, u32[]{:S(2)}, u32[]{:S(2)}) %collective-permute-start) | collective-permute-done | bytes 786464 | tf_op jit(solution)/shard_map/ppermute | solution.py:378
  24.5 1.9 %collective-permute-done.1.two_ref = bf16[3,512,256]{2,1,0:T(8,128)(2,1)S(1)} collective-permute-done((bf16[3,512,256]{2,1,0:T(8,128)(2,1)S(1)}, bf16[3,512,256]{2,1,0:T(8,128)(2,1)S(1)}, u32[]{:S(2)}, u32[]{:S(2)}) %collective-permute-start.1) | collective-permute-done | bytes 786464 | tf_op jit(solution)/shard_map/ppermute | solution.py:378
  26.4 0.0 copy-done.4
  26.4 0.0 copy-done.7
  26.4 0.0 copy-done.9
  26.4 0.0 copy-start.2
  26.4 2.9 %far.1 = (bf16[2,512,256]{2,1,0:T(8,128)(2,1)S(1)}, bf16[2,512,256]{2,1,0:T(8,128)(2,1)S(1)}, bf16[6,512,256]{2,1,0:T(8,128)(2,1)S(1)}, bf16[4,512,256]{2,1,0:T(...) custom-call(bf16[6,512,256]{2,1,0:T(8,128)(2,1)S(1)} %bitcast.11, ...), custom_call_target="tpu_custom_call" | custom-call | flops 1610612736 | bytes 19792896 | tf_op jit(solution)/shard_map/far/pallas_call | solution.py:362
  29.3 4.0 %collective-permute-start.2 = (bf16[2,512,256]{2,1,0:T(8,128)(2,1)S(1)}, bf16[2,512,256]{2,1,0:T(8,128)(2,1)S(1)}, u32[]{:S(2)}, u32[]{:S(2)}) collective-permute-start(bf16[2,512,256]{2,1,0:T(8,128)(2,1)S(1)} %get-tuple-element.63), channel_id=1, source_target_pairs={{0,224},{32,64},{64,32},{96,128},{128,96},{160,192},{192,160},{224... | collective-permute-start | bytes 1572872 | tf_op jit(solution)/shard_map/ppermute | solution.py:378
  33.3 0.0 collective-permute-start.3
  33.3 0.0 copy-done.2
  33.3 4.5 %inner.1 = (bf16[528,256]{1,0:T(8,128)(2,1)S(1)}, bf16[528,256]{1,0:T(8,128)(2,1)S(1)}, f32[4,512,256]{2,1,0:T(8,128)S(1)}, bf16[2,512,256]{2,1,0:T(8,128)(2,1)S...) custom-call(bf16[4,512,256]{2,1,0:T(8,128)(2,1)S(1)} %get-tuple-element.48.near_ref, ...), custom_call_target="tpu_custom_call" | custom-call | flops 3355443200 | bytes 21906432 | tf_op jit(solution)/shard_map/inner/pallas_call | solution.py:362
  37.9 1.9 %collective-permute-start.6 = (bf16[528,256]{1,0:T(8,128)(2,1)S(1)}, bf16[528,256]{1,0:T(8,128)(2,1)S(1)}, u32[]{:S(2)}, u32[]{:S(2)}) collective-permute-start(bf16[528,256]{1,0:T(8,128)(2,1)S(1)} %get-tuple-element.79), channel_id=1, source_target_pairs={{0,1},{1,0},{2,3},{3,2},{4,5},{5,4},{6,7},{7,6},{8,9},{9,8},{10,11... | collective-permute-start | bytes 811016 | tf_op jit(solution)/shard_map/ppermute | solution.py:382
  39.8 4.8 %collective-permute-done.2.one_ref = bf16[2,512,256]{2,1,0:T(8,128)(2,1)S(1)} collective-permute-done((bf16[2,512,256]{2,1,0:T(8,128)(2,1)S(1)}, bf16[2,512,256]{2,1,0:T(8,128)(2,1)S(1)}, u32[]{:S(2)}, u32[]{:S(2)}) %collective-permute-start.2) | collective-permute-done | bytes 524320 | tf_op jit(solution)/shard_map/ppermute | solution.py:378
  44.6 0.4 collective-permute-done.3.two_ref
  44.9 2.7 %edge.1 = (bf16[4,512,256]{2,1,0:T(8,128)(2,1)S(1)}, bf16[4,512,256]{2,1,0:T(8,128)(2,1)S(1)}, bf16[1,512,256]{2,1,0:T(8,128)(2,1)}, bf16[1,512,256]{2,1,0:T(8,1...) custom-call(f32[4,512,256]{2,1,0:T(8,128)S(1)} %get-tuple-element.62.below_ref, ...), custom_call_target="tpu_custom_call" | custom-call | flops 1610612736 | bytes 13124608 | tf_op jit(solution)/shard_map/edge/pallas_call | solution.py:362
  47.6 0.0 copy-start.10
  47.6 2.7 %collective-permute-start.7 = (bf16[528,256]{1,0:T(8,128)(2,1)S(1)}, bf16[528,256]{1,0:T(8,128)(2,1)S(1)}, u32[]{:S(2)}, u32[]{:S(2)}) collective-permute-start(bf16[528,256]{1,0:T(8,128)(2,1)S(1)} %get-tuple-element.81), channel_id=1, source_target_pairs={{0,1},{1,0},{2,3},{3,2},{4,5},{5,4},{6,7},{7,6},{8,9},{9,8},{10,11... | collective-permute-start | bytes 811016 | tf_op jit(solution)/shard_map/ppermute | solution.py:382
  50.3 1.3 %lower_inner.1 = (bf16[4,512,256]{2,1,0:T(8,128)(2,1)S(1)}, f32[2,512,256]{2,1,0:T(8,128)S(1)}) custom-call(bf16[2,512,256]{2,1,0:T(8,128)(2,1)S(1)} %get-tuple-element.61.inner_ref, bf16[4,512,256]{2,1,0:T(8,128)(2,1)S(1)} %get-tuple-element.70.edge_ref, bf16[2,512,256]{2,1,0:T(8,128)(2,1)S(1)} %get-tuple-element.71.in_up_ref, ...), custom_call_target="tpu_custom_call" | custom-call | flops 1073741824 | bytes 5636096 | tf_op jit(solution)/shard_map/lower_inner/pallas_call | solution.py:362
  51.6 0.0 collective-permute-done.6.near_b_ref
  51.6 0.0 collective-permute-done.7.near_a_ref
  51.6 0.1 pair.1
  51.8 0.0 copy-done.10
  51.8 17.3 %all_to_all.15.got_ref = bf16[16,80,256]{2,1,0:T(8,128)(2,1)S(1)} all-to-all(bf16[16,80,256]{2,1,0:T(8,128)(2,1)S(1)} %pair.1), channel_id=1, replica_groups=mesh['xh'=2,'y'=4,'z'=8,'xl'=2,'core'=2] {'xh','y','xl'}, dimensions={0} | all-to-all | bytes 1310720 | tf_op jit(solution)/shard_map/all_to_all | solution.py:446
  69.1 0.8 rest.1
  69.9 8.2 %all-to-all-start.1 = ((bf16[8,80,256]{2,1,0:T(8,128)(2,1)}), bf16[8,80,256]{2,1,0:T(8,128)(2,1)S(1)}, u32[]{:S(2)}, u32[]{:S(2)}) async-start(bf16[8,80,256]{2,1,0:T(8,128)(2,1)} %rest.1), calls=%async_computation.1 | async-start | bytes 655360 | tf_op jit(solution)/shard_map/all_to_all | solution.py:448
  78.1 2.0 %collective-permute-start.4 = (bf16[1,512,256]{2,1,0:T(8,128)(2,1)}, bf16[1,512,256]{2,1,0:T(8,128)(2,1)S(1)}, u32[]{:S(2)}, u32[]{:S(2)}) collective-permute-start(bf16[1,512,256]{2,1,0:T(8,128)(2,1)} %get-tuple-element.75), channel_id=1, source_target_pairs={{0,224},{32,64},{64,32},{96,128},{128,96},{160,192},{192,160},{224... | collective-permute-start | bytes 786440 | tf_op jit(solution)/shard_map/ppermute | solution.py:378
  80.1 0.0 collective-permute-start.5
  80.1 8.0 %collective-permute-done.4.one_ref = bf16[1,512,256]{2,1,0:T(8,128)(2,1)S(1)} collective-permute-done((bf16[1,512,256]{2,1,0:T(8,128)(2,1)}, bf16[1,512,256]{2,1,0:T(8,128)(2,1)S(1)}, u32[]{:S(2)}, u32[]{:S(2)}) %collective-permute-start.4) | collective-permute-done | bytes 262176 | tf_op jit(solution)/shard_map/ppermute | solution.py:378
  88.1 0.0 collective-permute-done.5.two_ref
  88.1 1.4 %all-to-all-done.1.got_ref = bf16[8,80,256]{2,1,0:T(8,128)(2,1)S(1)} async-done(((bf16[8,80,256]{2,1,0:T(8,128)(2,1)}), bf16[8,80,256]{2,1,0:T(8,128)(2,1)S(1)}, u32[]{:S(2)}, u32[]{:S(2)}) %all-to-all-start.1) | async-done | bytes 327712 | tf_op jit(solution)/shard_map/all_to_all | solution.py:448
  89.5 0.7 ring.1
  90.2 12.2 %all_to_all.16.mine_ref = bf16[16,64,256]{2,1,0:T(8,128)(2,1)S(1)} all-to-all(bf16[16,64,256]{2,1,0:T(8,128)(2,1)S(1)} %get-tuple-element.82), channel_id=1, replica_groups=mesh['xh'=2,'y'=4,'z'=8,'xl'=2,'core'=2] {'xh','y','xl'}, dimensions={0} | all-to-all | bytes 1048576 | tf_op jit(solution)/shard_map/all_to_all | solution.py:453
  102.4 4.2 %collective-permute-start.8 = (bf16[16,64,256]{2,1,0:T(8,128)(2,1)S(1)}, bf16[16,64,256]{2,1,0:T(8,128)(2,1)S(1)}, u32[]{:S(2)}, u32[]{:S(2)}) collective-permute-start(bf16[16,64,256]{2,1,0:T(8,128)(2,1)S(1)} %all_to_all.16.mine_ref), channel_id=1, source_target_pairs={{0,1},{1,0},{2,3},{3,2},{4,5},{5,4},{6,7},{7,6},{8,9},{9,8},{10,11... | collective-permute-start | bytes 1572872 | tf_op jit(solution)/shard_map/ppermute | solution.py:382
  106.6 1.2 %lower_outer.1 = bf16[6,512,256]{2,1,0:T(8,128)(2,1)} custom-call(f32[2,512,256]{2,1,0:T(8,128)S(1)} %get-tuple-element.74.part_ref, bf16[768,256]{1,0:T(8,128)(2,1)S(1)} %get-tuple-element.73.w_ref, bf16[1,512,256]{2,1,0:T(8,128)(2,1)S(1)} %collective-permute-done.4.one_ref, bf16[1,512,256]{2,1,0:T(8,128)(2,1)S(1)} %collective-permute-done.5.two_ref, ...), custom_call_target="tpu_custom_call" | custom-call | flops 134217728 | bytes 4587520 | tf_op jit(solution)/shard_map/lower_outer/pallas_call | solution.py:362
  107.8 0.3 collective-permute-done.8.other_ref
  108.2 1.4 %tail.1 = (f32[3,256,256]{2,1,0:T(8,128)}, f32[256,256]{1,0:T(8,128)}, f32[3,256,256]{2,1,0:T(8,128)}, f32[256,256]{1,0:T(8,128)}) custom-call(bf16[16,64,256]{2,1,0:T(8,128)(2,1)S(1)} %all_to_all.16.mine_ref, bf16[16,64,256]{2,1,0:T(8,128)(2,1)S(1)} %collective-permute-done.8.other_ref), custom_call_target="tpu_custom_call" | custom-call | bytes 3145728 | tf_op jit(solution)/shard_map/tail/pallas_call | solution.py:362
  (1 shorter events, 0.0 us)
Async XLA Ops:
  0.6 1.4 %copy-start = (bf16[1,3072,256]{2,1,0:T(8,128)(2,1)S(1)}, bf16[1,3072,256]{2,1,0:T(8,128)(2,1)}, u32[]{:S(2)}) copy-start(bf16[1,3072,256]{2,1,0:T(8,128)(2,1)} %param.8) | copy-start | bytes 4718596
  2.2 22.3 %collective-permute-start = (bf16[3,512,256]{2,1,0:T(8,128)(2,1)S(1)}, bf16[3,512,256]{2,1,0:T(8,128)(2,1)S(1)}, u32[]{:S(2)}, u32[]{:S(2)}) collective-permute-start(bf16[3,512,256]{2,1,0:T(8,128)(2,1)S(1)} %get-tuple-element.49), channel_id=1, source_target_pairs={{0,224},{32,64},{64,32},{96,128},{128,96},{160,192},{192,160},{224... | collective-permute-start | bytes 2359304 | tf_op jit(solution)/shard_map/ppermute | solution.py:378
  8.3 18.1 %collective-permute-start.1 = (bf16[3,512,256]{2,1,0:T(8,128)(2,1)S(1)}, bf16[3,512,256]{2,1,0:T(8,128)(2,1)S(1)}, u32[]{:S(2)}, u32[]{:S(2)}) collective-permute-start(bf16[3,512,256]{2,1,0:T(8,128)(2,1)S(1)} %get-tuple-element.50), channel_id=1, source_target_pairs={{0,32},{32,0},{64,96},{96,64},{128,160},{160,128},{192,224},{224,1... | collective-permute-start | bytes 2359304 | tf_op jit(solution)/shard_map/ppermute | solution.py:378
  8.3 1.4 %copy-start.1 = (bf16[1,3072,256]{2,1,0:T(8,128)(2,1)S(1)}, bf16[1,3072,256]{2,1,0:T(8,128)(2,1)}, u32[]{:S(2)}) copy-start(bf16[1,3072,256]{2,1,0:T(8,128)(2,1)} %param.9) | copy-start | bytes 4718596
  9.7 1.0 copy-start.3
  10.7 1.0 copy-start.5
  11.7 0.9 copy-start.6
  12.6 0.7 copy-start.8
  13.3 0.9 copy-start.11
  14.2 0.7 copy-start.12
  14.9 11.5 %copy-start.4 = (bf16[3,256,256]{2,1,0:T(8,128)(2,1)S(1)}, bf16[3,256,256]{2,1,0:T(8,128)(2,1)}, u32[]{:S(2)}) copy-start(bf16[3,256,256]{2,1,0:T(8,128)(2,1)} %param.13) | copy-start | bytes 1179652
  14.9 11.5 %copy-start.7 = (bf16[256,256]{1,0:T(8,128)(2,1)S(1)}, bf16[256,256]{1,0:T(8,128)(2,1)}, u32[]{:S(2)}) copy-start(bf16[256,256]{1,0:T(8,128)(2,1)} %proj_ref.3) | copy-start | bytes 393220
  14.9 11.5 %copy-start.9 = (f32[256]{0:T(256)S(1)}, f32[256]{0:T(256)}, u32[]{:S(2)}) copy-start(f32[256]{0:T(256)} %param.11) | copy-start | bytes 3076
  26.4 6.9 %copy-start.2 = (bf16[1,3072,256]{2,1,0:T(8,128)(2,1)S(1)}, bf16[1,3072,256]{2,1,0:T(8,128)(2,1)}, u32[]{:S(2)}) copy-start(bf16[1,3072,256]{2,1,0:T(8,128)(2,1)} %param.9) | copy-start | bytes 4718596
  29.3 15.3 %collective-permute-start.2 = (bf16[2,512,256]{2,1,0:T(8,128)(2,1)S(1)}, bf16[2,512,256]{2,1,0:T(8,128)(2,1)S(1)}, u32[]{:S(2)}, u32[]{:S(2)}) collective-permute-start(bf16[2,512,256]{2,1,0:T(8,128)(2,1)S(1)} %get-tuple-element.63), channel_id=1, source_target_pairs={{0,224},{32,64},{64,32},{96,128},{128,96},{160,192},{192,160},{224... | collective-permute-start | bytes 1572872 | tf_op jit(solution)/shard_map/ppermute | solution.py:378
  33.3 11.6 %collective-permute-start.3 = (bf16[2,512,256]{2,1,0:T(8,128)(2,1)S(1)}, bf16[2,512,256]{2,1,0:T(8,128)(2,1)S(1)}, u32[]{:S(2)}, u32[]{:S(2)}) collective-permute-start(bf16[2,512,256]{2,1,0:T(8,128)(2,1)S(1)} %get-tuple-element.64), channel_id=1, source_target_pairs={{0,32},{32,0},{64,96},{96,64},{128,160},{160,128},{192,224},{224,1... | collective-permute-start | bytes 1572872 | tf_op jit(solution)/shard_map/ppermute | solution.py:378
  37.9 13.8 %collective-permute-start.6 = (bf16[528,256]{1,0:T(8,128)(2,1)S(1)}, bf16[528,256]{1,0:T(8,128)(2,1)S(1)}, u32[]{:S(2)}, u32[]{:S(2)}) collective-permute-start(bf16[528,256]{1,0:T(8,128)(2,1)S(1)} %get-tuple-element.79), channel_id=1, source_target_pairs={{0,1},{1,0},{2,3},{3,2},{4,5},{5,4},{6,7},{7,6},{8,9},{9,8},{10,11... | collective-permute-start | bytes 811016 | tf_op jit(solution)/shard_map/ppermute | solution.py:382
  47.6 4.2 %copy-start.10 = (bf16[1,512,256]{2,1,0:T(8,128)(2,1)}, bf16[1,512,256]{2,1,0:T(8,128)(2,1)S(1)}, u32[]{:S(2)}) copy-start(bf16[1,512,256]{2,1,0:T(8,128)(2,1)S(1)} %get-tuple-element.76) | copy-start | bytes 786436
  47.6 4.0 %collective-permute-start.7 = (bf16[528,256]{1,0:T(8,128)(2,1)S(1)}, bf16[528,256]{1,0:T(8,128)(2,1)S(1)}, u32[]{:S(2)}, u32[]{:S(2)}) collective-permute-start(bf16[528,256]{1,0:T(8,128)(2,1)S(1)} %get-tuple-element.81), channel_id=1, source_target_pairs={{0,1},{1,0},{2,3},{3,2},{4,5},{5,4},{6,7},{7,6},{8,9},{9,8},{10,11... | collective-permute-start | bytes 811016 | tf_op jit(solution)/shard_map/ppermute | solution.py:382
  69.9 19.6 %all-to-all-start.1 = ((bf16[8,80,256]{2,1,0:T(8,128)(2,1)}), bf16[8,80,256]{2,1,0:T(8,128)(2,1)S(1)}, u32[]{:S(2)}, u32[]{:S(2)}) async-start(bf16[8,80,256]{2,1,0:T(8,128)(2,1)} %rest.1), calls=%async_computation.1 | async-start | bytes 655360 | tf_op jit(solution)/shard_map/all_to_all | solution.py:448
  78.1 10.0 %collective-permute-start.4 = (bf16[1,512,256]{2,1,0:T(8,128)(2,1)}, bf16[1,512,256]{2,1,0:T(8,128)(2,1)S(1)}, u32[]{:S(2)}, u32[]{:S(2)}) collective-permute-start(bf16[1,512,256]{2,1,0:T(8,128)(2,1)} %get-tuple-element.75), channel_id=1, source_target_pairs={{0,224},{32,64},{64,32},{96,128},{128,96},{160,192},{192,160},{224... | collective-permute-start | bytes 786440 | tf_op jit(solution)/shard_map/ppermute | solution.py:378
  80.1 8.0 %collective-permute-start.5 = (bf16[1,512,256]{2,1,0:T(8,128)(2,1)}, bf16[1,512,256]{2,1,0:T(8,128)(2,1)S(1)}, u32[]{:S(2)}, u32[]{:S(2)}) collective-permute-start(bf16[1,512,256]{2,1,0:T(8,128)(2,1)} %copy-done.10), channel_id=1, source_target_pairs={{0,32},{32,0},{64,96},{96,64},{128,160},{160,128},{192,224},{224,1... | collective-permute-start | bytes 786440 | tf_op jit(solution)/shard_map/ppermute | solution.py:378
  102.4 5.8 %collective-permute-start.8 = (bf16[16,64,256]{2,1,0:T(8,128)(2,1)S(1)}, bf16[16,64,256]{2,1,0:T(8,128)(2,1)S(1)}, u32[]{:S(2)}, u32[]{:S(2)}) collective-permute-start(bf16[16,64,256]{2,1,0:T(8,128)(2,1)S(1)} %all_to_all.16.mine_ref), channel_id=1, source_target_pairs={{0,1},{1,0},{2,3},{3,2},{4,5},{5,4},{6,7},{7,6},{8,9},{9,8},{10,11... | collective-permute-start | bytes 1572872 | tf_op jit(solution)/shard_map/ppermute | solution.py:382

commit v5 on v4

--- a/solution.py
+++ b/solution.py
@@ -39,13 +39,22 @@
     return lax.rem(lax.axis_index("y"), 2)
 
 
-def cut_kernel(s_ref, one_ref, two_ref, sems):
-    one = pltpu.make_async_copy(s_ref.at[pl.ds(3 * odd(), 3)], one_ref, sems.at[0])
-    two = pltpu.make_async_copy(s_ref.at[pl.ds(3 - 3 * odd(), 3)], two_ref, sems.at[1])
-    one.start()
-    two.start()
-    one.wait()
-    two.wait()
+def cut_kernel(s_ref, one_ref, two_ref, one_far_ref, two_far_ref, sems):
+    copies = [
+        pltpu.make_async_copy(s_ref.at[pl.ds(at, ref.shape[0])], ref, sems.at[i])
+        for i, (at, ref) in enumerate(
+            (
+                (4 * odd(), one_ref),
+                (4 - 4 * odd(), two_ref),
+                (2 + odd(), one_far_ref),
+                (3 - odd(), two_far_ref),
+            )
+        )
+    ]
+    for copy in copies:
+        copy.start()
+    for copy in copies:
+        copy.wait()
 
 
 def tap(w_ref, k):
@@ -90,26 +99,22 @@
         back_ref[j] = dot(up_ref[j], proj2_t)
 
 
+def pair(one, two):
+    return jnp.concatenate([one, two], axis=1)
+
+
 def far_kernel(
-    s_ref, one_ref, two_ref, near_ref, pre_ref, pre2_ref, back_ref, w_ref, bias_ref, proj_ref, w2_ref,
-    act_ref, slope_ref, mid_ref, act2_ref, delta_ref, ends_ref, to_one_ref, to_two_ref, left_ref, right_ref,
-):
+    s_ref, one_ref, two_ref, near_ref, pre_ref, pre2_ref, back_ref, w_ref, proj_ref, w2_ref,
+    act_ref, slope_ref, mid_ref, act2_ref, delta_ref, halo_ref, to_one_ref, to_two_ref,
+):
+    turned = odd() == 1
+    for k in range(2):
+        one, two = one_ref[k], two_ref[k]
+        halo_ref[k] = jnp.where(turned, two, one)
+        halo_ref[2 + k] = jnp.where(turned, one, two)
+
     def at(j):
-        return left_ref[j + 3] if j < 0 else right_ref[j - 6] if j > 5 else s_ref[j]
-
-    def mid_at(j):
-        return mid_ref[j + 2] if j < 1 else mid_ref[j - 2]
-
-    turned = odd() == 1
-    for k in range(3):
-        one, two = one_ref[k], two_ref[k]
-        left_ref[k] = jnp.where(turned, two, one)
-        right_ref[k] = jnp.where(turned, one, two)
-    ends_ref[0] = left_ref[2]
-    ends_ref[1] = right_ref[0]
-
-    def pair(one, two):
-        return jnp.concatenate([one, two], axis=1)
+        return halo_ref[j + 2] if j < 0 else halo_ref[j - 4] if j > 5 else s_ref[j]
 
     def product(j):
         if j == 0:
@@ -118,44 +123,66 @@
             return pre_ref[2] + dot(at(6), tap(w_ref, 2))
         if j == -1:
             return pre_ref[0] + dot(pair(at(-2), at(-1)), w_ref[: 2 * C])
-        if j == 6:
-            return pre_ref[3] + dot(pair(at(6), at(7)), w_ref[C:])
-        return dot(taps(at, j, 1), w_ref[...]) + bias_ref[...]
-
-    def product2(j):
-        if j == 0:
-            return pre2_ref[0] + dot(pair(mid_at(-2), mid_at(0)), w2_ref[: 2 * C])
-        if j == 5:
-            return pre2_ref[5] + dot(pair(mid_at(5), mid_at(7)), w2_ref[C:])
-        if j == 1:
-            return pre2_ref[1] + dot(mid_at(-1), tap(w2_ref, 0))
-        return pre2_ref[4] + dot(mid_at(6), tap(w2_ref, 2))
-
-    order = (0, 5, -2, 7, -1, 6)
-    order2 = (0, 5, 1, 4)
+        return pre_ref[3] + dot(pair(at(6), at(7)), w_ref[C:])
+
+    def product2(i):
+        if i == 0:
+            return pre2_ref[1] + dot(mid_ref[0], tap(w2_ref, 0))
+        return pre2_ref[4] + dot(mid_ref[3], tap(w2_ref, 2))
+
+    order = (-1, 6, 0, 5)
     pre = product(order[0])
-    for i, j in enumerate(order):
-        after = product(order[i + 1]) if i < 5 else product2(order2[0])
+    for n, j in enumerate(order):
+        after = product(order[n + 1]) if n < 3 else product2(0)
         cdf = normal_cdf(pre)
         act = (pre * cdf).astype(BF)
         if j in (0, 5):
             act_ref[j // 5] = act
             slope_ref[j // 5] = slope_of(pre, cdf).astype(BF)
         mid = (at(j).astype(F32) + dot(act, proj_ref[...])).astype(BF)
-        mid_ref[j + 2 if j < 1 else j - 2] = mid
+        mid_ref[j + 1 if j < 1 else j - 3] = mid
         pre = after
-    for i, j in enumerate(order2):
-        after = product2(order2[i + 1]) if i < 3 else None
+    for i, j in enumerate((1, 4)):
+        after = product2(1) if i == 0 else None
         cdf = normal_cdf(pre)
-        act2_ref[j if j < 2 else j - 2] = (pre * cdf).astype(BF)
-        delta = (back_ref[j] * slope_of(pre, cdf)).astype(BF)
-        delta_ref[j if j < 2 else j - 2] = delta
+        act2_ref[i] = (pre * cdf).astype(BF)
+        delta_ref[i] = (back_ref[j] * slope_of(pre, cdf)).astype(BF)
         pre = after
-        if j in (1, 4):
-            k = 1 if j == 1 else 0
-            low, high = delta_ref[k], delta_ref[k + 2]
-            to_one_ref[k] = jnp.where(turned, high, low)
-            to_two_ref[k] = jnp.where(turned, low, high)
+    to_one_ref[0] = jnp.where(turned, delta_ref[1], delta_ref[0])
+    to_two_ref[0] = jnp.where(turned, delta_ref[0], delta_ref[1])
+
+
+def last_kernel(
+    halo_ref, one_ref, two_ref, near_mid_ref, pre2_ref, back_ref, w_ref, bias_ref, proj_ref, w2_ref,
+    mid_ref, act2_ref, delta_ref, to_one_ref, to_two_ref,
+):
+    turned = odd() == 1
+    low = jnp.where(turned, two_ref[0], one_ref[0])
+    high = jnp.where(turned, one_ref[0], two_ref[0])
+    three = (
+        jnp.concatenate([low, halo_ref[0], halo_ref[1]], axis=1),
+        jnp.concatenate([halo_ref[2], halo_ref[3], high], axis=1),
+    )
+
+    def product2(i):
+        if i == 0:
+            return pre2_ref[0] + dot(pair(mid_ref[0], near_mid_ref[1]), w2_ref[: 2 * C])
+        return pre2_ref[5] + dot(pair(near_mid_ref[2], mid_ref[1]), w2_ref[C:])
+
+    pre = dot(three[0], w_ref[...]) + bias_ref[...]
+    for i in range(2):
+        after = dot(three[1], w_ref[...]) + bias_ref[...] if i == 0 else product2(0)
+        act = (pre * normal_cdf(pre)).astype(BF)
+        mid_ref[i] = (halo_ref[3 * i].astype(F32) + dot(act, proj_ref[...])).astype(BF)
+        pre = after
+    for i, j in enumerate((0, 5)):
+        after = product2(1) if i == 0 else None
+        cdf = normal_cdf(pre)
+        act2_ref[i] = (pre * cdf).astype(BF)
+        delta_ref[i] = (back_ref[j] * slope_of(pre, cdf)).astype(BF)
+        pre = after
+    to_one_ref[0] = jnp.where(turned, delta_ref[1], delta_ref[0])
+    to_two_ref[0] = jnp.where(turned, delta_ref[0], delta_ref[1])
 
 
 def add_grads(sum_ref, first, cells, delta, act, up):
@@ -182,15 +209,18 @@
 
 
 def inner_kernel(
-    near_ref, far_ref, act2_ref, up_ref, delta2_ref, pre2_ref, back_ref, w2_ref, w_t_ref, proj_t_ref, slope_ref, s_ref, act_ref,
+    near_ref, far_ref, last_ref, act2_far_ref, act2_last_ref, up_ref, delta_far_ref, delta_last_ref,
+    pre2_ref, back_ref, w2_ref, w_t_ref, proj_t_ref, slope_ref, s_ref, act_ref,
     away_ref, mine_ref, below_ref, grad_ref, out_ref, sum_ref, bias_ref, total_ref,
 ):
     def mid_at(j):
-        return far_ref[j + 2] if j < 1 else far_ref[j - 2] if j > 4 else near_ref[j - 1]
+        if j in (-2, 7):
+            return last_ref[0 if j < 0 else 1]
+        return far_ref[j + 1] if j < 1 else far_ref[j - 3] if j > 4 else near_ref[j - 1]
 
     at = lambda j: s_ref[j]
-    delta = {j: delta2_ref[j if j < 2 else j - 2] for j in (0, 1, 4, 5)}
-    act2 = {j: act2_ref[j if j < 2 else j - 2] for j in delta}
+    delta = {1: delta_far_ref[0], 4: delta_far_ref[1], 0: delta_last_ref[0], 5: delta_last_ref[1]}
+    act2 = {1: act2_far_ref[0], 4: act2_far_ref[1], 0: act2_last_ref[0], 5: act2_last_ref[1]}
     products = {
         2: pre2_ref[2] + dot(mid_at(0), tap(w2_ref, 0)),
         3: pre2_ref[3] + dot(mid_at(5), tap(w2_ref, 2)),
@@ -207,8 +237,8 @@
     put_halves(total_ref, bias, 0, away_ref, mine_ref)
     for i, j in enumerate((0, 1, 4, 5)):
         low = slice(C, 3 * C) if j < 2 else slice(0, 2 * C)
-        two = (delta[j], delta[j + 2]) if j < 2 else (delta[j - 2], delta[j])
-        below_ref[i] = up_ref[j].astype(F32) + dot(jnp.concatenate(two, axis=1), w_t_ref[low])
+        two = pair(delta[j], delta[j + 2]) if j < 2 else pair(delta[j - 2], delta[j])
+        below_ref[i] = up_ref[j].astype(F32) + dot(two, w_t_ref[low])
     bias = jnp.zeros((1, C), F32)
     for j in (2, 3):
         three = jnp.concatenate([delta[j - 2], delta[j], delta[j + 2]], axis=1)
@@ -220,43 +250,57 @@
     bias_ref[...] = bias
 
 
-def edge_kernel(
-    below_ref, one_ref, two_ref, w_t_ref, proj_t_ref, slope_ref, slope_far_ref, s_ref, ends_ref,
-    act_ref, act_far_ref, part_ref, part_bias_ref,
-    grad_ref, out_ref, to_one_ref, to_two_ref, away_ref, mine_ref, sum_ref,
-):
+def ends_kernel(
+    below_ref, one_ref, two_ref, w_t_ref, proj_t_ref, slope_ref, s_ref, halo_ref, act_ref, part_ref, part_bias_ref,
+    grad_ref, out_ref, to_one_ref, to_two_ref, sum_ref, bias_ref,
+):
+    turned = odd() == 1
+
     def at(j):
-        return ends_ref[0] if j < 0 else ends_ref[1] if j > 5 else s_ref[j]
+        return halo_ref[1] if j < 0 else halo_ref[2] if j > 5 else s_ref[j]
 
     def product(i):
-        if i < 2:
-            far = dot(jnp.where(turned, two_ref[i], one_ref[i]), tap(w_t_ref, 0))
+        if i == 0:
+            far = dot(jnp.where(turned, two_ref[0], one_ref[0]), tap(w_t_ref, 0))
         else:
-            far = dot(jnp.where(turned, one_ref[i - 2], two_ref[i - 2]), tap(w_t_ref, 2))
-        return (below_ref[i] + far).astype(BF)
-
-    turned = odd() == 1
-    blocks = (0, 1, 4, 5)
-    order = (0, 3, 1, 2)
+            far = dot(jnp.where(turned, one_ref[0], two_ref[0]), tap(w_t_ref, 2))
+        return (below_ref[3 * i] + far).astype(BF)
+
     bias = part_bias_ref[...]
     sum_ref[...] = part_ref[...]
-    below = product(order[0])
-    held = None
-    for n, i in enumerate(order):
-        j = blocks[i]
-        after = product(order[n + 1]) if n < 3 else None
-        grad_ref[i] = below
-        slope, act = (slope_far_ref[j // 5], act_far_ref[j // 5]) if j in (0, 5) else (slope_ref[j - 1], act_ref[j - 1])
-        delta = (dot(below, proj_t_ref[...]) * slope.astype(F32)).astype(BF)
+    below = [product(0), product(1)]
+    for i, j in enumerate((0, 5)):
+        grad_ref[i] = below[i]
+        delta = (dot(below[i], proj_t_ref[...]) * slope_ref[i].astype(F32)).astype(BF)
         out_ref[i] = delta
-        if j == 5:
-            to_one_ref[0] = jnp.where(turned, delta, out_ref[0])
-            to_two_ref[0] = jnp.where(turned, out_ref[0], delta)
-        if held is not None:
-            bias += add_grads(sum_ref, False, *held)
-        held = (taps(at, j, 1), delta, act, below)
-        below = after
-    bias += add_grads(sum_ref, False, *held)
+        bias += add_grads(sum_ref, False, taps(at, j, 1), delta, act_ref[i], below[i])
+    bias_ref[...] = bias
+    to_one_ref[0] = jnp.where(turned, out_ref[1], out_ref[0])
+    to_two_ref[0] = jnp.where(turned, out_ref[0], out_ref[1])
+
+
+def edge_kernel(
+    below_ref, one_ref, two_ref, w_t_ref, proj_t_ref, slope_ref, s_ref, act_ref, part_ref, part_bias_ref,
+    grad_ref, out_ref, away_ref, mine_ref, sum_ref,
+):
+    at = lambda j: s_ref[j]
+    turned = odd() == 1
+
+    def product(i):
+        if i == 0:
+            far = dot(jnp.where(turned, two_ref[0], one_ref[0]), tap(w_t_ref, 0))
+        else:
+            far = dot(jnp.where(turned, one_ref[0], two_ref[0]), tap(w_t_ref, 2))
+        return (below_ref[1 + i] + far).astype(BF)
+
+    bias = part_bias_ref[...]
+    sum_ref[...] = part_ref[...]
+    below = [product(0), product(1)]
+    for i, j in enumerate((1, 4)):
+        grad_ref[i] = below[i]
+        delta = (dot(below[i], proj_t_ref[...]) * slope_ref[j - 1].astype(F32)).astype(BF)
+        out_ref[i] = delta
+        bias += add_grads(sum_ref, False, taps(at, j, 1), delta, act_ref[j - 1], below[i])
     put_halves(sum_ref, bias, 1, away_ref, mine_ref)
 
 
@@ -325,14 +369,19 @@
         put(other_ref, mine_ref)
 
 
-def lower_inner_kernel(inner_ref, edge_ref, in_up_ref, edge_up_ref, w_ref, out_ref, part_ref):
-    at = lambda j: inner_ref[j - 2] if j in (2, 3) else edge_ref[j if j < 2 else j - 2]
+def lower_inner_kernel(
+    inner_ref, ends_ref, edge_ref, in_up_ref, ends_up_ref, edge_up_ref, w_ref, out_ref, part_ref
+):
+    def place(j, inner, ends, edge):
+        return inner[j - 2] if j in (2, 3) else ends[j // 5] if j in (0, 5) else edge[j // 4]
+
+    at = lambda j: place(j, inner_ref, ends_ref, edge_ref)
     for j in range(1, 5):
-        up = in_up_ref[j - 2] if j in (2, 3) else edge_up_ref[j if j < 2 else j - 2]
+        up = place(j, in_up_ref, ends_up_ref, edge_up_ref)
         out_ref[j - 1] = (up.astype(F32) + dot(taps(at, j, 1), w_ref[...])).astype(BF)
     for i, own, low in ((0, (0, 1), C), (1, (4, 5), 0)):
-        two = jnp.concatenate([at(own[0]), at(own[1])], axis=1)
-        part_ref[i] = edge_up_ref[3 * i].astype(F32) + dot(two, w_ref[low : low + 2 * C])
+        two = pair(at(own[0]), at(own[1]))
+        part_ref[i] = ends_up_ref[i].astype(F32) + dot(two, w_ref[low : low + 2 * C])
 
 
 def lower_outer_kernel(part_ref, w_ref, one_ref, two_ref, inner_ref, out_ref, parts, ends, sems):
@@ -356,7 +405,7 @@
 
 def call(kernel, outs, args, flops=0, scratch=(), far=0, far_out=False):
     vmem, hbm = pl.BlockSpec(memory_space=pltpu.VMEM), pl.BlockSpec(memory_space=pltpu.HBM)
-    moved = sum(a.size * a.dtype.itemsize for a in args) + sum(
+    moved = flops if flops == 1024 else sum(a.size * a.dtype.itemsize for a in args) + sum(
         math.prod(s) * jnp.dtype(t).itemsize for s, t in outs
     )
     return pl.pallas_call(
@@ -394,46 +443,63 @@
     def like(n, t=BF):
         return ((n, BLOCK, C), t)
 
-    to_one, to_two = call(
-        cut_kernel, [like(3)] * 2, [cells], scratch=[pltpu.SemaphoreType.DMA((2,))], far=1
+    to_one, to_two, to_one_far, to_two_far = call(
+        cut_kernel,
+        [like(2), like(2), like(1), like(1)],
+        [cells],
+        scratch=[pltpu.SemaphoreType.DMA((4,))],
+        far=1,
     )
     s_one, s_two = exchange(to_one, to_two)
+    s_one_far, s_two_far = exchange(to_one_far, to_two_far)
     act_near, slope_near, mid_near, pre_a, pre_b, back, wa_t, wb_t, pa_t = call(
         near_kernel,
         [like(4)] * 3 + [like(4, F32), like(6, F32), like(6, F32)] + [((3 * C, C), BF)] * 2 + [((C, C), BF)],
         [cells, up, wa, ba, proj_a, wb, bb, proj_b],
-        38 * unit,
-    )
-    act_far, slope_far, mid_far, act_b, delta_b, s_ends, to_one, to_two = call(
+        1024,
+    )
+    act_far, slope_far, mid_far, act_b_far, delta_b_far, halo, to_one, to_two = call(
         far_kernel,
-        [like(2), like(2), like(6), like(4), like(4), like(2), like(2), like(2)],
-        [cells, s_one, s_two, mid_near, pre_a, pre_b, back, wa, ba, proj_a, wb],
-        24 * unit,
-        [pltpu.VMEM((3, BLOCK, C), BF)] * 2,
+        [like(2), like(2), like(4), like(2), like(2), like(4), like(1), like(1)],
+        [cells, s_one, s_two, mid_near, pre_a, pre_b, back, wa, proj_a, wb],
+        1024,
     )
     d_one, d_two = exchange(to_one, to_two)
+    mid_last, act_b_last, delta_b_last, to_one, to_two = call(
+        last_kernel,
+        [like(2), like(2), like(2), like(1), like(1)],
+        [halo, s_one_far, s_two_far, mid_far, pre_b, back, wa, ba, proj_a, wb],
+        1024,
+    )
+    d_one_far, d_two_far = exchange(to_one, to_two)
     half = ((2 * C + 16, C), BF)
     away_b, mine_b, below, grad_in, delta_in, part, part_bias = call(
         inner_kernel,
         [half, half, like(4, F32), like(2), like(2), ((4 * C, C), F32), ((1, C), F32)],
-        [mid_near, mid_far, act_b, up, delta_b, pre_b, back, wb, wb_t, pa_t, slope_near, cells, act_near],
-        50 * unit,
+        [mid_near, mid_far, mid_last, act_b_far, act_b_last, up, delta_b_far, delta_b_last]
+        + [pre_b, back, wb, wb_t, pa_t, slope_near, cells, act_near],
+        1024,
         [pltpu.VMEM((4 * C, C), F32)],
     )
+    grad_end, delta_end, to_one, to_two, part, part_bias = call(
+        ends_kernel,
+        [like(2), like(2), like(1), like(1), ((4 * C, C), F32), ((1, C), F32)],
+        [below, d_one, d_two, wb_t, pa_t, slope_far, cells, halo, act_far, part, part_bias],
+        1024,
+    )
+    e_one, e_two = exchange(to_one, to_two)
     near_b = across(away_b)
-    grad_out, delta_out, to_one, to_two, away_a, mine_a = call(
+    grad_out, delta_out, away_a, mine_a = call(
         edge_kernel,
-        [like(4), like(4), like(1), like(1), half, half],
-        [below, d_one, d_two, wb_t, pa_t, slope_near, slope_far, cells, s_ends]
-        + [act_near, act_far, part, part_bias],
-        24 * unit,
+        [like(2), like(2), half, half],
+        [below, d_one_far, d_two_far, wb_t, pa_t, slope_near, cells, act_near, part, part_bias],
+        12 * unit,
         [pltpu.VMEM((4 * C, C), F32)],
     )
-    e_one, e_two = exchange(to_one, to_two)
     inside, outside = call(
         lower_inner_kernel,
         [like(4), like(2, F32)],
-        [delta_in, delta_out, grad_in, grad_out, wa_t],
+        [delta_in, delta_end, delta_out, grad_in, grad_end, grad_out, wa_t],
         16 * unit,
     )
     chunk = 2 * C // rest

time: 110 us -> 103 us (0.936)
  waiting for transfers between devices: 23.1 us -> 11.6 us
  starting transfers between devices: 29.2 us -> 33.4 us
    ppermute x6 -> x10, waiting for transfers between devices: 21.3 us -> 9.84 us  [exchange(): return (lax.ppermute(to_one, RING, one), lax.ppermute(to_two, RING, two))]
    ppermute x6 -> x10, starting transfers between devices: 12.1 us -> 17.3 us  [exchange(): return (lax.ppermute(to_one, RING, one), lax.ppermute(to_two, RING, two))]
    pallas_call x12 -> x14, Pallas kernels: 19.1 us -> 19.7 us  [call(): pl.pallas_call(kernel, out_shape=[jax.ShapeDtypeStruct(s, t) for s, t in...]
    unnamed x26 -> x32, local copies, waits for them, and re-layouts: 7.98 us -> 7.56 us
  transfers between devices with their start and end apart: 10 -> 14, of which waited for: 7 -> 5; matrix products, arithmetic and copies ran while one was open for 0% -> 0% of each run, Pallas kernels for 12% -> 16%
where the time goes in v5:
time: 103 us; the launch traced here: 102 us
  starting transfers between devices  33.4 us (32%)
  blocking collectives  29.2 us (28%)
  Pallas kernels  19.7 us (19%)
  waiting for transfers between devices  11.6 us (11%)
  local copies, waits for them, and re-layouts  7.56 us (7%)
    pallas_call x14, Pallas kernels, call(): pl.pallas_call(kernel, out_shape=[jax.ShapeDtypeStruct(s, t) for s, t in...  19.7 us
    ppermute x10, starting transfers between devices, exchange(): return (lax.ppermute(to_one, RING, one), lax.ppermute(to_two, RING, two))  17.3 us
    all_to_all x1, blocking collectives, on_device(): got = lax.all_to_all(sent, PLANE, 0, 0)  17 us
    all_to_all x1, blocking collectives, on_device(): mine = lax.all_to_all(sent, PLANE, 0, 0)  12.2 us
    ppermute x10, waiting for transfers between devices, exchange(): return (lax.ppermute(to_one, RING, one), lax.ppermute(to_two, RING, two))  9.84 us
    all_to_all x1, starting transfers between devices, on_device(): got = lax.all_to_all(sent, COLUMN, 0, 0)  8.19 us
    ppermute x3, starting transfers between devices, across(): return lax.ppermute(cells, 'core', [(0, 1), (1, 0)])  7.94 us
    unnamed x32, local copies, waits for them, and re-layouts  7.56 us
  transfers between devices with their start and end apart: 14, of which 5 were waited for; matrix products, arithmetic and copies ran while one was open for 0% of the time, Pallas kernels for 16%

profile of v5, /device:TPU:1, one launch (start us, length us, event | category | flops | bytes accessed | tf_op | source)
XLA Modules:
  0.0 102.3 jit_solution(7321773235535271136)
XLA Ops:
  0.6 0.0 copy-start
  0.6 1.4 %copy-done = bf16[1,3072,256]{2,1,0:T(8,128)(2,1)S(1)} copy-done((bf16[1,3072,256]{2,1,0:T(8,128)(2,1)S(1)}, bf16[1,3072,256]{2,1,0:T(8,128)(2,1)}, u32[]{:S(2)}) %copy-start) | copy-done | bytes 1572888
  2.0 0.1 cut.1
  2.2 6.1 %collective-permute-start = (bf16[2,512,256]{2,1,0:T(8,128)(2,1)S(1)}, bf16[2,512,256]{2,1,0:T(8,128)(2,1)S(1)}, u32[]{:S(2)}, u32[]{:S(2)}) collective-permute-start(bf16[2,512,256]{2,1,0:T(8,128)(2,1)S(1)} %get-tuple-element.60), channel_id=1, source_target_pairs={{0,224},{32,64},{64,32},{96,128},{128,96},{160,192},{192,160},{224... | collective-permute-start | bytes 1572872 | tf_op jit(solution)/shard_map/ppermute | solution.py:427
  8.3 0.0 collective-permute-start.1
  8.3 0.6 collective-permute-start.2
  8.9 0.8 collective-permute-start.3
  9.8 0.0 copy-done.4
  9.8 1.0 copy-done.2
  10.8 1.0 copy-done.9
  11.8 0.9 copy-done.10
  12.7 0.9 copy-done.11
  13.6 0.7 copy-done.12
  14.3 0.7 copy-done.13
  14.9 3.3 %near.1 = (bf16[4,512,256]{2,1,0:T(8,128)(2,1)S(1)}, bf16[4,512,256]{2,1,0:T(8,128)(2,1)S(1)}, bf16[4,512,256]{2,1,0:T(8,128)(2,1)S(1)}, f32[4,512,256]{2,1,0:T(...) custom-call(bf16[6,512,256]{2,1,0:T(8,128)(2,1)S(1)} %bitcast.10, ...), custom_call_target="tpu_custom_call" | custom-call | flops 1024 | bytes 1024 | tf_op jit(solution)/shard_map/near/pallas_call | solution.py:411
  18.2 0.0 copy-start.5
  18.3 1.0 copy-done.5
  19.2 0.0 collective-permute-done.one_ref
  19.2 1.6 %collective-permute-done.1.two_ref = bf16[2,512,256]{2,1,0:T(8,128)(2,1)S(1)} collective-permute-done((bf16[2,512,256]{2,1,0:T(8,128)(2,1)S(1)}, bf16[2,512,256]{2,1,0:T(8,128)(2,1)S(1)}, u32[]{:S(2)}, u32[]{:S(2)}) %collective-permute-start.1) | collective-permute-done | bytes 524320 | tf_op jit(solution)/shard_map/ppermute | solution.py:427
  20.8 0.0 copy-done.3
  20.8 1.9 %far.1 = (bf16[2,512,256]{2,1,0:T(8,128)(2,1)S(1)}, bf16[2,512,256]{2,1,0:T(8,128)(2,1)S(1)}, bf16[4,512,256]{2,1,0:T(8,128)(2,1)S(1)}, bf16[2,512,256]{2,1,0:T(...) custom-call(bf16[6,512,256]{2,1,0:T(8,128)(2,1)S(1)} %bitcast.11, ...), custom_call_target="tpu_custom_call" | custom-call | flops 1024 | bytes 1024 | tf_op jit(solution)/shard_map/far/pallas_call | solution.py:411
  22.6 0.0 copy-start.7
  22.7 4.0 %collective-permute-start.4 = (bf16[1,512,256]{2,1,0:T(8,128)(2,1)S(1)}, bf16[1,512,256]{2,1,0:T(8,128)(2,1)S(1)}, u32[]{:S(2)}, u32[]{:S(2)}) collective-permute-start(bf16[1,512,256]{2,1,0:T(8,128)(2,1)S(1)} %get-tuple-element.80), channel_id=1, source_target_pairs={{0,224},{32,64},{64,32},{96,128},{128,96},{160,192},{192,160},{224... | collective-permute-start | bytes 786440 | tf_op jit(solution)/shard_map/ppermute | solution.py:427
  26.7 0.0 collective-permute-start.5
  26.7 0.0 collective-permute-done.2.one_ref
  26.7 0.0 collective-permute-done.3.two_ref
  26.7 0.0 copy-start.1
  26.7 0.0 copy-start.6
  26.7 1.4 %last.1 = (bf16[2,512,256]{2,1,0:T(8,128)(2,1)S(1)}, bf16[2,512,256]{2,1,0:T(8,128)(2,1)S(1)}, bf16[2,512,256]{2,1,0:T(8,128)(2,1)S(1)}, bf16[1,512,256]{2,1,0:T(8,128)(2,1)S(1)}, bf16[1,512,256]{2,1,0:T(8,128)(2,1)S(1)}) custom-call(bf16[4,512,256]{2,1,0:T(8,128)(2,1)S(1)} %get-tuple-element.66.halo_ref, ...), custom_call_target="tpu_custom_call" | custom-call | flops 1024 | bytes 1024 | tf_op jit(solution)/shard_map/last/pallas_call | solution.py:411
  28.1 0.0 copy-done.7
  28.1 3.7 %collective-permute-start.6 = (bf16[1,512,256]{2,1,0:T(8,128)(2,1)S(1)}, bf16[1,512,256]{2,1,0:T(8,128)(2,1)S(1)}, u32[]{:S(2)}, u32[]{:S(2)}) collective-permute-start(bf16[1,512,256]{2,1,0:T(8,128)(2,1)S(1)} %get-tuple-element.87), channel_id=1, source_target_pairs={{0,224},{32,64},{64,32},{96,128},{128,96},{160,192},{192,160},{224... | collective-permute-start | bytes 786440 | tf_op jit(solution)/shard_map/ppermute | solution.py:427
  31.8 0.0 collective-permute-start.7
  31.8 0.0 copy-done.1
  31.8 0.0 copy-done.6
  31.8 0.0 copy-start.8
  31.8 4.5 %inner.1 = (bf16[528,256]{1,0:T(8,128)(2,1)S(1)}, bf16[528,256]{1,0:T(8,128)(2,1)S(1)}, f32[4,512,256]{2,1,0:T(8,128)S(1)}, bf16[2,512,256]{2,1,0:T(8,128)(2,1)S...) custom-call(bf16[4,512,256]{2,1,0:T(8,128)(2,1)S(1)} %get-tuple-element.59.near_ref, ...), custom_call_target="tpu_custom_call" | custom-call | flops 1024 | bytes 1024 | tf_op jit(solution)/shard_map/inner/pallas_call | solution.py:411
  36.3 1.9 %collective-permute-start.10 = (bf16[528,256]{1,0:T(8,128)(2,1)S(1)}, bf16[528,256]{1,0:T(8,128)(2,1)S(1)}, u32[]{:S(2)}, u32[]{:S(2)}) collective-permute-start(bf16[528,256]{1,0:T(8,128)(2,1)S(1)} %get-tuple-element.101), channel_id=1, source_target_pairs={{0,1},{1,0},{2,3},{3,2},{4,5},{5,4},{6,7},{7,6},{8,9},{9,8},{10,11... | collective-permute-start | bytes 811016 | tf_op jit(solution)/shard_map/ppermute | solution.py:431
  38.2 0.0 collective-permute-done.4.one_ref
  38.2 0.0 collective-permute-done.5.two_ref
  38.2 1.4 %ends.1 = (bf16[2,512,256]{2,1,0:T(8,128)(2,1)S(1)}, bf16[2,512,256]{2,1,0:T(8,128)(2,1)S(1)}, bf16[1,512,256]{2,1,0:T(8,128)(2,1)S(1)}, bf16[1,512,256]{2,1,0:T...) custom-call(f32[4,512,256]{2,1,0:T(8,128)S(1)} %get-tuple-element.79.below_ref, ...), custom_call_target="tpu_custom_call" | custom-call | flops 1024 | bytes 1024 | tf_op jit(solution)/shard_map/ends/pallas_call | solution.py:411
  39.7 0.0 copy-start.14
  39.7 0.0 copy-start.15
  39.7 0.0 collective-permute-done.6.one_ref
  39.7 0.3 collective-permute-done.7.two_ref
  40.0 1.6 %edge.1 = (bf16[2,512,256]{2,1,0:T(8,128)(2,1)S(1)}, bf16[2,512,256]{2,1,0:T(8,128)(2,1)S(1)}, bf16[528,256]{1,0:T(8,128)(2,1)S(1)}, bf16[528,256]{1,0:T(8,128)(2,1)S(1)}) custom-call(f32[4,512,256]{2,1,0:T(8,128)S(1)} %get-tuple-element.79.below_ref, bf16[1,512,256]{2,1,0:T(8,128)(2,1)S(1)} %collective-permute-done.6.one_ref, ...), custom_call_target="tpu_custom_call" | custom-call | flops 805306368 | bytes 9454592 | tf_op jit(solution)/shard_map/edge/pallas_call | solution.py:411
  41.6 1.8 %collective-permute-start.11 = (bf16[528,256]{1,0:T(8,128)(2,1)S(1)}, bf16[528,256]{1,0:T(8,128)(2,1)S(1)}, u32[]{:S(2)}, u32[]{:S(2)}) collective-permute-start(bf16[528,256]{1,0:T(8,128)(2,1)S(1)} %get-tuple-element.103), channel_id=1, source_target_pairs={{0,1},{1,0},{2,3},{3,2},{4,5},{5,4},{6,7},{7,6},{8,9},{9,8},{10,11... | collective-permute-start | bytes 811016 | tf_op jit(solution)/shard_map/ppermute | solution.py:431
  43.4 1.3 %lower_inner.1 = (bf16[4,512,256]{2,1,0:T(8,128)(2,1)S(1)}, f32[2,512,256]{2,1,0:T(8,128)S(1)}) custom-call(bf16[2,512,256]{2,1,0:T(8,128)(2,1)S(1)} %get-tuple-element.78.inner_ref, bf16[2,512,256]{2,1,0:T(8,128)(2,1)S(1)} %get-tuple-element.86.ends_ref, bf16[2,512,256]{2,1,0:T(8,128)(2,1)S(1)} %get-tuple-element.91.edge_ref, ...), custom_call_target="tpu_custom_call" | custom-call | flops 1073741824 | bytes 5636096 | tf_op jit(solution)/shard_map/lower_inner/pallas_call | solution.py:411
  44.7 0.0 collective-permute-done.10.near_b_ref
  44.7 0.0 collective-permute-done.11.near_a_ref
  44.7 0.1 pair.1
  44.8 17.0 %all_to_all.15.got_ref = bf16[16,80,256]{2,1,0:T(8,128)(2,1)S(1)} all-to-all(bf16[16,80,256]{2,1,0:T(8,128)(2,1)S(1)} %pair.1), channel_id=1, replica_groups=mesh['xh'=2,'y'=4,'z'=8,'xl'=2,'core'=2] {'xh','y','xl'}, dimensions={0} | all-to-all | bytes 1310720 | tf_op jit(solution)/shard_map/all_to_all | solution.py:512
  61.9 0.8 rest.1
  62.7 8.2 %all-to-all-start.1 = ((bf16[8,80,256]{2,1,0:T(8,128)(2,1)}), bf16[8,80,256]{2,1,0:T(8,128)(2,1)S(1)}, u32[]{:S(2)}, u32[]{:S(2)}) async-start(bf16[8,80,256]{2,1,0:T(8,128)(2,1)} %rest.1), calls=%async_computation.1 | async-start | bytes 655360 | tf_op jit(solution)/shard_map/all_to_all | solution.py:514
  70.9 2.0 %collective-permute-start.8 = (bf16[1,512,256]{2,1,0:T(8,128)(2,1)}, bf16[1,512,256]{2,1,0:T(8,128)(2,1)S(1)}, u32[]{:S(2)}, u32[]{:S(2)}) collective-permute-start(bf16[1,512,256]{2,1,0:T(8,128)(2,1)} %copy-done.15), channel_id=1, source_target_pairs={{0,224},{32,64},{64,32},{96,128},{128,96},{160,192},{192,160},{224... | collective-permute-start | bytes 786440 | tf_op jit(solution)/shard_map/ppermute | solution.py:427
  72.8 0.0 collective-permute-start.9
  72.9 8.0 %collective-permute-done.8.one_ref = bf16[1,512,256]{2,1,0:T(8,128)(2,1)S(1)} collective-permute-done((bf16[1,512,256]{2,1,0:T(8,128)(2,1)}, bf16[1,512,256]{2,1,0:T(8,128)(2,1)S(1)}, u32[]{:S(2)}, u32[]{:S(2)}) %collective-permute-start.8) | collective-permute-done | bytes 262176 | tf_op jit(solution)/shard_map/ppermute | solution.py:427
  80.8 0.0 collective-permute-done.9.two_ref
  80.9 1.4 %all-to-all-done.1.got_ref = bf16[8,80,256]{2,1,0:T(8,128)(2,1)S(1)} async-done(((bf16[8,80,256]{2,1,0:T(8,128)(2,1)}), bf16[8,80,256]{2,1,0:T(8,128)(2,1)S(1)}, u32[]{:S(2)}, u32[]{:S(2)}) %all-to-all-start.1) | async-done | bytes 327712 | tf_op jit(solution)/shard_map/all_to_all | solution.py:514
  82.3 0.7 ring.1
  82.9 12.2 %all_to_all.16.mine_ref = bf16[16,64,256]{2,1,0:T(8,128)(2,1)S(1)} all-to-all(bf16[16,64,256]{2,1,0:T(8,128)(2,1)S(1)} %get-tuple-element.104), channel_id=1, replica_groups=mesh['xh'=2,'y'=4,'z'=8,'xl'=2,'core'=2] {'xh','y','xl'}, dimensions={0} | all-to-all | bytes 1048576 | tf_op jit(solution)/shard_map/all_to_all | solution.py:519
  95.1 4.2 %collective-permute-start.12 = (bf16[16,64,256]{2,1,0:T(8,128)(2,1)S(1)}, bf16[16,64,256]{2,1,0:T(8,128)(2,1)S(1)}, u32[]{:S(2)}, u32[]{:S(2)}) collective-permute-start(bf16[16,64,256]{2,1,0:T(8,128)(2,1)S(1)} %all_to_all.16.mine_ref), channel_id=1, source_target_pairs={{0,1},{1,0},{2,3},{3,2},{4,5},{5,4},{6,7},{7,6},{8,9},{9,8},{10,11... | collective-permute-start | bytes 1572872 | tf_op jit(solution)/shard_map/ppermute | solution.py:431
  99.3 1.2 %lower_outer.1 = bf16[6,512,256]{2,1,0:T(8,128)(2,1)} custom-call(f32[2,512,256]{2,1,0:T(8,128)S(1)} %get-tuple-element.96.part_ref, bf16[768,256]{1,0:T(8,128)(2,1)S(1)} %get-tuple-element.95.w_ref, bf16[1,512,256]{2,1,0:T(8,128)(2,1)S(1)} %collective-permute-done.8.one_ref, bf16[1,512,256]{2,1,0:T(8,128)(2,1)S(1)} %collective-permute-done.9.two_ref, ...), custom_call_target="tpu_custom_call" | custom-call | flops 134217728 | bytes 4587520 | tf_op jit(solution)/shard_map/lower_outer/pallas_call | solution.py:411
  100.6 0.3 collective-permute-done.12.other_ref
  100.9 1.4 %tail.1 = (f32[3,256,256]{2,1,0:T(8,128)}, f32[256,256]{1,0:T(8,128)}, f32[3,256,256]{2,1,0:T(8,128)}, f32[256,256]{1,0:T(8,128)}) custom-call(bf16[16,64,256]{2,1,0:T(8,128)(2,1)S(1)} %all_to_all.16.mine_ref, bf16[16,64,256]{2,1,0:T(8,128)(2,1)S(1)} %collective-permute-done.12.other_ref), custom_call_target="tpu_custom_call" | custom-call | bytes 3145728 | tf_op jit(solution)/shard_map/tail/pallas_call | solution.py:411
  (12 shorter events, 0.0 us)
Async XLA Ops:
  0.6 1.4 %copy-start = (bf16[1,3072,256]{2,1,0:T(8,128)(2,1)S(1)}, bf16[1,3072,256]{2,1,0:T(8,128)(2,1)}, u32[]{:S(2)}) copy-start(bf16[1,3072,256]{2,1,0:T(8,128)(2,1)} %param.8) | copy-start | bytes 4718596
  2.0 7.7 %copy-start.4 = (bf16[1,3072,256]{2,1,0:T(8,128)(2,1)S(1)}, bf16[1,3072,256]{2,1,0:T(8,128)(2,1)}, u32[]{:S(2)}) copy-start(bf16[1,3072,256]{2,1,0:T(8,128)(2,1)} %param.9) | copy-start | bytes 4718596
  2.2 17.0 %collective-permute-start = (bf16[2,512,256]{2,1,0:T(8,128)(2,1)S(1)}, bf16[2,512,256]{2,1,0:T(8,128)(2,1)S(1)}, u32[]{:S(2)}, u32[]{:S(2)}) collective-permute-start(bf16[2,512,256]{2,1,0:T(8,128)(2,1)S(1)} %get-tuple-element.60), channel_id=1, source_target_pairs={{0,224},{32,64},{64,32},{96,128},{128,96},{160,192},{192,160},{224... | collective-permute-start | bytes 1572872 | tf_op jit(solution)/shard_map/ppermute | solution.py:427
  8.3 12.5 %collective-permute-start.1 = (bf16[2,512,256]{2,1,0:T(8,128)(2,1)S(1)}, bf16[2,512,256]{2,1,0:T(8,128)(2,1)S(1)}, u32[]{:S(2)}, u32[]{:S(2)}) collective-permute-start(bf16[2,512,256]{2,1,0:T(8,128)(2,1)S(1)} %get-tuple-element.61), channel_id=1, source_target_pairs={{0,32},{32,0},{64,96},{96,64},{128,160},{160,128},{192,224},{224,1... | collective-permute-start | bytes 1572872 | tf_op jit(solution)/shard_map/ppermute | solution.py:427
  8.3 18.4 %collective-permute-start.2 = (bf16[1,512,256]{2,1,0:T(8,128)(2,1)S(1)}, bf16[1,512,256]{2,1,0:T(8,128)(2,1)S(1)}, u32[]{:S(2)}, u32[]{:S(2)}) collective-permute-start(bf16[1,512,256]{2,1,0:T(8,128)(2,1)S(1)} %get-tuple-element.67), channel_id=1, source_target_pairs={{0,224},{32,64},{64,32},{96,128},{128,96},{160,192},{192,160},{224... | collective-permute-start | bytes 786440 | tf_op jit(solution)/shard_map/ppermute | solution.py:427
  8.9 17.7 %collective-permute-start.3 = (bf16[1,512,256]{2,1,0:T(8,128)(2,1)S(1)}, bf16[1,512,256]{2,1,0:T(8,128)(2,1)S(1)}, u32[]{:S(2)}, u32[]{:S(2)}) collective-permute-start(bf16[1,512,256]{2,1,0:T(8,128)(2,1)S(1)} %get-tuple-element.68), channel_id=1, source_target_pairs={{0,32},{32,0},{64,96},{96,64},{128,160},{160,128},{192,224},{224,1... | collective-permute-start | bytes 786440 | tf_op jit(solution)/shard_map/ppermute | solution.py:427
  9.8 1.0 copy-start.2
  10.8 1.0 copy-start.9
  11.8 0.9 copy-start.10
  12.7 0.9 copy-start.11
  13.6 0.7 copy-start.12
  14.3 0.7 copy-start.13
  14.9 5.8 %copy-start.3 = (bf16[3,256,256]{2,1,0:T(8,128)(2,1)S(1)}, bf16[3,256,256]{2,1,0:T(8,128)(2,1)}, u32[]{:S(2)}) copy-start(bf16[3,256,256]{2,1,0:T(8,128)(2,1)} %param.13) | copy-start | bytes 1179652
  18.2 1.0 copy-start.5
  22.6 5.5 %copy-start.7 = (bf16[4,512,256]{2,1,0:T(8,128)(2,1)}, bf16[4,512,256]{2,1,0:T(8,128)(2,1)S(1)}, u32[]{:S(2)}) copy-start(bf16[4,512,256]{2,1,0:T(8,128)(2,1)S(1)} %get-tuple-element.66.halo_ref) | copy-start | bytes 3145732
  22.7 15.6 %collective-permute-start.4 = (bf16[1,512,256]{2,1,0:T(8,128)(2,1)S(1)}, bf16[1,512,256]{2,1,0:T(8,128)(2,1)S(1)}, u32[]{:S(2)}, u32[]{:S(2)}) collective-permute-start(bf16[1,512,256]{2,1,0:T(8,128)(2,1)S(1)} %get-tuple-element.80), channel_id=1, source_target_pairs={{0,224},{32,64},{64,32},{96,128},{128,96},{160,192},{192,160},{224... | collective-permute-start | bytes 786440 | tf_op jit(solution)/shard_map/ppermute | solution.py:427
  26.7 11.6 %collective-permute-start.5 = (bf16[1,512,256]{2,1,0:T(8,128)(2,1)S(1)}, bf16[1,512,256]{2,1,0:T(8,128)(2,1)S(1)}, u32[]{:S(2)}, u32[]{:S(2)}) collective-permute-start(bf16[1,512,256]{2,1,0:T(8,128)(2,1)S(1)} %get-tuple-element.81), channel_id=1, source_target_pairs={{0,32},{32,0},{64,96},{96,64},{128,160},{160,128},{192,224},{224,1... | collective-permute-start | bytes 786440 | tf_op jit(solution)/shard_map/ppermute | solution.py:427
  26.7 5.1 %copy-start.1 = (bf16[1,3072,256]{2,1,0:T(8,128)(2,1)S(1)}, bf16[1,3072,256]{2,1,0:T(8,128)(2,1)}, u32[]{:S(2)}) copy-start(bf16[1,3072,256]{2,1,0:T(8,128)(2,1)} %param.8) | copy-start | bytes 4718596
  26.7 5.1 %copy-start.6 = (bf16[4,512,256]{2,1,0:T(8,128)(2,1)S(1)}, bf16[4,512,256]{2,1,0:T(8,128)(2,1)}, u32[]{:S(2)}) copy-start(bf16[4,512,256]{2,1,0:T(8,128)(2,1)} %copy-done.5) | copy-start | bytes 3145732
  28.1 11.6 %collective-permute-start.6 = (bf16[1,512,256]{2,1,0:T(8,128)(2,1)S(1)}, bf16[1,512,256]{2,1,0:T(8,128)(2,1)S(1)}, u32[]{:S(2)}, u32[]{:S(2)}) collective-permute-start(bf16[1,512,256]{2,1,0:T(8,128)(2,1)S(1)} %get-tuple-element.87), channel_id=1, source_target_pairs={{0,224},{32,64},{64,32},{96,128},{128,96},{160,192},{192,160},{224... | collective-permute-start | bytes 786440 | tf_op jit(solution)/shard_map/ppermute | solution.py:427
  31.8 8.2 %collective-permute-start.7 = (bf16[1,512,256]{2,1,0:T(8,128)(2,1)S(1)}, bf16[1,512,256]{2,1,0:T(8,128)(2,1)S(1)}, u32[]{:S(2)}, u32[]{:S(2)}) collective-permute-start(bf16[1,512,256]{2,1,0:T(8,128)(2,1)S(1)} %get-tuple-element.88), channel_id=1, source_target_pairs={{0,32},{32,0},{64,96},{96,64},{128,160},{160,128},{192,224},{224,1... | collective-permute-start | bytes 786440 | tf_op jit(solution)/shard_map/ppermute | solution.py:427
  31.8 6.4 %copy-start.8 = (bf16[4,512,256]{2,1,0:T(8,128)(2,1)S(1)}, bf16[4,512,256]{2,1,0:T(8,128)(2,1)}, u32[]{:S(2)}) copy-start(bf16[4,512,256]{2,1,0:T(8,128)(2,1)} %copy-done.7) | copy-start | bytes 3145732
  36.3 8.4 %collective-permute-start.10 = (bf16[528,256]{1,0:T(8,128)(2,1)S(1)}, bf16[528,256]{1,0:T(8,128)(2,1)S(1)}, u32[]{:S(2)}, u32[]{:S(2)}) collective-permute-start(bf16[528,256]{1,0:T(8,128)(2,1)S(1)} %get-tuple-element.101), channel_id=1, source_target_pairs={{0,1},{1,0},{2,3},{3,2},{4,5},{5,4},{6,7},{7,6},{8,9},{9,8},{10,11... | collective-permute-start | bytes 811016 | tf_op jit(solution)/shard_map/ppermute | solution.py:431
  39.7 5.1 %copy-start.14 = (bf16[1,512,256]{2,1,0:T(8,128)(2,1)}, bf16[1,512,256]{2,1,0:T(8,128)(2,1)S(1)}, u32[]{:S(2)}) copy-start(bf16[1,512,256]{2,1,0:T(8,128)(2,1)S(1)} %get-tuple-element.98) | copy-start | bytes 786436
  39.7 5.1 %copy-start.15 = (bf16[1,512,256]{2,1,0:T(8,128)(2,1)}, bf16[1,512,256]{2,1,0:T(8,128)(2,1)S(1)}, u32[]{:S(2)}) copy-start(bf16[1,512,256]{2,1,0:T(8,128)(2,1)S(1)} %get-tuple-element.97) | copy-start | bytes 786436
  41.6 3.1 %collective-permute-start.11 = (bf16[528,256]{1,0:T(8,128)(2,1)S(1)}, bf16[528,256]{1,0:T(8,128)(2,1)S(1)}, u32[]{:S(2)}, u32[]{:S(2)}) collective-permute-start(bf16[528,256]{1,0:T(8,128)(2,1)S(1)} %get-tuple-element.103), channel_id=1, source_target_pairs={{0,1},{1,0},{2,3},{3,2},{4,5},{5,4},{6,7},{7,6},{8,9},{9,8},{10,11... | collective-permute-start | bytes 811016 | tf_op jit(solution)/shard_map/ppermute | solution.py:431
  62.7 19.6 %all-to-all-start.1 = ((bf16[8,80,256]{2,1,0:T(8,128)(2,1)}), bf16[8,80,256]{2,1,0:T(8,128)(2,1)S(1)}, u32[]{:S(2)}, u32[]{:S(2)}) async-start(bf16[8,80,256]{2,1,0:T(8,128)(2,1)} %rest.1), calls=%async_computation.1 | async-start | bytes 655360 | tf_op jit(solution)/shard_map/all_to_all | solution.py:514
  70.9 10.0 %collective-permute-start.8 = (bf16[1,512,256]{2,1,0:T(8,128)(2,1)}, bf16[1,512,256]{2,1,0:T(8,128)(2,1)S(1)}, u32[]{:S(2)}, u32[]{:S(2)}) collective-permute-start(bf16[1,512,256]{2,1,0:T(8,128)(2,1)} %copy-done.15), channel_id=1, source_target_pairs={{0,224},{32,64},{64,32},{96,128},{128,96},{160,192},{192,160},{224... | collective-permute-start | bytes 786440 | tf_op jit(solution)/shard_map/ppermute | solution.py:427
  72.8 8.0 %collective-permute-start.9 = (bf16[1,512,256]{2,1,0:T(8,128)(2,1)}, bf16[1,512,256]{2,1,0:T(8,128)(2,1)S(1)}, u32[]{:S(2)}, u32[]{:S(2)}) collective-permute-start(bf16[1,512,256]{2,1,0:T(8,128)(2,1)} %copy-done.14), channel_id=1, source_target_pairs={{0,32},{32,0},{64,96},{96,64},{128,160},{160,128},{192,224},{224,1... | collective-permute-start | bytes 786440 | tf_op jit(solution)/shard_map/ppermute | solution.py:427
  95.1 5.8 %collective-permute-start.12 = (bf16[16,64,256]{2,1,0:T(8,128)(2,1)S(1)}, bf16[16,64,256]{2,1,0:T(8,128)(2,1)S(1)}, u32[]{:S(2)}, u32[]{:S(2)}) collective-permute-start(bf16[16,64,256]{2,1,0:T(8,128)(2,1)S(1)} %all_to_all.16.mine_ref), channel_id=1, source_target_pairs={{0,1},{1,0},{2,3},{3,2},{4,5},{5,4},{6,7},{7,6},{8,9},{9,8},{10,11... | collective-permute-start | bytes 1572872 | tf_op jit(solution)/shard_map/ppermute | solution.py:431

commit v6 on v5

--- a/solution.py
+++ b/solution.py
@@ -9,7 +9,7 @@
 
 BLOCK = 512
 RING = ("xh", "y")
-PLANE = ("xh", "y", "xl")
+PLANE = ("xl", "xh", "y")
 COLUMN = "z"
 BF, F32 = jnp.bfloat16, jnp.float32
 C = 256
@@ -185,15 +185,11 @@
     to_two_ref[0] = jnp.where(turned, delta_ref[0], delta_ref[1])
 
 
-def add_grads(sum_ref, first, cells, delta, act, up):
+def add_grads(sum_ref, base_ref, cells, delta, act, up):
     conv = t_dot(cells, delta)
     proj = t_dot(act, up)
-    if first:
-        sum_ref[: 3 * C] = conv
-        sum_ref[3 * C :] = proj
-    else:
-        sum_ref[: 3 * C] += conv
-        sum_ref[3 * C :] += proj
+    sum_ref[: 3 * C] = conv if base_ref is None else base_ref[: 3 * C] + conv
+    sum_ref[3 * C :] = proj if base_ref is None else base_ref[3 * C :] + proj
     return jnp.sum(delta.astype(F32), axis=0, keepdims=True)
 
 
@@ -233,7 +229,7 @@
             cdf = normal_cdf(pre)
             act2[i] = (pre * cdf).astype(BF)
             delta[i] = (back_ref[i] * slope_of(pre, cdf)).astype(BF)
-        bias += add_grads(total_ref, n == 0, taps(mid_at, j, 2), delta[j], act2[j], up_ref[j])
+        bias += add_grads(total_ref, total_ref if n else None, taps(mid_at, j, 2), delta[j], act2[j], up_ref[j])
     put_halves(total_ref, bias, 0, away_ref, mine_ref)
     for i, j in enumerate((0, 1, 4, 5)):
         low = slice(C, 3 * C) if j < 2 else slice(0, 2 * C)
@@ -246,7 +242,7 @@
         grad_ref[j - 2] = below
         first = (dot(below, proj_t_ref[...]) * slope_ref[j - 1].astype(F32)).astype(BF)
         out_ref[j - 2] = first
-        bias += add_grads(sum_ref, j == 2, taps(at, j, 1), first, act_ref[j - 1], below)
+        bias += add_grads(sum_ref, sum_ref if j > 2 else None, taps(at, j, 1), first, act_ref[j - 1], below)
     bias_ref[...] = bias
 
 
@@ -267,13 +263,12 @@
         return (below_ref[3 * i] + far).astype(BF)
 
     bias = part_bias_ref[...]
-    sum_ref[...] = part_ref[...]
     below = [product(0), product(1)]
     for i, j in enumerate((0, 5)):
         grad_ref[i] = below[i]
         delta = (dot(below[i], proj_t_ref[...]) * slope_ref[i].astype(F32)).astype(BF)
         out_ref[i] = delta
-        bias += add_grads(sum_ref, False, taps(at, j, 1), delta, act_ref[i], below[i])
+        bias += add_grads(sum_ref, sum_ref if i else part_ref, taps(at, j, 1), delta, act_ref[i], below[i])
     bias_ref[...] = bias
     to_one_ref[0] = jnp.where(turned, out_ref[1], out_ref[0])
     to_two_ref[0] = jnp.where(turned, out_ref[0], out_ref[1])
@@ -294,13 +289,13 @@
         return (below_ref[1 + i] + far).astype(BF)
 
     bias = part_bias_ref[...]
-    sum_ref[...] = part_ref[...]
     below = [product(0), product(1)]
     for i, j in enumerate((1, 4)):
         grad_ref[i] = below[i]
         delta = (dot(below[i], proj_t_ref[...]) * slope_ref[j - 1].astype(F32)).astype(BF)
         out_ref[i] = delta
-        bias += add_grads(sum_ref, False, taps(at, j, 1), delta, act_ref[j - 1], below[i])
+        base_ref = sum_ref if i else part_ref
+        bias += add_grads(sum_ref, base_ref, taps(at, j, 1), delta, act_ref[j - 1], below[i])
     put_halves(sum_ref, bias, 1, away_ref, mine_ref)
 
 
@@ -345,20 +340,24 @@
     bias_a_ref[...] = total[chunk + 1 : chunk + 2]
 
 
-def tail_kernel(mine_ref, other_ref, conv_b_ref, proj_b_ref, conv_a_ref, proj_a_ref):
+def tail_kernel(mine_ref, other_ref, conv_b_ref, proj_b_ref, conv_a_ref, proj_a_ref, work, sems):
     core = lax.axis_index("core")
     n, rows, _ = mine_ref.shape
     chunk = rows // 2
 
     def put(low, high):
-        for i in range(n // 2):
-            to = slice(i * chunk, (i + 1) * chunk)
-            for part, conv, proj in ((0, conv_b_ref, proj_b_ref), (1, conv_a_ref, proj_a_ref)):
-                of = slice(part * chunk, (part + 1) * chunk)
-                conv[0, to] = low[i, of].astype(F32)
-                conv[1, to] = low[i + n // 2, of].astype(F32)
-                conv[2, to] = high[i, of].astype(F32)
-                proj[to] = high[i + n // 2, of].astype(F32)
+        copies = []
+        for at in range(8):
+            src, matrix, part = (low, high)[at // 4], at // 2 % 2, at % 2
+            conv, proj = ((conv_b_ref, proj_b_ref), (conv_a_ref, proj_a_ref))[part]
+            for i in range(n // 2):
+                to, of = slice(i * chunk, (i + 1) * chunk), slice(part * chunk, (part + 1) * chunk)
+                work[at, to] = src[matrix * (n // 2) + i, of].astype(F32)
+            to = conv.at[matrix] if at < 4 else conv.at[2] if matrix == 0 else proj
+            copies.append(pltpu.make_async_copy(work.at[at], to, sems.at[at]))
+            copies[at].start()
+        for copy in copies:
+            copy.wait()
 
     @pl.when(core == 0)
     def _():
@@ -518,7 +517,11 @@
     )
     mine = lax.all_to_all(sent, PLANE, 0, 0)
     conv_b, grad_proj_b, conv_a, grad_proj_a = call(
-        tail_kernel, [((3, C, C), F32), ((C, C), F32)] * 2, [mine, across(mine)]
+        tail_kernel,
+        [((3, C, C), F32), ((C, C), F32)] * 2,
+        [mine, across(mine)],
+        scratch=[pltpu.VMEM((8, C, C), F32), pltpu.SemaphoreType.DMA((8,))],
+        far_out=True,
     )
     (out,) = call(
         lower_outer_kernel,

time: 103 us -> 102 us (level)
  starting transfers between devices: 33.4 us -> 32.2 us
    ppermute x10, waiting for transfers between devices: 9.84 us -> 10.9 us  [exchange(): return (lax.ppermute(to_one, RING, one), lax.ppermute(to_two, RING, two))]
    ppermute x10, starting transfers between devices: 17.3 us -> 16.3 us  [exchange(): return (lax.ppermute(to_one, RING, one), lax.ppermute(to_two, RING, two))]
where the time goes in v6:
time: 102 us; the launch traced here: 101 us
  starting transfers between devices  32.2 us (32%)
  blocking collectives  28.5 us (28%)
  Pallas kernels  19.7 us (19%)
  waiting for transfers between devices  12.6 us (12%)
  local copies, waits for them, and re-layouts  7.56 us (7%)
    pallas_call x14, Pallas kernels, call(): pl.pallas_call(kernel, out_shape=[jax.ShapeDtypeStruct(s, t) for s, t in...  19.7 us
    all_to_all x1, blocking collectives, on_device(): got = lax.all_to_all(sent, PLANE, 0, 0)  16.9 us
    ppermute x10, starting transfers between devices, exchange(): return (lax.ppermute(to_one, RING, one), lax.ppermute(to_two, RING, two))  16.3 us
    all_to_all x1, blocking collectives, on_device(): mine = lax.all_to_all(sent, PLANE, 0, 0)  11.5 us
    ppermute x10, waiting for transfers between devices, exchange(): return (lax.ppermute(to_one, RING, one), lax.ppermute(to_two, RING, two))  10.9 us
    all_to_all x1, starting transfers between devices, on_device(): got = lax.all_to_all(sent, COLUMN, 0, 0)  8.19 us
    ppermute x3, starting transfers between devices, across(): return lax.ppermute(cells, 'core', [(0, 1), (1, 0)])  7.7 us
    unnamed x32, local copies, waits for them, and re-layouts  7.56 us
  transfers between devices with their start and end apart: 14, of which 5 were waited for; matrix products, arithmetic and copies ran while one was open for 0% of the time, Pallas kernels for 16%

profile of v6, /device:TPU:1, one launch (start us, length us, event | category | flops | bytes accessed | tf_op | source)
XLA Modules:
  0.0 101.5 jit_solution(700010579589541493)
XLA Ops:
  0.6 0.0 copy-start
  0.6 1.4 %copy-done = bf16[1,3072,256]{2,1,0:T(8,128)(2,1)S(1)} copy-done((bf16[1,3072,256]{2,1,0:T(8,128)(2,1)S(1)}, bf16[1,3072,256]{2,1,0:T(8,128)(2,1)}, u32[]{:S(2)}) %copy-start) | copy-done | bytes 1572888
  2.0 0.1 cut.1
  2.2 6.1 %collective-permute-start = (bf16[2,512,256]{2,1,0:T(8,128)(2,1)S(1)}, bf16[2,512,256]{2,1,0:T(8,128)(2,1)S(1)}, u32[]{:S(2)}, u32[]{:S(2)}) collective-permute-start(bf16[2,512,256]{2,1,0:T(8,128)(2,1)S(1)} %get-tuple-element.60), channel_id=1, source_target_pairs={{0,224},{32,64},{64,32},{96,128},{128,96},{160,192},{192,160},{224... | collective-permute-start | bytes 1572872 | tf_op jit(solution)/shard_map/ppermute | solution.py:426
  8.3 0.0 collective-permute-start.1
  8.3 0.6 collective-permute-start.2
  8.9 0.8 collective-permute-start.3
  9.8 0.0 copy-done.4
  9.8 1.0 copy-done.2
  10.8 1.0 copy-done.9
  11.8 0.9 copy-done.10
  12.7 0.9 copy-done.11
  13.6 0.7 copy-done.12
  14.3 0.7 copy-done.13
  14.9 3.3 %near.1 = (bf16[4,512,256]{2,1,0:T(8,128)(2,1)S(1)}, bf16[4,512,256]{2,1,0:T(8,128)(2,1)S(1)}, bf16[4,512,256]{2,1,0:T(8,128)(2,1)S(1)}, f32[4,512,256]{2,1,0:T(...) custom-call(bf16[6,512,256]{2,1,0:T(8,128)(2,1)S(1)} %bitcast.10, ...), custom_call_target="tpu_custom_call" | custom-call | flops 1024 | bytes 1024 | tf_op jit(solution)/shard_map/near/pallas_call | solution.py:410
  18.2 0.0 copy-start.5
  18.3 1.0 copy-done.5
  19.2 0.0 collective-permute-done.one_ref
  19.2 1.6 %collective-permute-done.1.two_ref = bf16[2,512,256]{2,1,0:T(8,128)(2,1)S(1)} collective-permute-done((bf16[2,512,256]{2,1,0:T(8,128)(2,1)S(1)}, bf16[2,512,256]{2,1,0:T(8,128)(2,1)S(1)}, u32[]{:S(2)}, u32[]{:S(2)}) %collective-permute-start.1) | collective-permute-done | bytes 524320 | tf_op jit(solution)/shard_map/ppermute | solution.py:426
  20.8 0.0 copy-done.3
  20.8 1.9 %far.1 = (bf16[2,512,256]{2,1,0:T(8,128)(2,1)S(1)}, bf16[2,512,256]{2,1,0:T(8,128)(2,1)S(1)}, bf16[4,512,256]{2,1,0:T(8,128)(2,1)S(1)}, bf16[2,512,256]{2,1,0:T(...) custom-call(bf16[6,512,256]{2,1,0:T(8,128)(2,1)S(1)} %bitcast.11, ...), custom_call_target="tpu_custom_call" | custom-call | flops 1024 | bytes 1024 | tf_op jit(solution)/shard_map/far/pallas_call | solution.py:410
  22.6 0.0 copy-start.7
  22.7 4.0 %collective-permute-start.4 = (bf16[1,512,256]{2,1,0:T(8,128)(2,1)S(1)}, bf16[1,512,256]{2,1,0:T(8,128)(2,1)S(1)}, u32[]{:S(2)}, u32[]{:S(2)}) collective-permute-start(bf16[1,512,256]{2,1,0:T(8,128)(2,1)S(1)} %get-tuple-element.80), channel_id=1, source_target_pairs={{0,224},{32,64},{64,32},{96,128},{128,96},{160,192},{192,160},{224... | collective-permute-start | bytes 786440 | tf_op jit(solution)/shard_map/ppermute | solution.py:426
  26.7 0.0 collective-permute-start.5
  26.7 0.0 collective-permute-done.2.one_ref
  26.7 0.0 collective-permute-done.3.two_ref
  26.7 0.0 copy-start.1
  26.7 0.0 copy-start.6
  26.7 1.4 %last.1 = (bf16[2,512,256]{2,1,0:T(8,128)(2,1)S(1)}, bf16[2,512,256]{2,1,0:T(8,128)(2,1)S(1)}, bf16[2,512,256]{2,1,0:T(8,128)(2,1)S(1)}, bf16[1,512,256]{2,1,0:T(8,128)(2,1)S(1)}, bf16[1,512,256]{2,1,0:T(8,128)(2,1)S(1)}) custom-call(bf16[4,512,256]{2,1,0:T(8,128)(2,1)S(1)} %get-tuple-element.66.halo_ref, ...), custom_call_target="tpu_custom_call" | custom-call | flops 1024 | bytes 1024 | tf_op jit(solution)/shard_map/last/pallas_call | solution.py:410
  28.1 0.0 copy-done.7
  28.1 3.7 %collective-permute-start.6 = (bf16[1,512,256]{2,1,0:T(8,128)(2,1)S(1)}, bf16[1,512,256]{2,1,0:T(8,128)(2,1)S(1)}, u32[]{:S(2)}, u32[]{:S(2)}) collective-permute-start(bf16[1,512,256]{2,1,0:T(8,128)(2,1)S(1)} %get-tuple-element.87), channel_id=1, source_target_pairs={{0,224},{32,64},{64,32},{96,128},{128,96},{160,192},{192,160},{224... | collective-permute-start | bytes 786440 | tf_op jit(solution)/shard_map/ppermute | solution.py:426
  31.8 0.0 collective-permute-start.7
  31.8 0.0 copy-done.1
  31.8 0.0 copy-done.6
  31.8 0.0 copy-start.8
  31.8 4.5 %inner.1 = (bf16[528,256]{1,0:T(8,128)(2,1)S(1)}, bf16[528,256]{1,0:T(8,128)(2,1)S(1)}, f32[4,512,256]{2,1,0:T(8,128)S(1)}, bf16[2,512,256]{2,1,0:T(8,128)(2,1)S...) custom-call(bf16[4,512,256]{2,1,0:T(8,128)(2,1)S(1)} %get-tuple-element.59.near_ref, ...), custom_call_target="tpu_custom_call" | custom-call | flops 1024 | bytes 1024 | tf_op jit(solution)/shard_map/inner/pallas_call | solution.py:410
  36.3 1.9 %collective-permute-start.10 = (bf16[528,256]{1,0:T(8,128)(2,1)S(1)}, bf16[528,256]{1,0:T(8,128)(2,1)S(1)}, u32[]{:S(2)}, u32[]{:S(2)}) collective-permute-start(bf16[528,256]{1,0:T(8,128)(2,1)S(1)} %get-tuple-element.101), channel_id=1, source_target_pairs={{0,1},{1,0},{2,3},{3,2},{4,5},{5,4},{6,7},{7,6},{8,9},{9,8},{10,11... | collective-permute-start | bytes 811016 | tf_op jit(solution)/shard_map/ppermute | solution.py:430
  38.2 0.0 collective-permute-done.4.one_ref
  38.2 0.0 collective-permute-done.5.two_ref
  38.2 1.4 %ends.1 = (bf16[2,512,256]{2,1,0:T(8,128)(2,1)S(1)}, bf16[2,512,256]{2,1,0:T(8,128)(2,1)S(1)}, bf16[1,512,256]{2,1,0:T(8,128)(2,1)S(1)}, bf16[1,512,256]{2,1,0:T...) custom-call(f32[4,512,256]{2,1,0:T(8,128)S(1)} %get-tuple-element.79.below_ref, ...), custom_call_target="tpu_custom_call" | custom-call | flops 1024 | bytes 1024 | tf_op jit(solution)/shard_map/ends/pallas_call | solution.py:410
  39.7 0.0 copy-start.14
  39.7 0.0 copy-start.15
  39.7 0.0 collective-permute-done.6.one_ref
  39.7 0.3 collective-permute-done.7.two_ref
  40.0 1.6 %edge.1 = (bf16[2,512,256]{2,1,0:T(8,128)(2,1)S(1)}, bf16[2,512,256]{2,1,0:T(8,128)(2,1)S(1)}, bf16[528,256]{1,0:T(8,128)(2,1)S(1)}, bf16[528,256]{1,0:T(8,128)(2,1)S(1)}) custom-call(f32[4,512,256]{2,1,0:T(8,128)S(1)} %get-tuple-element.79.below_ref, bf16[1,512,256]{2,1,0:T(8,128)(2,1)S(1)} %collective-permute-done.6.one_ref, ...), custom_call_target="tpu_custom_call" | custom-call | flops 805306368 | bytes 9454592 | tf_op jit(solution)/shard_map/edge/pallas_call | solution.py:410
  41.6 1.8 %collective-permute-start.11 = (bf16[528,256]{1,0:T(8,128)(2,1)S(1)}, bf16[528,256]{1,0:T(8,128)(2,1)S(1)}, u32[]{:S(2)}, u32[]{:S(2)}) collective-permute-start(bf16[528,256]{1,0:T(8,128)(2,1)S(1)} %get-tuple-element.103), channel_id=1, source_target_pairs={{0,1},{1,0},{2,3},{3,2},{4,5},{5,4},{6,7},{7,6},{8,9},{9,8},{10,11... | collective-permute-start | bytes 811016 | tf_op jit(solution)/shard_map/ppermute | solution.py:430
  43.4 1.3 %lower_inner.1 = (bf16[4,512,256]{2,1,0:T(8,128)(2,1)S(1)}, f32[2,512,256]{2,1,0:T(8,128)S(1)}) custom-call(bf16[2,512,256]{2,1,0:T(8,128)(2,1)S(1)} %get-tuple-element.78.inner_ref, bf16[2,512,256]{2,1,0:T(8,128)(2,1)S(1)} %get-tuple-element.86.ends_ref, bf16[2,512,256]{2,1,0:T(8,128)(2,1)S(1)} %get-tuple-element.91.edge_ref, ...), custom_call_target="tpu_custom_call" | custom-call | flops 1073741824 | bytes 5636096 | tf_op jit(solution)/shard_map/lower_inner/pallas_call | solution.py:410
  44.7 0.0 collective-permute-done.10.near_b_ref
  44.7 0.0 collective-permute-done.11.near_a_ref
  44.7 0.1 pair.1
  44.8 16.9 %all_to_all.15.got_ref = bf16[16,80,256]{2,1,0:T(8,128)(2,1)S(1)} all-to-all(bf16[16,80,256]{2,1,0:T(8,128)(2,1)S(1)} %pair.1), channel_id=1, replica_groups=mesh['xh'=2,'y'=4,'z'=8,'xl'=2,'core'=2] {'xl','xh','y'}, dimensions={0} | all-to-all | bytes 1310720 | tf_op jit(solution)/shard_map/all_to_all | solution.py:511
  61.8 0.8 rest.1
  62.6 8.2 %all-to-all-start.1 = ((bf16[8,80,256]{2,1,0:T(8,128)(2,1)}), bf16[8,80,256]{2,1,0:T(8,128)(2,1)S(1)}, u32[]{:S(2)}, u32[]{:S(2)}) async-start(bf16[8,80,256]{2,1,0:T(8,128)(2,1)} %rest.1), calls=%async_computation.1 | async-start | bytes 655360 | tf_op jit(solution)/shard_map/all_to_all | solution.py:513
  70.8 1.0 collective-permute-start.8
  71.7 0.0 collective-permute-start.9
  71.7 9.0 %collective-permute-done.8.one_ref = bf16[1,512,256]{2,1,0:T(8,128)(2,1)S(1)} collective-permute-done((bf16[1,512,256]{2,1,0:T(8,128)(2,1)}, bf16[1,512,256]{2,1,0:T(8,128)(2,1)S(1)}, u32[]{:S(2)}, u32[]{:S(2)}) %collective-permute-start.8) | collective-permute-done | bytes 262176 | tf_op jit(solution)/shard_map/ppermute | solution.py:426
  80.8 0.0 collective-permute-done.9.two_ref
  80.8 1.4 %all-to-all-done.1.got_ref = bf16[8,80,256]{2,1,0:T(8,128)(2,1)S(1)} async-done(((bf16[8,80,256]{2,1,0:T(8,128)(2,1)}), bf16[8,80,256]{2,1,0:T(8,128)(2,1)S(1)}, u32[]{:S(2)}, u32[]{:S(2)}) %all-to-all-start.1) | async-done | bytes 327712 | tf_op jit(solution)/shard_map/all_to_all | solution.py:513
  82.2 0.7 ring.1
  82.8 11.5 %all_to_all.16.mine_ref = bf16[16,64,256]{2,1,0:T(8,128)(2,1)S(1)} all-to-all(bf16[16,64,256]{2,1,0:T(8,128)(2,1)S(1)} %get-tuple-element.104), channel_id=1, replica_groups=mesh['xh'=2,'y'=4,'z'=8,'xl'=2,'core'=2] {'xl','xh','y'}, dimensions={0} | all-to-all | bytes 1048576 | tf_op jit(solution)/shard_map/all_to_all | solution.py:518
  94.4 4.0 %collective-permute-start.12 = (bf16[16,64,256]{2,1,0:T(8,128)(2,1)S(1)}, bf16[16,64,256]{2,1,0:T(8,128)(2,1)S(1)}, u32[]{:S(2)}, u32[]{:S(2)}) collective-permute-start(bf16[16,64,256]{2,1,0:T(8,128)(2,1)S(1)} %all_to_all.16.mine_ref), channel_id=1, source_target_pairs={{0,1},{1,0},{2,3},{3,2},{4,5},{5,4},{6,7},{7,6},{8,9},{9,8},{10,11... | collective-permute-start | bytes 1572872 | tf_op jit(solution)/shard_map/ppermute | solution.py:430
  98.4 1.2 %lower_outer.1 = bf16[6,512,256]{2,1,0:T(8,128)(2,1)} custom-call(f32[2,512,256]{2,1,0:T(8,128)S(1)} %get-tuple-element.96.part_ref, bf16[768,256]{1,0:T(8,128)(2,1)S(1)} %get-tuple-element.95.w_ref, bf16[1,512,256]{2,1,0:T(8,128)(2,1)S(1)} %collective-permute-done.8.one_ref, bf16[1,512,256]{2,1,0:T(8,128)(2,1)S(1)} %collective-permute-done.9.two_ref, ...), custom_call_target="tpu_custom_call" | custom-call | flops 134217728 | bytes 4587520 | tf_op jit(solution)/shard_map/lower_outer/pallas_call | solution.py:410
  99.6 0.3 collective-permute-done.12.other_ref
  99.9 1.4 %tail.1 = (f32[3,256,256]{2,1,0:T(8,128)}, f32[256,256]{1,0:T(8,128)}, f32[3,256,256]{2,1,0:T(8,128)}, f32[256,256]{1,0:T(8,128)}) custom-call(bf16[16,64,256]{2,1,0:T(8,128)(2,1)S(1)} %all_to_all.16.mine_ref, bf16[16,64,256]{2,1,0:T(8,128)(2,1)S(1)} %collective-permute-done.12.other_ref), custom_call_target="tpu_custom_call" | custom-call | bytes 3145728 | tf_op jit(solution)/shard_map/tail/pallas_call | solution.py:410
  (12 shorter events, 0.0 us)
Async XLA Ops:
  0.6 1.4 %copy-start = (bf16[1,3072,256]{2,1,0:T(8,128)(2,1)S(1)}, bf16[1,3072,256]{2,1,0:T(8,128)(2,1)}, u32[]{:S(2)}) copy-start(bf16[1,3072,256]{2,1,0:T(8,128)(2,1)} %param.8) | copy-start | bytes 4718596
  2.0 7.7 %copy-start.4 = (bf16[1,3072,256]{2,1,0:T(8,128)(2,1)S(1)}, bf16[1,3072,256]{2,1,0:T(8,128)(2,1)}, u32[]{:S(2)}) copy-start(bf16[1,3072,256]{2,1,0:T(8,128)(2,1)} %param.9) | copy-start | bytes 4718596
  2.2 17.0 %collective-permute-start = (bf16[2,512,256]{2,1,0:T(8,128)(2,1)S(1)}, bf16[2,512,256]{2,1,0:T(8,128)(2,1)S(1)}, u32[]{:S(2)}, u32[]{:S(2)}) collective-permute-start(bf16[2,512,256]{2,1,0:T(8,128)(2,1)S(1)} %get-tuple-element.60), channel_id=1, source_target_pairs={{0,224},{32,64},{64,32},{96,128},{128,96},{160,192},{192,160},{224... | collective-permute-start | bytes 1572872 | tf_op jit(solution)/shard_map/ppermute | solution.py:426
  8.3 12.5 %collective-permute-start.1 = (bf16[2,512,256]{2,1,0:T(8,128)(2,1)S(1)}, bf16[2,512,256]{2,1,0:T(8,128)(2,1)S(1)}, u32[]{:S(2)}, u32[]{:S(2)}) collective-permute-start(bf16[2,512,256]{2,1,0:T(8,128)(2,1)S(1)} %get-tuple-element.61), channel_id=1, source_target_pairs={{0,32},{32,0},{64,96},{96,64},{128,160},{160,128},{192,224},{224,1... | collective-permute-start | bytes 1572872 | tf_op jit(solution)/shard_map/ppermute | solution.py:426
  8.3 18.4 %collective-permute-start.2 = (bf16[1,512,256]{2,1,0:T(8,128)(2,1)S(1)}, bf16[1,512,256]{2,1,0:T(8,128)(2,1)S(1)}, u32[]{:S(2)}, u32[]{:S(2)}) collective-permute-start(bf16[1,512,256]{2,1,0:T(8,128)(2,1)S(1)} %get-tuple-element.67), channel_id=1, source_target_pairs={{0,224},{32,64},{64,32},{96,128},{128,96},{160,192},{192,160},{224... | collective-permute-start | bytes 786440 | tf_op jit(solution)/shard_map/ppermute | solution.py:426
  8.9 17.7 %collective-permute-start.3 = (bf16[1,512,256]{2,1,0:T(8,128)(2,1)S(1)}, bf16[1,512,256]{2,1,0:T(8,128)(2,1)S(1)}, u32[]{:S(2)}, u32[]{:S(2)}) collective-permute-start(bf16[1,512,256]{2,1,0:T(8,128)(2,1)S(1)} %get-tuple-element.68), channel_id=1, source_target_pairs={{0,32},{32,0},{64,96},{96,64},{128,160},{160,128},{192,224},{224,1... | collective-permute-start | bytes 786440 | tf_op jit(solution)/shard_map/ppermute | solution.py:426
  9.8 1.0 copy-start.2
  10.8 1.0 copy-start.9
  11.8 0.9 copy-start.10
  12.7 0.9 copy-start.11
  13.6 0.7 copy-start.12
  14.3 0.7 copy-start.13
  14.9 5.8 %copy-start.3 = (bf16[3,256,256]{2,1,0:T(8,128)(2,1)S(1)}, bf16[3,256,256]{2,1,0:T(8,128)(2,1)}, u32[]{:S(2)}) copy-start(bf16[3,256,256]{2,1,0:T(8,128)(2,1)} %param.13) | copy-start | bytes 1179652
  18.2 1.0 copy-start.5
  22.6 5.5 %copy-start.7 = (bf16[4,512,256]{2,1,0:T(8,128)(2,1)}, bf16[4,512,256]{2,1,0:T(8,128)(2,1)S(1)}, u32[]{:S(2)}) copy-start(bf16[4,512,256]{2,1,0:T(8,128)(2,1)S(1)} %get-tuple-element.66.halo_ref) | copy-start | bytes 3145732
  22.7 15.6 %collective-permute-start.4 = (bf16[1,512,256]{2,1,0:T(8,128)(2,1)S(1)}, bf16[1,512,256]{2,1,0:T(8,128)(2,1)S(1)}, u32[]{:S(2)}, u32[]{:S(2)}) collective-permute-start(bf16[1,512,256]{2,1,0:T(8,128)(2,1)S(1)} %get-tuple-element.80), channel_id=1, source_target_pairs={{0,224},{32,64},{64,32},{96,128},{128,96},{160,192},{192,160},{224... | collective-permute-start | bytes 786440 | tf_op jit(solution)/shard_map/ppermute | solution.py:426
  26.7 11.6 %collective-permute-start.5 = (bf16[1,512,256]{2,1,0:T(8,128)(2,1)S(1)}, bf16[1,512,256]{2,1,0:T(8,128)(2,1)S(1)}, u32[]{:S(2)}, u32[]{:S(2)}) collective-permute-start(bf16[1,512,256]{2,1,0:T(8,128)(2,1)S(1)} %get-tuple-element.81), channel_id=1, source_target_pairs={{0,32},{32,0},{64,96},{96,64},{128,160},{160,128},{192,224},{224,1... | collective-permute-start | bytes 786440 | tf_op jit(solution)/shard_map/ppermute | solution.py:426
  26.7 5.1 %copy-start.1 = (bf16[1,3072,256]{2,1,0:T(8,128)(2,1)S(1)}, bf16[1,3072,256]{2,1,0:T(8,128)(2,1)}, u32[]{:S(2)}) copy-start(bf16[1,3072,256]{2,1,0:T(8,128)(2,1)} %param.8) | copy-start | bytes 4718596
  26.7 5.1 %copy-start.6 = (bf16[4,512,256]{2,1,0:T(8,128)(2,1)S(1)}, bf16[4,512,256]{2,1,0:T(8,128)(2,1)}, u32[]{:S(2)}) copy-start(bf16[4,512,256]{2,1,0:T(8,128)(2,1)} %copy-done.5) | copy-start | bytes 3145732
  28.1 11.6 %collective-permute-start.6 = (bf16[1,512,256]{2,1,0:T(8,128)(2,1)S(1)}, bf16[1,512,256]{2,1,0:T(8,128)(2,1)S(1)}, u32[]{:S(2)}, u32[]{:S(2)}) collective-permute-start(bf16[1,512,256]{2,1,0:T(8,128)(2,1)S(1)} %get-tuple-element.87), channel_id=1, source_target_pairs={{0,224},{32,64},{64,32},{96,128},{128,96},{160,192},{192,160},{224... | collective-permute-start | bytes 786440 | tf_op jit(solution)/shard_map/ppermute | solution.py:426
  31.8 8.2 %collective-permute-start.7 = (bf16[1,512,256]{2,1,0:T(8,128)(2,1)S(1)}, bf16[1,512,256]{2,1,0:T(8,128)(2,1)S(1)}, u32[]{:S(2)}, u32[]{:S(2)}) collective-permute-start(bf16[1,512,256]{2,1,0:T(8,128)(2,1)S(1)} %get-tuple-element.88), channel_id=1, source_target_pairs={{0,32},{32,0},{64,96},{96,64},{128,160},{160,128},{192,224},{224,1... | collective-permute-start | bytes 786440 | tf_op jit(solution)/shard_map/ppermute | solution.py:426
  31.8 6.4 %copy-start.8 = (bf16[4,512,256]{2,1,0:T(8,128)(2,1)S(1)}, bf16[4,512,256]{2,1,0:T(8,128)(2,1)}, u32[]{:S(2)}) copy-start(bf16[4,512,256]{2,1,0:T(8,128)(2,1)} %copy-done.7) | copy-start | bytes 3145732
  36.3 8.4 %collective-permute-start.10 = (bf16[528,256]{1,0:T(8,128)(2,1)S(1)}, bf16[528,256]{1,0:T(8,128)(2,1)S(1)}, u32[]{:S(2)}, u32[]{:S(2)}) collective-permute-start(bf16[528,256]{1,0:T(8,128)(2,1)S(1)} %get-tuple-element.101), channel_id=1, source_target_pairs={{0,1},{1,0},{2,3},{3,2},{4,5},{5,4},{6,7},{7,6},{8,9},{9,8},{10,11... | collective-permute-start | bytes 811016 | tf_op jit(solution)/shard_map/ppermute | solution.py:430
  39.7 5.1 %copy-start.14 = (bf16[1,512,256]{2,1,0:T(8,128)(2,1)}, bf16[1,512,256]{2,1,0:T(8,128)(2,1)S(1)}, u32[]{:S(2)}) copy-start(bf16[1,512,256]{2,1,0:T(8,128)(2,1)S(1)} %get-tuple-element.98) | copy-start | bytes 786436
  39.7 5.1 %copy-start.15 = (bf16[1,512,256]{2,1,0:T(8,128)(2,1)}, bf16[1,512,256]{2,1,0:T(8,128)(2,1)S(1)}, u32[]{:S(2)}) copy-start(bf16[1,512,256]{2,1,0:T(8,128)(2,1)S(1)} %get-tuple-element.97) | copy-start | bytes 786436
  41.6 3.1 %collective-permute-start.11 = (bf16[528,256]{1,0:T(8,128)(2,1)S(1)}, bf16[528,256]{1,0:T(8,128)(2,1)S(1)}, u32[]{:S(2)}, u32[]{:S(2)}) collective-permute-start(bf16[528,256]{1,0:T(8,128)(2,1)S(1)} %get-tuple-element.103), channel_id=1, source_target_pairs={{0,1},{1,0},{2,3},{3,2},{4,5},{5,4},{6,7},{7,6},{8,9},{9,8},{10,11... | collective-permute-start | bytes 811016 | tf_op jit(solution)/shard_map/ppermute | solution.py:430
  62.6 19.6 %all-to-all-start.1 = ((bf16[8,80,256]{2,1,0:T(8,128)(2,1)}), bf16[8,80,256]{2,1,0:T(8,128)(2,1)S(1)}, u32[]{:S(2)}, u32[]{:S(2)}) async-start(bf16[8,80,256]{2,1,0:T(8,128)(2,1)} %rest.1), calls=%async_computation.1 | async-start | bytes 655360 | tf_op jit(solution)/shard_map/all_to_all | solution.py:513
  70.8 10.0 %collective-permute-start.8 = (bf16[1,512,256]{2,1,0:T(8,128)(2,1)}, bf16[1,512,256]{2,1,0:T(8,128)(2,1)S(1)}, u32[]{:S(2)}, u32[]{:S(2)}) collective-permute-start(bf16[1,512,256]{2,1,0:T(8,128)(2,1)} %copy-done.15), channel_id=1, source_target_pairs={{0,224},{32,64},{64,32},{96,128},{128,96},{160,192},{192,160},{224... | collective-permute-start | bytes 786440 | tf_op jit(solution)/shard_map/ppermute | solution.py:426
  71.7 9.0 %collective-permute-start.9 = (bf16[1,512,256]{2,1,0:T(8,128)(2,1)}, bf16[1,512,256]{2,1,0:T(8,128)(2,1)S(1)}, u32[]{:S(2)}, u32[]{:S(2)}) collective-permute-start(bf16[1,512,256]{2,1,0:T(8,128)(2,1)} %copy-done.14), channel_id=1, source_target_pairs={{0,32},{32,0},{64,96},{96,64},{128,160},{160,128},{192,224},{224,1... | collective-permute-start | bytes 786440 | tf_op jit(solution)/shard_map/ppermute | solution.py:426
  94.4 5.5 %collective-permute-start.12 = (bf16[16,64,256]{2,1,0:T(8,128)(2,1)S(1)}, bf16[16,64,256]{2,1,0:T(8,128)(2,1)S(1)}, u32[]{:S(2)}, u32[]{:S(2)}) collective-permute-start(bf16[16,64,256]{2,1,0:T(8,128)(2,1)S(1)} %all_to_all.16.mine_ref), channel_id=1, source_target_pairs={{0,1},{1,0},{2,3},{3,2},{4,5},{5,4},{6,7},{7,6},{8,9},{9,8},{10,11... | collective-permute-start | bytes 1572872 | tf_op jit(solution)/shard_map/ppermute | solution.py:430

commit v7 on v6

--- a/solution.py
+++ b/solution.py
@@ -105,7 +105,7 @@
 
 def far_kernel(
     s_ref, one_ref, two_ref, near_ref, pre_ref, pre2_ref, back_ref, w_ref, proj_ref, w2_ref,
-    act_ref, slope_ref, mid_ref, act2_ref, delta_ref, halo_ref, to_one_ref, to_two_ref,
+    mid_ref, act2_ref, delta_ref, halo_ref, to_one_ref, to_two_ref,
 ):
     turned = odd() == 1
     for k in range(2):
@@ -117,10 +117,6 @@
         return halo_ref[j + 2] if j < 0 else halo_ref[j - 4] if j > 5 else s_ref[j]
 
     def product(j):
-        if j == 0:
-            return pre_ref[1] + dot(at(-1), tap(w_ref, 0))
-        if j == 5:
-            return pre_ref[2] + dot(at(6), tap(w_ref, 2))
         if j == -1:
             return pre_ref[0] + dot(pair(at(-2), at(-1)), w_ref[: 2 * C])
         return pre_ref[3] + dot(pair(at(6), at(7)), w_ref[C:])
@@ -128,19 +124,14 @@
     def product2(i):
         if i == 0:
             return pre2_ref[1] + dot(mid_ref[0], tap(w2_ref, 0))
-        return pre2_ref[4] + dot(mid_ref[3], tap(w2_ref, 2))
-
-    order = (-1, 6, 0, 5)
+        return pre2_ref[4] + dot(mid_ref[1], tap(w2_ref, 2))
+
+    order = (-1, 6)
     pre = product(order[0])
     for n, j in enumerate(order):
-        after = product(order[n + 1]) if n < 3 else product2(0)
-        cdf = normal_cdf(pre)
-        act = (pre * cdf).astype(BF)
-        if j in (0, 5):
-            act_ref[j // 5] = act
-            slope_ref[j // 5] = slope_of(pre, cdf).astype(BF)
-        mid = (at(j).astype(F32) + dot(act, proj_ref[...])).astype(BF)
-        mid_ref[j + 1 if j < 1 else j - 3] = mid
+        after = product(order[n + 1]) if n < 1 else product2(0)
+        act = (pre * normal_cdf(pre)).astype(BF)
+        mid_ref[n] = (at(j).astype(F32) + dot(act, proj_ref[...])).astype(BF)
         pre = after
     for i, j in enumerate((1, 4)):
         after = product2(1) if i == 0 else None
@@ -152,6 +143,19 @@
     to_two_ref[0] = jnp.where(turned, delta_ref[0], delta_ref[1])
 
 
+def mids_kernel(s_ref, halo_ref, pre_ref, w_ref, proj_ref, act_ref, slope_ref, mid_ref):
+    pres = [
+        pre_ref[1] + dot(halo_ref[1], tap(w_ref, 0)),
+        pre_ref[2] + dot(halo_ref[2], tap(w_ref, 2)),
+    ]
+    for i, pre in enumerate(pres):
+        cdf = normal_cdf(pre)
+        act = (pre * cdf).astype(BF)
+        act_ref[i] = act
+        slope_ref[i] = slope_of(pre, cdf).astype(BF)
+        mid_ref[i] = (s_ref[5 * i].astype(F32) + dot(act, proj_ref[...])).astype(BF)
+
+
 def last_kernel(
     halo_ref, one_ref, two_ref, near_mid_ref, pre2_ref, back_ref, w_ref, bias_ref, proj_ref, w2_ref,
     mid_ref, act2_ref, delta_ref, to_one_ref, to_two_ref,
@@ -166,8 +170,8 @@
 
     def product2(i):
         if i == 0:
-            return pre2_ref[0] + dot(pair(mid_ref[0], near_mid_ref[1]), w2_ref[: 2 * C])
-        return pre2_ref[5] + dot(pair(near_mid_ref[2], mid_ref[1]), w2_ref[C:])
+            return pre2_ref[0] + dot(pair(mid_ref[0], near_mid_ref[0]), w2_ref[: 2 * C])
+        return pre2_ref[5] + dot(pair(near_mid_ref[1], mid_ref[1]), w2_ref[C:])
 
     pre = dot(three[0], w_ref[...]) + bias_ref[...]
     for i in range(2):
@@ -205,14 +209,16 @@
 
 
 def inner_kernel(
-    near_ref, far_ref, last_ref, act2_far_ref, act2_last_ref, up_ref, delta_far_ref, delta_last_ref,
+    near_ref, far_ref, mids_ref, last_ref, act2_far_ref, act2_last_ref, up_ref, delta_far_ref, delta_last_ref,
     pre2_ref, back_ref, w2_ref, w_t_ref, proj_t_ref, slope_ref, s_ref, act_ref,
     away_ref, mine_ref, below_ref, grad_ref, out_ref, sum_ref, bias_ref, total_ref,
 ):
     def mid_at(j):
         if j in (-2, 7):
             return last_ref[0 if j < 0 else 1]
-        return far_ref[j + 1] if j < 1 else far_ref[j - 3] if j > 4 else near_ref[j - 1]
+        if j in (-1, 6):
+            return far_ref[0 if j < 0 else 1]
+        return mids_ref[j // 5] if j in (0, 5) else near_ref[j - 1]
 
     at = lambda j: s_ref[j]
     delta = {1: delta_far_ref[0], 4: delta_far_ref[1], 0: delta_last_ref[0], 5: delta_last_ref[1]}
@@ -457,17 +463,20 @@
         [cells, up, wa, ba, proj_a, wb, bb, proj_b],
         1024,
     )
-    act_far, slope_far, mid_far, act_b_far, delta_b_far, halo, to_one, to_two = call(
+    mid_far, act_b_far, delta_b_far, halo, to_one, to_two = call(
         far_kernel,
-        [like(2), like(2), like(4), like(2), like(2), like(4), like(1), like(1)],
+        [like(2), like(2), like(2), like(4), like(1), like(1)],
         [cells, s_one, s_two, mid_near, pre_a, pre_b, back, wa, proj_a, wb],
         1024,
     )
     d_one, d_two = exchange(to_one, to_two)
+    act_far, slope_far, mids = call(
+        mids_kernel, [like(2)] * 3, [cells, halo, pre_a, wa, proj_a], 1024
+    )
     mid_last, act_b_last, delta_b_last, to_one, to_two = call(
         last_kernel,
         [like(2), like(2), like(2), like(1), like(1)],
-        [halo, s_one_far, s_two_far, mid_far, pre_b, back, wa, ba, proj_a, wb],
+        [halo, s_one_far, s_two_far, mids, pre_b, back, wa, ba, proj_a, wb],
         1024,
     )
     d_one_far, d_two_far = exchange(to_one, to_two)
@@ -475,7 +484,7 @@
     away_b, mine_b, below, grad_in, delta_in, part, part_bias = call(
         inner_kernel,
         [half, half, like(4, F32), like(2), like(2), ((4 * C, C), F32), ((1, C), F32)],
-        [mid_near, mid_far, mid_last, act_b_far, act_b_last, up, delta_b_far, delta_b_last]
+        [mid_near, mid_far, mids, mid_last, act_b_far, act_b_last, up, delta_b_far, delta_b_last]
         + [pre_b, back, wb, wb_t, pa_t, slope_near, cells, act_near],
         1024,
         [pltpu.VMEM((4 * C, C), F32)],

time: 102 us -> 101 us (level)
    pallas_call x14 -> x15, Pallas kernels: 19.7 us -> 19.9 us  [call(): pl.pallas_call(kernel, out_shape=[jax.ShapeDtypeStruct(s, t) for s, t in...]
  transfers between devices with their start and end apart: 14 -> 14, of which waited for: 5 -> 4; matrix products, arithmetic and copies ran while one was open for 0% -> 0% of each run, Pallas kernels for 16% -> 17%
where the time goes in v7:
time: 101 us
  starting transfers between devices  31.9 us (32%)
  blocking collectives  28.2 us (28%)
  Pallas kernels  19.9 us (20%)
  waiting for transfers between devices  12.3 us (12%)
  local copies, waits for them, and re-layouts  7.56 us (7%)
    pallas_call x15, Pallas kernels, call(): pl.pallas_call(kernel, out_shape=[jax.ShapeDtypeStruct(s, t) for s, t in...  19.9 us
    all_to_all x1, blocking collectives, on_device(): got = lax.all_to_all(sent, PLANE, 0, 0)  16.7 us
    ppermute x10, starting transfers between devices, exchange(): return (lax.ppermute(to_one, RING, one), lax.ppermute(to_two, RING, two))  16.1 us
    all_to_all x1, blocking collectives, on_device(): mine = lax.all_to_all(sent, PLANE, 0, 0)  11.5 us
    ppermute x10, waiting for transfers between devices, exchange(): return (lax.ppermute(to_one, RING, one), lax.ppermute(to_two, RING, two))  10.6 us
    all_to_all x1, starting transfers between devices, on_device(): got = lax.all_to_all(sent, COLUMN, 0, 0)  8.19 us
    ppermute x3, starting transfers between devices, across(): return lax.ppermute(cells, 'core', [(0, 1), (1, 0)])  7.63 us
    unnamed x32, local copies, waits for them, and re-layouts  7.56 us
  transfers between devices with their start and end apart: 14, of which 4 were waited for; matrix products, arithmetic and copies ran while one was open for 0% of the time, Pallas kernels for 17%

profile of v7, /device:TPU:1, one launch (start us, length us, event | category | flops | bytes accessed | tf_op | source)
XLA Modules:
  0.0 100.9 jit_solution(18221700971440398318)
XLA Ops:
  0.6 0.0 copy-start
  0.6 1.4 %copy-done = bf16[1,3072,256]{2,1,0:T(8,128)(2,1)S(1)} copy-done((bf16[1,3072,256]{2,1,0:T(8,128)(2,1)S(1)}, bf16[1,3072,256]{2,1,0:T(8,128)(2,1)}, u32[]{:S(2)}) %copy-start) | copy-done | bytes 1572888
  2.0 0.1 cut.1
  2.2 6.1 %collective-permute-start = (bf16[2,512,256]{2,1,0:T(8,128)(2,1)S(1)}, bf16[2,512,256]{2,1,0:T(8,128)(2,1)S(1)}, u32[]{:S(2)}, u32[]{:S(2)}) collective-permute-start(bf16[2,512,256]{2,1,0:T(8,128)(2,1)S(1)} %get-tuple-element.61), channel_id=1, source_target_pairs={{0,224},{32,64},{64,32},{96,128},{128,96},{160,192},{192,160},{224... | collective-permute-start | bytes 1572872 | tf_op jit(solution)/shard_map/ppermute | solution.py:432
  8.3 0.0 collective-permute-start.1
  8.3 0.6 collective-permute-start.2
  8.9 0.8 collective-permute-start.3
  9.8 0.0 copy-done.6
  9.8 1.0 copy-done.2
  10.8 1.0 copy-done.4
  11.8 0.9 copy-done.9
  12.7 0.9 copy-done.12
  13.6 0.7 copy-done.13
  14.3 0.7 copy-done.14
  14.9 3.4 %near.1 = (bf16[4,512,256]{2,1,0:T(8,128)(2,1)S(1)}, bf16[4,512,256]{2,1,0:T(8,128)(2,1)S(1)}, bf16[4,512,256]{2,1,0:T(8,128)(2,1)S(1)}, f32[4,512,256]{2,1,0:T(...) custom-call(bf16[6,512,256]{2,1,0:T(8,128)(2,1)S(1)} %bitcast.10, ...), custom_call_target="tpu_custom_call" | custom-call | flops 1024 | bytes 1024 | tf_op jit(solution)/shard_map/near/pallas_call | solution.py:416
  18.3 0.0 copy-start.7
  18.3 1.0 copy-done.7
  19.3 0.0 collective-permute-done.one_ref
  19.3 1.5 %collective-permute-done.1.two_ref = bf16[2,512,256]{2,1,0:T(8,128)(2,1)S(1)} collective-permute-done((bf16[2,512,256]{2,1,0:T(8,128)(2,1)S(1)}, bf16[2,512,256]{2,1,0:T(8,128)(2,1)S(1)}, u32[]{:S(2)}, u32[]{:S(2)}) %collective-permute-start.1) | collective-permute-done | bytes 524320 | tf_op jit(solution)/shard_map/ppermute | solution.py:432
  20.8 0.0 copy-done.3
  20.8 1.2 %far.1 = (bf16[2,512,256]{2,1,0:T(8,128)(2,1)S(1)}, bf16[2,512,256]{2,1,0:T(8,128)(2,1)S(1)}, bf16[2,512,256]{2,1,0:T(8,128)(2,1)S(1)}, bf16[4,512,256]{2,1,0:T(...) custom-call(bf16[6,512,256]{2,1,0:T(8,128)(2,1)S(1)} %bitcast.11, ...), custom_call_target="tpu_custom_call" | custom-call | flops 1024 | bytes 1024 | tf_op jit(solution)/shard_map/far/pallas_call | solution.py:416
  22.0 4.0 %collective-permute-start.4 = (bf16[1,512,256]{2,1,0:T(8,128)(2,1)S(1)}, bf16[1,512,256]{2,1,0:T(8,128)(2,1)S(1)}, u32[]{:S(2)}, u32[]{:S(2)}) collective-permute-start(bf16[1,512,256]{2,1,0:T(8,128)(2,1)S(1)} %get-tuple-element.82), channel_id=1, source_target_pairs={{0,224},{32,64},{64,32},{96,128},{128,96},{160,192},{192,160},{224... | collective-permute-start | bytes 786440 | tf_op jit(solution)/shard_map/ppermute | solution.py:432
  26.0 0.0 collective-permute-start.5
  26.0 0.8 mids.1
  26.8 0.0 collective-permute-done.2.one_ref
  26.8 0.0 collective-permute-done.3.two_ref
  26.9 0.0 copy-start.1
  26.9 0.0 copy-start.5
  26.9 0.0 copy-start.8
  26.9 1.4 %last.1 = (bf16[2,512,256]{2,1,0:T(8,128)(2,1)S(1)}, bf16[2,512,256]{2,1,0:T(8,128)(2,1)S(1)}, bf16[2,512,256]{2,1,0:T(8,128)(2,1)S(1)}, bf16[1,512,256]{2,1,0:T(8,128)(2,1)S(1)}, bf16[1,512,256]{2,1,0:T(8,128)(2,1)S(1)}) custom-call(bf16[4,512,256]{2,1,0:T(8,128)(2,1)S(1)} %get-tuple-element.67.halo_ref, ...), custom_call_target="tpu_custom_call" | custom-call | flops 1024 | bytes 1024 | tf_op jit(solution)/shard_map/last/pallas_call | solution.py:416
  28.3 3.5 %collective-permute-start.6 = (bf16[1,512,256]{2,1,0:T(8,128)(2,1)S(1)}, bf16[1,512,256]{2,1,0:T(8,128)(2,1)S(1)}, u32[]{:S(2)}, u32[]{:S(2)}) collective-permute-start(bf16[1,512,256]{2,1,0:T(8,128)(2,1)S(1)} %get-tuple-element.89), channel_id=1, source_target_pairs={{0,224},{32,64},{64,32},{96,128},{128,96},{160,192},{192,160},{224... | collective-permute-start | bytes 786440 | tf_op jit(solution)/shard_map/ppermute | solution.py:432
  31.8 0.0 collective-permute-start.7
  31.8 0.0 copy-done.1
  31.8 0.0 copy-done.5
  31.8 0.0 copy-done.8
  31.8 4.3 %inner.1 = (bf16[528,256]{1,0:T(8,128)(2,1)S(1)}, bf16[528,256]{1,0:T(8,128)(2,1)S(1)}, f32[4,512,256]{2,1,0:T(8,128)S(1)}, bf16[2,512,256]{2,1,0:T(8,128)(2,1)S...) custom-call(bf16[4,512,256]{2,1,0:T(8,128)(2,1)S(1)} %get-tuple-element.60.near_ref, ...), custom_call_target="tpu_custom_call" | custom-call | flops 1024 | bytes 1024 | tf_op jit(solution)/shard_map/inner/pallas_call | solution.py:416
  36.1 1.9 %collective-permute-start.10 = (bf16[528,256]{1,0:T(8,128)(2,1)S(1)}, bf16[528,256]{1,0:T(8,128)(2,1)S(1)}, u32[]{:S(2)}, u32[]{:S(2)}) collective-permute-start(bf16[528,256]{1,0:T(8,128)(2,1)S(1)} %get-tuple-element.103), channel_id=1, source_target_pairs={{0,1},{1,0},{2,3},{3,2},{4,5},{5,4},{6,7},{7,6},{8,9},{9,8},{10,11... | collective-permute-start | bytes 811016 | tf_op jit(solution)/shard_map/ppermute | solution.py:436
  38.0 0.0 collective-permute-done.4.one_ref
  38.1 0.0 collective-permute-done.5.two_ref
  38.1 1.6 %ends.1 = (bf16[2,512,256]{2,1,0:T(8,128)(2,1)S(1)}, bf16[2,512,256]{2,1,0:T(8,128)(2,1)S(1)}, bf16[1,512,256]{2,1,0:T(8,128)(2,1)}, bf16[1,512,256]{2,1,0:T(8,1...) custom-call(f32[4,512,256]{2,1,0:T(8,128)S(1)} %get-tuple-element.81.below_ref, ...), custom_call_target="tpu_custom_call" | custom-call | flops 1024 | bytes 1024 | tf_op jit(solution)/shard_map/ends/pallas_call | solution.py:416
  39.6 0.0 collective-permute-done.6.one_ref
  39.6 0.0 collective-permute-done.7.two_ref
  39.6 1.6 %edge.1 = (bf16[2,512,256]{2,1,0:T(8,128)(2,1)S(1)}, bf16[2,512,256]{2,1,0:T(8,128)(2,1)S(1)}, bf16[528,256]{1,0:T(8,128)(2,1)S(1)}, bf16[528,256]{1,0:T(8,128)(2,1)S(1)}) custom-call(f32[4,512,256]{2,1,0:T(8,128)S(1)} %get-tuple-element.81.below_ref, bf16[1,512,256]{2,1,0:T(8,128)(2,1)S(1)} %collective-permute-done.6.one_ref, ...), custom_call_target="tpu_custom_call" | custom-call | flops 805306368 | bytes 9454592 | tf_op jit(solution)/shard_map/edge/pallas_call | solution.py:416
  41.3 0.0 copy-done.15
  41.3 1.7 %collective-permute-start.11 = (bf16[528,256]{1,0:T(8,128)(2,1)S(1)}, bf16[528,256]{1,0:T(8,128)(2,1)S(1)}, u32[]{:S(2)}, u32[]{:S(2)}) collective-permute-start(bf16[528,256]{1,0:T(8,128)(2,1)S(1)} %get-tuple-element.105), channel_id=1, source_target_pairs={{0,1},{1,0},{2,3},{3,2},{4,5},{5,4},{6,7},{7,6},{8,9},{9,8},{10,11... | collective-permute-start | bytes 811016 | tf_op jit(solution)/shard_map/ppermute | solution.py:436
  43.0 0.0 copy-done.10
  43.0 1.3 %lower_inner.1 = (bf16[4,512,256]{2,1,0:T(8,128)(2,1)S(1)}, f32[2,512,256]{2,1,0:T(8,128)S(1)}) custom-call(bf16[2,512,256]{2,1,0:T(8,128)(2,1)S(1)} %get-tuple-element.80.inner_ref, bf16[2,512,256]{2,1,0:T(8,128)(2,1)S(1)} %get-tuple-element.88.ends_ref, bf16[2,512,256]{2,1,0:T(8,128)(2,1)S(1)} %get-tuple-element.93.edge_ref, ...), custom_call_target="tpu_custom_call" | custom-call | flops 1073741824 | bytes 5636096 | tf_op jit(solution)/shard_map/lower_inner/pallas_call | solution.py:416
  44.3 0.0 collective-permute-done.10.near_b_ref
  44.3 0.0 collective-permute-done.11.near_a_ref
  44.3 0.1 pair.1
  44.5 16.7 %all_to_all.15.got_ref = bf16[16,80,256]{2,1,0:T(8,128)(2,1)S(1)} all-to-all(bf16[16,80,256]{2,1,0:T(8,128)(2,1)S(1)} %pair.1), channel_id=1, replica_groups=mesh['xh'=2,'y'=4,'z'=8,'xl'=2,'core'=2] {'xl','xh','y'}, dimensions={0} | all-to-all | bytes 1310720 | tf_op jit(solution)/shard_map/all_to_all | solution.py:520
  61.2 0.8 rest.1
  62.0 8.2 %all-to-all-start.1 = ((bf16[8,80,256]{2,1,0:T(8,128)(2,1)}), bf16[8,80,256]{2,1,0:T(8,128)(2,1)S(1)}, u32[]{:S(2)}, u32[]{:S(2)}) async-start(bf16[8,80,256]{2,1,0:T(8,128)(2,1)} %rest.1), calls=%async_computation.1 | async-start | bytes 655360 | tf_op jit(solution)/shard_map/all_to_all | solution.py:522
  70.2 0.9 collective-permute-start.8
  71.1 0.0 collective-permute-start.9
  71.1 9.1 %collective-permute-done.8.one_ref = bf16[1,512,256]{2,1,0:T(8,128)(2,1)S(1)} collective-permute-done((bf16[1,512,256]{2,1,0:T(8,128)(2,1)}, bf16[1,512,256]{2,1,0:T(8,128)(2,1)S(1)}, u32[]{:S(2)}, u32[]{:S(2)}) %collective-permute-start.8) | collective-permute-done | bytes 262176 | tf_op jit(solution)/shard_map/ppermute | solution.py:432
  80.2 0.0 collective-permute-done.9.two_ref
  80.2 1.4 %all-to-all-done.1.got_ref = bf16[8,80,256]{2,1,0:T(8,128)(2,1)S(1)} async-done(((bf16[8,80,256]{2,1,0:T(8,128)(2,1)}), bf16[8,80,256]{2,1,0:T(8,128)(2,1)S(1)}, u32[]{:S(2)}, u32[]{:S(2)}) %all-to-all-start.1) | async-done | bytes 327712 | tf_op jit(solution)/shard_map/all_to_all | solution.py:522
  81.6 0.7 ring.1
  82.3 11.5 %all_to_all.16.mine_ref = bf16[16,64,256]{2,1,0:T(8,128)(2,1)S(1)} all-to-all(bf16[16,64,256]{2,1,0:T(8,128)(2,1)S(1)} %get-tuple-element.106), channel_id=1, replica_groups=mesh['xh'=2,'y'=4,'z'=8,'xl'=2,'core'=2] {'xl','xh','y'}, dimensions={0} | all-to-all | bytes 1048576 | tf_op jit(solution)/shard_map/all_to_all | solution.py:527
  93.8 4.0 %collective-permute-start.12 = (bf16[16,64,256]{2,1,0:T(8,128)(2,1)S(1)}, bf16[16,64,256]{2,1,0:T(8,128)(2,1)S(1)}, u32[]{:S(2)}, u32[]{:S(2)}) collective-permute-start(bf16[16,64,256]{2,1,0:T(8,128)(2,1)S(1)} %all_to_all.16.mine_ref), channel_id=1, source_target_pairs={{0,1},{1,0},{2,3},{3,2},{4,5},{5,4},{6,7},{7,6},{8,9},{9,8},{10,11... | collective-permute-start | bytes 1572872 | tf_op jit(solution)/shard_map/ppermute | solution.py:436
  97.8 1.2 %lower_outer.1 = bf16[6,512,256]{2,1,0:T(8,128)(2,1)} custom-call(f32[2,512,256]{2,1,0:T(8,128)S(1)} %get-tuple-element.98.part_ref, bf16[768,256]{1,0:T(8,128)(2,1)S(1)} %copy-done.11, bf16[1,512,256]{2,1,0:T(8,128)(2,1)S(1)} %collective-permute-done.8.one_ref, bf16[1,512,256]{2,1,0:T(8,128)(2,1)S(1)} %collective-permute-done.9.two_ref, ...), custom_call_target="tpu_custom_call" | custom-call | flops 134217728 | bytes 4587520 | tf_op jit(solution)/shard_map/lower_outer/pallas_call | solution.py:416
  99.0 0.3 collective-permute-done.12.other_ref
  99.3 1.4 %tail.1 = (f32[3,256,256]{2,1,0:T(8,128)}, f32[256,256]{1,0:T(8,128)}, f32[3,256,256]{2,1,0:T(8,128)}, f32[256,256]{1,0:T(8,128)}) custom-call(bf16[16,64,256]{2,1,0:T(8,128)(2,1)S(1)} %all_to_all.16.mine_ref, bf16[16,64,256]{2,1,0:T(8,128)(2,1)S(1)} %collective-permute-done.12.other_ref), custom_call_target="tpu_custom_call" | custom-call | bytes 3145728 | tf_op jit(solution)/shard_map/tail/pallas_call | solution.py:416
  (13 shorter events, 0.0 us)
Async XLA Ops:
  0.6 1.4 %copy-start = (bf16[1,3072,256]{2,1,0:T(8,128)(2,1)S(1)}, bf16[1,3072,256]{2,1,0:T(8,128)(2,1)}, u32[]{:S(2)}) copy-start(bf16[1,3072,256]{2,1,0:T(8,128)(2,1)} %param.8) | copy-start | bytes 4718596
  2.0 7.7 %copy-start.6 = (bf16[1,3072,256]{2,1,0:T(8,128)(2,1)S(1)}, bf16[1,3072,256]{2,1,0:T(8,128)(2,1)}, u32[]{:S(2)}) copy-start(bf16[1,3072,256]{2,1,0:T(8,128)(2,1)} %param.9) | copy-start | bytes 4718596
  2.2 17.1 %collective-permute-start = (bf16[2,512,256]{2,1,0:T(8,128)(2,1)S(1)}, bf16[2,512,256]{2,1,0:T(8,128)(2,1)S(1)}, u32[]{:S(2)}, u32[]{:S(2)}) collective-permute-start(bf16[2,512,256]{2,1,0:T(8,128)(2,1)S(1)} %get-tuple-element.61), channel_id=1, source_target_pairs={{0,224},{32,64},{64,32},{96,128},{128,96},{160,192},{192,160},{224... | collective-permute-start | bytes 1572872 | tf_op jit(solution)/shard_map/ppermute | solution.py:432
  8.3 12.5 %collective-permute-start.1 = (bf16[2,512,256]{2,1,0:T(8,128)(2,1)S(1)}, bf16[2,512,256]{2,1,0:T(8,128)(2,1)S(1)}, u32[]{:S(2)}, u32[]{:S(2)}) collective-permute-start(bf16[2,512,256]{2,1,0:T(8,128)(2,1)S(1)} %get-tuple-element.62), channel_id=1, source_target_pairs={{0,32},{32,0},{64,96},{96,64},{128,160},{160,128},{192,224},{224,1... | collective-permute-start | bytes 1572872 | tf_op jit(solution)/shard_map/ppermute | solution.py:432
  8.3 18.5 %collective-permute-start.2 = (bf16[1,512,256]{2,1,0:T(8,128)(2,1)S(1)}, bf16[1,512,256]{2,1,0:T(8,128)(2,1)S(1)}, u32[]{:S(2)}, u32[]{:S(2)}) collective-permute-start(bf16[1,512,256]{2,1,0:T(8,128)(2,1)S(1)} %get-tuple-element.69), channel_id=1, source_target_pairs={{0,224},{32,64},{64,32},{96,128},{128,96},{160,192},{192,160},{224... | collective-permute-start | bytes 786440 | tf_op jit(solution)/shard_map/ppermute | solution.py:432
  8.9 17.9 %collective-permute-start.3 = (bf16[1,512,256]{2,1,0:T(8,128)(2,1)S(1)}, bf16[1,512,256]{2,1,0:T(8,128)(2,1)S(1)}, u32[]{:S(2)}, u32[]{:S(2)}) collective-permute-start(bf16[1,512,256]{2,1,0:T(8,128)(2,1)S(1)} %get-tuple-element.70), channel_id=1, source_target_pairs={{0,32},{32,0},{64,96},{96,64},{128,160},{160,128},{192,224},{224,1... | collective-permute-start | bytes 786440 | tf_op jit(solution)/shard_map/ppermute | solution.py:432
  9.8 1.0 copy-start.2
  10.8 1.0 copy-start.4
  11.8 0.9 copy-start.9
  12.7 0.9 copy-start.12
  13.6 0.7 copy-start.13
  14.3 0.7 copy-start.14
  14.9 5.8 %copy-start.3 = (bf16[3,256,256]{2,1,0:T(8,128)(2,1)S(1)}, bf16[3,256,256]{2,1,0:T(8,128)(2,1)}, u32[]{:S(2)}) copy-start(bf16[3,256,256]{2,1,0:T(8,128)(2,1)} %param.10) | copy-start | bytes 1179652
  18.3 1.0 copy-start.7
  19.3 23.7 %copy-start.10 = (bf16[768,256]{1,0:T(8,128)(2,1)}, bf16[768,256]{1,0:T(8,128)(2,1)S(1)}, u32[]{:S(2)}) copy-start(bf16[768,256]{1,0:T(8,128)(2,1)S(1)} %get-tuple-element.97.w_ref) | copy-start | bytes 1179652
  22.0 16.0 %collective-permute-start.4 = (bf16[1,512,256]{2,1,0:T(8,128)(2,1)S(1)}, bf16[1,512,256]{2,1,0:T(8,128)(2,1)S(1)}, u32[]{:S(2)}, u32[]{:S(2)}) collective-permute-start(bf16[1,512,256]{2,1,0:T(8,128)(2,1)S(1)} %get-tuple-element.82), channel_id=1, source_target_pairs={{0,224},{32,64},{64,32},{96,128},{128,96},{160,192},{192,160},{224... | collective-permute-start | bytes 786440 | tf_op jit(solution)/shard_map/ppermute | solution.py:432
  26.0 12.0 %collective-permute-start.5 = (bf16[1,512,256]{2,1,0:T(8,128)(2,1)S(1)}, bf16[1,512,256]{2,1,0:T(8,128)(2,1)S(1)}, u32[]{:S(2)}, u32[]{:S(2)}) collective-permute-start(bf16[1,512,256]{2,1,0:T(8,128)(2,1)S(1)} %get-tuple-element.83), channel_id=1, source_target_pairs={{0,32},{32,0},{64,96},{96,64},{128,160},{160,128},{192,224},{224,1... | collective-permute-start | bytes 786440 | tf_op jit(solution)/shard_map/ppermute | solution.py:432
  26.9 5.0 %copy-start.1 = (bf16[1,3072,256]{2,1,0:T(8,128)(2,1)S(1)}, bf16[1,3072,256]{2,1,0:T(8,128)(2,1)}, u32[]{:S(2)}) copy-start(bf16[1,3072,256]{2,1,0:T(8,128)(2,1)} %param.8) | copy-start | bytes 4718596
  26.9 5.0 %copy-start.5 = (bf16[3,256,256]{2,1,0:T(8,128)(2,1)S(1)}, bf16[3,256,256]{2,1,0:T(8,128)(2,1)}, u32[]{:S(2)}) copy-start(bf16[3,256,256]{2,1,0:T(8,128)(2,1)} %param.13) | copy-start | bytes 1179652
  26.9 4.9 %copy-start.8 = (bf16[4,512,256]{2,1,0:T(8,128)(2,1)S(1)}, bf16[4,512,256]{2,1,0:T(8,128)(2,1)}, u32[]{:S(2)}) copy-start(bf16[4,512,256]{2,1,0:T(8,128)(2,1)} %copy-done.7) | copy-start | bytes 3145732
  28.3 11.4 %collective-permute-start.6 = (bf16[1,512,256]{2,1,0:T(8,128)(2,1)S(1)}, bf16[1,512,256]{2,1,0:T(8,128)(2,1)S(1)}, u32[]{:S(2)}, u32[]{:S(2)}) collective-permute-start(bf16[1,512,256]{2,1,0:T(8,128)(2,1)S(1)} %get-tuple-element.89), channel_id=1, source_target_pairs={{0,224},{32,64},{64,32},{96,128},{128,96},{160,192},{192,160},{224... | collective-permute-start | bytes 786440 | tf_op jit(solution)/shard_map/ppermute | solution.py:432
  31.8 7.8 %collective-permute-start.7 = (bf16[1,512,256]{2,1,0:T(8,128)(2,1)S(1)}, bf16[1,512,256]{2,1,0:T(8,128)(2,1)S(1)}, u32[]{:S(2)}, u32[]{:S(2)}) collective-permute-start(bf16[1,512,256]{2,1,0:T(8,128)(2,1)S(1)} %get-tuple-element.90), channel_id=1, source_target_pairs={{0,32},{32,0},{64,96},{96,64},{128,160},{160,128},{192,224},{224,1... | collective-permute-start | bytes 786440 | tf_op jit(solution)/shard_map/ppermute | solution.py:432
  36.1 8.2 %collective-permute-start.10 = (bf16[528,256]{1,0:T(8,128)(2,1)S(1)}, bf16[528,256]{1,0:T(8,128)(2,1)S(1)}, u32[]{:S(2)}, u32[]{:S(2)}) collective-permute-start(bf16[528,256]{1,0:T(8,128)(2,1)S(1)} %get-tuple-element.103), channel_id=1, source_target_pairs={{0,1},{1,0},{2,3},{3,2},{4,5},{5,4},{6,7},{7,6},{8,9},{9,8},{10,11... | collective-permute-start | bytes 811016 | tf_op jit(solution)/shard_map/ppermute | solution.py:436
  39.6 1.6 %copy-start.15 = (bf16[1,512,256]{2,1,0:T(8,128)(2,1)}, bf16[1,512,256]{2,1,0:T(8,128)(2,1)S(1)}, u32[]{:S(2)}) copy-start(bf16[1,512,256]{2,1,0:T(8,128)(2,1)S(1)} %get-tuple-element.100) | copy-start | bytes 786436
  41.3 3.0 %collective-permute-start.11 = (bf16[528,256]{1,0:T(8,128)(2,1)S(1)}, bf16[528,256]{1,0:T(8,128)(2,1)S(1)}, u32[]{:S(2)}, u32[]{:S(2)}) collective-permute-start(bf16[528,256]{1,0:T(8,128)(2,1)S(1)} %get-tuple-element.105), channel_id=1, source_target_pairs={{0,1},{1,0},{2,3},{3,2},{4,5},{5,4},{6,7},{7,6},{8,9},{9,8},{10,11... | collective-permute-start | bytes 811016 | tf_op jit(solution)/shard_map/ppermute | solution.py:436
  61.2 36.6 %copy-start.11 = (bf16[768,256]{1,0:T(8,128)(2,1)S(1)}, bf16[768,256]{1,0:T(8,128)(2,1)}, u32[]{:S(2)}) copy-start(bf16[768,256]{1,0:T(8,128)(2,1)} %copy-done.10) | copy-start | bytes 1179652
  62.0 19.6 %all-to-all-start.1 = ((bf16[8,80,256]{2,1,0:T(8,128)(2,1)}), bf16[8,80,256]{2,1,0:T(8,128)(2,1)S(1)}, u32[]{:S(2)}, u32[]{:S(2)}) async-start(bf16[8,80,256]{2,1,0:T(8,128)(2,1)} %rest.1), calls=%async_computation.1 | async-start | bytes 655360 | tf_op jit(solution)/shard_map/all_to_all | solution.py:522
  70.2 10.0 %collective-permute-start.8 = (bf16[1,512,256]{2,1,0:T(8,128)(2,1)}, bf16[1,512,256]{2,1,0:T(8,128)(2,1)S(1)}, u32[]{:S(2)}, u32[]{:S(2)}) collective-permute-start(bf16[1,512,256]{2,1,0:T(8,128)(2,1)} %get-tuple-element.99), channel_id=1, source_target_pairs={{0,224},{32,64},{64,32},{96,128},{128,96},{160,192},{192,160},{224... | collective-permute-start | bytes 786440 | tf_op jit(solution)/shard_map/ppermute | solution.py:432
  71.1 9.1 %collective-permute-start.9 = (bf16[1,512,256]{2,1,0:T(8,128)(2,1)}, bf16[1,512,256]{2,1,0:T(8,128)(2,1)S(1)}, u32[]{:S(2)}, u32[]{:S(2)}) collective-permute-start(bf16[1,512,256]{2,1,0:T(8,128)(2,1)} %copy-done.15), channel_id=1, source_target_pairs={{0,32},{32,0},{64,96},{96,64},{128,160},{160,128},{192,224},{224,1... | collective-permute-start | bytes 786440 | tf_op jit(solution)/shard_map/ppermute | solution.py:432
  93.8 5.5 %collective-permute-start.12 = (bf16[16,64,256]{2,1,0:T(8,128)(2,1)S(1)}, bf16[16,64,256]{2,1,0:T(8,128)(2,1)S(1)}, u32[]{:S(2)}, u32[]{:S(2)}) collective-permute-start(bf16[16,64,256]{2,1,0:T(8,128)(2,1)S(1)} %all_to_all.16.mine_ref), channel_id=1, source_target_pairs={{0,1},{1,0},{2,3},{3,2},{4,5},{5,4},{6,7},{7,6},{8,9},{9,8},{10,11... | collective-permute-start | bytes 1572872 | tf_op jit(solution)/shard_map/ppermute | solution.py:436
